TPU v7x, 256 devices: a whole 4x4x8 slice. The times are simulated.
256 devices in a mesh: ctx: 32 (over x, z), tp: 8 (over y, core).
Axes of the slice: x: 4, y: 4, z: 8, core: 2. Of those that a mesh axis runs over, the one named last changes fastest.
Arguments:
- head_input: bfloat16 [16384, 4096], P('ctx', 'tp'), may hold values from -6 to 6
- write_vector: bfloat16 [16384, 128], P('ctx'), may hold values from -0.119628906 to 0.119628906
- read_vector: bfloat16 [16384, 128], P('ctx'), may hold values from -0.5 to 0.5
- log_decay: float32 [64, 16384], P('tp', 'ctx'), may hold values from -1 to 0
- skip_gain: float32 [64], P('tp'), may hold values from 0.5 to 2
- out_grad: bfloat16 [16384, 4096], P('ctx'), may hold values from -12 to 12
- out_master: float32 [4096, 4096], P('ctx', 'tp'), may hold values from -0.09375 to 0.09375
- first_moment: float32 [4096, 4096], P('ctx', 'tp'), may hold values from -180 to 180
- squared_average: float32 [64], P('tp'), may hold values from 16.384 to 163.84
Outputs:
- input_grad: bfloat16 [16384, 4096], P('ctx', 'tp')
- write_grad: float32 [16384, 128], P('ctx')
- read_grad: float32 [16384, 128], P('ctx')
- decay_grad: float32 [64, 16384], P('tp', 'ctx')
- skip_grad: float32 [64], P('tp')
- new_master: float32 [4096, 4096], P('ctx', 'tp')
- new_first: float32 [4096, 4096], P('ctx', 'tp')
- new_second: float32 [64], P('tp')
All inputs are finite; a program needn't handle non-finite values.
Results may differ from a plain program's by a relative error of at most 0.008.
Values may be sent and summed in bfloat16 or wider, within the bound.
No kernel may reach another device: no remote copies, remote signals or barrier semaphores. Data moves between devices by JAX's collectives and lax.ppermute only.
A program may use at most 128 MiB of HBM per device.

v0:
```python
import jax
import jax.numpy as jnp
from jax import lax
from jax.sharding import PartitionSpec as P

WIDTH = 4096


highest = lax.Precision.HIGHEST
beta_one = 0.9
beta_two = 0.95
learn_rate = 0.004
decoupled_decay = 0.1
adam_eps = 1e-08
bias_one = 0.9999734386011124
bias_two = 0.994079470779666


def entering(value, axis, combine, identity, reverse):
    count, position = (lax.axis_size(axis), lax.axis_index(axis))
    everything = jax.tree.map(lambda part: lax.all_gather(part, axis), value)
    start = jax.tree.map(
        lambda part, zero: jnp.broadcast_to(jnp.asarray(zero, part.dtype), part.shape),
        value,
        identity,
    )

    def hop(k, before):
        at = count - 1 - k if reverse else k
        reached = at > position if reverse else at < position
        new = combine(before, jax.tree.map(lambda part: part[at], everything))
        return jax.tree.map(lambda a, b: jnp.where(reached, a, b), new, before)

    return lax.fori_loop(0, count, hop, start)


def decay_tables(block_log):
    running = jnp.cumsum(block_log, axis=1)
    last_sum = running[:, -1:]
    gap = running[:, :, None] - running[:, None, :]
    row_index = lax.broadcasted_iota(jnp.int32, gap.shape, 1)
    col_index = lax.broadcasted_iota(jnp.int32, gap.shape, 2)
    lower_decay = jnp.exp(jnp.where(row_index >= col_index, gap, -1e30))
    to_end = jnp.exp(last_sum - running)
    from_start = jnp.exp(running)
    return (lower_decay, to_end, from_start, jnp.exp(last_sum[:, 0]))


def chain_terms(head_x, write_b, read_c, output_gradient, to_end, from_start):
    local_state = jnp.einsum(
        "shp,sn->hpn", head_x * to_end.T[:, :, None], write_b, precision=highest
    )
    carried = jnp.einsum(
        "shp,sn->hpn", output_gradient * from_start.T[:, :, None], read_c, precision=highest
    )
    return (local_state, carried)


def finish_block(
    head_low,
    write_low,
    read_low,
    grad_low,
    skip_gain,
    lower_decay,
    to_end,
    from_start,
    start_state,
    end_adjoint,
):
    head_x = head_low.astype(jnp.float32)
    output_gradient = grad_low.astype(jnp.float32)
    write_b = write_low.astype(jnp.float32)
    read_c = read_low.astype(jnp.float32)
    scores = jnp.dot(read_low, write_low.T, preferred_element_type=jnp.float32)
    mixed = (lower_decay * scores[None]).astype(jnp.bfloat16)
    core_y = jnp.einsum("hts,shp->thp", mixed, head_low, preferred_element_type=jnp.float32)
    core_y = (
        core_y
        + jnp.einsum("hpn,tn->thp", start_state, read_c, precision=highest)
        * from_start.T[:, :, None]
    )
    out_y = (core_y + skip_gain[None, :, None] * head_x).astype(jnp.bfloat16)
    core_grad = jnp.einsum("hst,shp->thp", mixed, grad_low, preferred_element_type=jnp.float32)
    core_grad = (
        core_grad
        + jnp.einsum("hpn,tn->thp", end_adjoint, write_b, precision=highest) * to_end.T[:, :, None]
    )
    input_grad = (core_grad + skip_gain[None, :, None] * output_gradient).astype(jnp.bfloat16)
    cross_dots = jnp.einsum("thp,shp->hts", grad_low, head_low, preferred_element_type=jnp.float32)
    pair_weights = jnp.sum(lower_decay * cross_dots, axis=0)
    read_grad = jnp.dot(pair_weights, write_b, precision=highest)
    read_grad = read_grad + jnp.einsum(
        "hpn,thp,ht->tn", start_state, output_gradient, from_start, precision=highest
    )
    write_grad = lax.dot_general(pair_weights, read_c, (((0,), (0,)), ((), ())), precision=highest)
    write_grad = write_grad + jnp.einsum(
        "hpn,thp,ht->tn", end_adjoint, head_x, to_end, precision=highest
    )
    skip_part = jnp.sum(output_gradient * head_x, axis=(0, 2))
    decay_part = (jnp.sum(output_gradient * core_y, axis=2) - jnp.sum(head_x * core_grad, axis=2)).T
    return (out_y, input_grad, write_grad, read_grad, skip_part, decay_part)


def combine_pairs(earlier, later):
    return (earlier[0] * later[0], later[0][:, None, None] * earlier[1] + later[1])


def add_pair(earlier, later):
    return earlier + later


def shards(
    head_input,
    write_vector,
    read_vector,
    log_decay,
    skip_gain,
    out_grad,
    out_master,
    first_moment,
    squared_average,
):
    tokens = head_input.shape[0]
    head_count = log_decay.shape[0]
    head_width = head_input.shape[1] // head_count
    head_low = head_input.reshape(tokens, head_count, head_width)
    head_x = head_low.astype(jnp.float32)
    write_b = write_vector.astype(jnp.float32)
    read_c = read_vector.astype(jnp.float32)
    weight_bf = out_master.astype(jnp.bfloat16)
    columns = out_grad
    grad_flat = jnp.dot(
        columns,
        lax.all_gather(weight_bf, "ctx", axis=0, tiled=True),
        preferred_element_type=jnp.float32,
    )
    grad_low = grad_flat.astype(jnp.bfloat16).reshape(tokens, head_count, head_width)
    output_gradient = grad_low.astype(jnp.float32)
    lower_decay, to_end, from_start, decay_per_block = decay_tables(log_decay)
    local_state, carried = chain_terms(head_x, write_b, read_c, output_gradient, to_end, from_start)
    identity = (jnp.ones_like(decay_per_block), jnp.zeros_like(local_state))
    start_decay, start_state = entering(
        (decay_per_block, local_state), "ctx", combine_pairs, identity, False
    )
    end_decay, end_adjoint = entering(
        (decay_per_block, carried), "ctx", combine_pairs, identity, True
    )
    out_y, input_grad, write_grad, read_grad, skip_part, decay_part = finish_block(
        head_low,
        write_vector,
        read_vector,
        grad_low,
        skip_gain,
        lower_decay,
        to_end,
        from_start,
        start_state,
        end_adjoint,
    )
    skip_total = lax.psum(skip_part, "ctx")
    write_sum, read_sum = lax.psum((write_grad, read_grad), "tp")
    local_tail = jnp.flip(jnp.cumsum(jnp.flip(decay_part, 1), axis=1), 1)
    block_total = local_tail[:, 0]
    above = entering(block_total, "ctx", add_pair, jnp.zeros_like(block_total), True)
    decay_grad = local_tail + above[:, None]
    out_flat = out_y.reshape(tokens, head_count * head_width)
    rows_here = out_master.shape[0]
    columns = out_grad
    weight_grad = lax.psum_scatter(
        lax.dot_general(
            columns, out_flat, (((0,), (0,)), ((), ())), preferred_element_type=jnp.float32
        ).astype(jnp.bfloat16),
        "ctx",
        scatter_dimension=0,
        tiled=True,
    ).astype(jnp.float32)
    square_part = jnp.sum(
        (weight_grad * weight_grad).reshape(rows_here, head_count, head_width), axis=(0, 2)
    )
    square_total = lax.psum(square_part, "ctx")
    mean_square = square_total / float(WIDTH * head_width)
    new_second = beta_two * squared_average + (1.0 - beta_two) * mean_square
    new_first = beta_one * first_moment + (1.0 - beta_one) * weight_grad
    scale = jnp.repeat(jnp.sqrt(new_second / bias_two) + adam_eps, head_width)
    new_master = out_master - learn_rate * (
        new_first / bias_one / scale[None, :] + decoupled_decay * out_master
    )
    return (
        input_grad.reshape(tokens, head_count * head_width),
        write_sum,
        read_sum,
        decay_grad,
        skip_total,
        new_master,
        new_first,
        new_second,
    )


def solution(mesh):
    in_specs = (
        P("ctx", "tp"),
        P("ctx", None),
        P("ctx", None),
        P("tp", "ctx"),
        P("tp"),
        P("ctx", None),
        P("ctx", "tp"),
        P("ctx", "tp"),
        P("tp"),
    )
    out_specs = (
        P("ctx", "tp"),
        P("ctx", None),
        P("ctx", None),
        P("tp", "ctx"),
        P("tp"),
        P("ctx", "tp"),
        P("ctx", "tp"),
        P("tp"),
    )
    return jax.shard_map(shards, mesh=mesh, in_specs=in_specs, out_specs=out_specs, check_vma=False)
```

profile of v0, /device:TPU:8, one launch (start us, length us, event | category | flops | bytes accessed | tf_op | source)
XLA Modules:
  0.0 652.2 jit_solution(17458774482409052123)
XLA Ops:
  7.2 1.7 convert_element_type.42
  9.0 2.2 reduce-window.14
  11.4 1.3 copy.55
  13.0 1.4 fusion.19
  14.4 81.4 %all-gather.8.cloned.1.call-done = bf16[4096,512]{1,0:T(8,128)(2,1)} async-done(((bf16[128,512]{1,0:T(8,128)(2,1)}), bf16[4096,512]{1,0:T(8,128)(2,1)}) %all-gather.8.cloned.1.call-update) | async-done | bytes 4194320 | tf_op jit(solution)/shard_map/all_gather | solution.py:135
  95.8 5.9 multiply_reduce_fusion.1
  101.8 1.4 fusion.11
  104.7 73.1 %all-reduce = f32[256]{0:T(256)S(1)} all-reduce(f32[256]{0:T(256)S(1)} %dynamic-update-slice), channel_id=2, replica_groups=mesh['ctx'=32,'tp'=8] {'ctx'}, use_global_device_ids=true, to_apply=%add | all-reduce | flops 256 | bytes 2048
  178.3 3.3 fusion.6
  181.6 2.4 fusion.5
  184.0 10.9 %all-gather.12.cloned.1.call-done = f32[256,64,128]{2,1,0:T(8,128)} async-done(((f32[8,64,128]{2,1,0:T(8,128)}), f32[256,64,128]{2,1,0:T(8,128)}) %all-gather.12.cloned.1.call-update) | async-done | bytes 8388624 | tf_op jit(solution)/shard_map/all_gather | solution.py:21
  194.9 35.1 %while.47 = (s32[]{:T(128)}, f32[8,64,128]{2,1,0:T(8,128)S(1)}, s32[]{:T(128)}, f32[32,8]{1,0:T(8,128)S(1)}, f32[32,8,64,128]{3,2,1,0:T(8,128)}, /*index=5*/s32[]{:T(128)}, s32[]{:T(128)}) while((s32[]{:T(128)}, f32[8,64,128]{2,1,0:T(8,128)S(1)}, s32[]{:T(128)}, f32[32,8]{1,0:T(8,128)S(1)}, f32[32,8,64,128]{3,2,1,0:T(8,128)}, ...), condition=%wide.region_7.8_spmd.clone, body=%wide.region_6.7_spmd.clone.sunk | while | flops 262148 | bytes 786641 | solution.py:34
  196.0 1.1 fusion.59
  197.1 1.1 fusion.59
  198.2 1.1 fusion.59
  199.3 1.1 fusion.59
  200.4 1.1 fusion.59
  201.5 1.1 fusion.59
  202.6 1.1 fusion.59
  203.7 1.1 fusion.59
  204.8 1.1 fusion.59
  207.0 1.1 fusion.59
  208.1 1.1 fusion.59
  209.2 1.1 fusion.59
  212.5 1.1 fusion.59
  213.6 1.1 fusion.59
  215.8 1.1 fusion.59
  216.9 1.1 fusion.59
  220.2 1.1 fusion.59
  221.3 1.1 fusion.59
  222.4 1.1 fusion.59
  225.7 1.1 fusion.59
  226.8 1.1 fusion.59
  230.1 1.8 fusion.10
  231.9 61.9 %all-gather.10.cloned.1.call-done = f32[256,64,128]{2,1,0:T(8,128)} async-done(((f32[8,64,128]{2,1,0:T(8,128)}), f32[256,64,128]{2,1,0:T(8,128)}) %all-gather.10.cloned.1.call-update) | async-done | bytes 8388624 | tf_op jit(solution)/shard_map/all_gather | solution.py:21
  293.8 35.3 %while.46 = (s32[]{:T(128)}, f32[8,64,128]{2,1,0:T(8,128)S(1)}, s32[]{:T(128)}, f32[32,8]{1,0:T(8,128)S(1)}, f32[32,8,64,128]{3,2,1,0:T(8,128)}, /*index=5*/s32[]{:T(128)}, s32[]{:T(128)}, s32[]{:T(128)}, s32[]{:T(128)}) while((s32[]{:T(128)}, f32[8,64,128]{2,1,0:T(8,128)S(1)}, s32[]{:T(128)}, f32[32,8]{1,0:T(8,128)S(1)}, ...), condition=%wide.region_3.4_spmd.clone, body=%wide.region_2.3_spmd.clone.sunk | while | flops 262152 | bytes 786703 | solution.py:34
  297.1 1.1 fusion.58
  298.2 1.1 fusion.58
  302.6 1.1 fusion.58
  303.7 1.1 fusion.58
  308.1 1.1 fusion.58
  309.2 1.1 fusion.58
  312.5 1.1 fusion.58
  313.6 1.1 fusion.58
  314.7 1.1 fusion.58
  318.0 1.1 fusion.58
  319.1 1.1 fusion.58
  323.6 1.1 fusion.58
  324.7 1.1 fusion.58
  329.0 2.2 fusion.20
  331.3 6.5 fusion.2
  337.8 6.5 copy.63
  346.5 2.0 multiply_reduce_fusion
  348.4 1.8 convolution_bitcast_fusion.2
  350.2 1.3 convolution_add_fusion
  352.9 1.1 reduce-window.16
  355.0 1.8 convolution_bitcast_fusion.3
  356.8 1.7 convolution_add_fusion.1
  358.5 204.1 %reduce-scatter.4.cloned.1.call-done = bf16[128,512]{1,0:T(8,128)(2,1)} async-done(((bf16[4096,512]{1,0:T(8,128)(2,1)}), bf16[128,512]{1,0:T(8,128)(2,1)}) %reduce-scatter.4.cloned.1.call-update) | async-done | bytes 131088
  564.0 72.6 %all-reduce.2 = (f32[256]{0:T(256)S(1)}, f32[8]{0:T(128)}, f32[8]{0:T(128)S(1)}) all-reduce(f32[256]{0:T(256)S(1)} %dynamic-update-slice.1, f32[8]{0:T(128)S(1)} %reduce_sum.64, f32[8]{0:T(128)S(1)} %reduce_sum.67), channel_id=5, replica_groups=mesh['ctx'=32,'tp'=8] {'ctx'}, use_global_device_ids=true, to_apply=%add.1 | all-reduce | flops 272 | bytes 2176
  637.4 1.4 while.48
  638.8 1.2 multiply_subtract_fusion
  642.3 1.7 copy.93
  644.0 1.7 copy.94
  (191 shorter events, 43.7 us)
Async XLA Ops:
  7.2 5.8 copy-start
  7.2 88.7 %all-gather.8.cloned.1.call-start = ((), (), s32[]{:S(2)}) async-start(), calls=%async_computation.1 | async-start | bytes 4325376 | tf_op jit(solution)/shard_map/all_gather | solution.py:135
  8.9 186.0 %all-gather.12.cloned.1.call-start = ((), (), s32[]{:S(2)}) async-start(), calls=%async_computation.3 | async-start | bytes 8650752 | tf_op jit(solution)/shard_map/all_gather | solution.py:21
  12.6 89.1 %copy-start.1 = (bf16[512,128]{1,0:T(8,128)(2,1)S(1)}, bf16[512,128]{1,0:T(8,128)(2,1)}, u32[]{:S(2)}) copy-start(bf16[512,128]{1,0:T(8,128)(2,1)} %param.17) | copy-start | bytes 393220
  14.4 88.9 %copy-start.6 = (u32[256]{0:T(256)S(1)}, u32[256]{0:T(256)}, u32[]{:S(2)}) copy-start(u32[256]{0:T(256)} %constant.147) | copy-start | bytes 3076
  14.4 279.4 %all-gather.10.cloned.1.call-start = ((), (), s32[]{:S(2)}) async-start(), calls=%async_computation.2 | async-start | bytes 8650752 | tf_op jit(solution)/shard_map/all_gather | solution.py:21
  103.2 459.5 %reduce-scatter.4.cloned.1.call-start = ((), (), s32[]{:S(2)}) async-start(), calls=%async_computation.4 | async-start | bytes 4325376
  184.0 145.1 %copy-start.4 = (f32[8]{0:T(128)S(1)}, f32[8]{0:T(128)}, u32[]{:S(2)}) copy-start(f32[8]{0:T(128)} %param.19) | copy-start | bytes 100
  337.8 6.8 %copy-start.2 = (f32[128,512]{1,0:T(8,128)S(1)}, f32[128,512]{1,0:T(8,128)}, u32[]{:S(2)}) copy-start(f32[128,512]{1,0:T(8,128)} %param.21) | copy-start | bytes 786436
  337.8 7.6 %copy-start.3 = (f32[128,512]{1,0:T(8,128)S(1)}, f32[128,512]{1,0:T(8,128)}, u32[]{:S(2)}) copy-start(f32[128,512]{1,0:T(8,128)} %param.22) | copy-start | bytes 786436
  344.3 298.0 %all-reduce.6.cloned.1.call-start = ((), (), s32[]{:S(2)}) async-start(), calls=%async_computation.5 | async-start | bytes 1048576 | tf_op jit(solution)/shard_map/psum | solution.py:162
  346.4 290.2 %copy-start.5 = (f32[8]{0:T(128)S(1)}, f32[8]{0:T(128)}, u32[]{:S(2)}) copy-start(f32[8]{0:T(128)} %param.23) | copy-start | bytes 100
Sparse Core Ops, SparseCore 0:
  11.2 84.6 all-gather.7
  99.0 95.8 all-gather.11
  198.1 95.6 all-gather.9
  344.4 218.1 reduce-scatter.3
  565.6 62.4 all-reduce.5
where the time goes:
time: 655 us; the launch traced here: 652 us
  waiting for transfers between devices  358 us (55%)
  blocking collectives  146 us (22%)
  other arithmetic  76.2 us (12%)
  matrix products  33.8 us (5%)
  local copies, waits for them, and re-layouts  19.9 us (3%)
  between operations  14.6 us (2%)
    unnamed x6, waiting for transfers between devices  204 us
    unnamed x2, blocking collectives  146 us
    all_gather x1, waiting for transfers between devices, shards(): lax.all_gather(weight_bf, 'ctx', axis=0, tiled=True)  81.4 us
    all_gather x2, waiting for transfers between devices, entering(): everything = jax.tree.map(lambda part: lax.all_gather(part, axis), value)  72.8 us
    select_n x96, other arithmetic, hop(): return jax.tree.map(lambda a, b: jnp.where(reached, a, b), new, before)  68.2 us
    unnamed x29, local copies, waits for them, and re-layouts  17.6 us
  transfers between devices with their start and end apart: 5, of which 4 were waited for; matrix products, arithmetic and copies ran while one was open for 12% of the time, Pallas kernels for 0%

commit v1 on v0

v1 whole, which is shorter than its diff:
```python
import jax
import jax.numpy as jnp
from jax import lax
from jax.sharding import Mesh, PartitionSpec as P

WIDTH = 4096
beta_one = 0.9
beta_two = 0.95
learn_rate = 0.004
decoupled_decay = 0.1
adam_eps = 1e-08
bias_one = 0.9999734386011124
bias_two = 0.994079470779666

f32 = jnp.float32
bf16 = jnp.bfloat16
CTX = ("x", "z")
TP = ("y", "core")
BLOCKS = 32


def mm(a, b, dims):
    return lax.dot_general(a, b, (dims, ((), ())), preferred_element_type=f32)


def block_weights(logs):
    i = lax.broadcasted_iota(jnp.int32, (BLOCKS, BLOCKS, BLOCKS), 0)
    j = lax.broadcasted_iota(jnp.int32, (BLOCKS, BLOCKS, BLOCKS), 1)
    r = lax.broadcasted_iota(jnp.int32, (BLOCKS, BLOCKS, BLOCKS), 2)
    between = jnp.sum(jnp.where((r > j) & (r < i), logs[None, None, :], 0.0), axis=2)
    rows = lax.broadcasted_iota(jnp.int32, (BLOCKS, BLOCKS), 0)
    cols = lax.broadcasted_iota(jnp.int32, (BLOCKS, BLOCKS), 1)
    return jnp.where(rows > cols, jnp.exp(between), 0.0)


def swap(value, axes):
    return lax.all_to_all(value, axes, 0, 0, tiled=True)


def chain(weights, parts, reverse):
    dims = ((0,), (0,)) if reverse else ((1,), (0,))
    flat = parts.astype(f32).reshape(BLOCKS, 16 * 128)
    out = lax.dot_general(
        weights, flat, (dims, ((), ())), precision=lax.Precision.HIGHEST, preferred_element_type=f32
    )
    return out.astype(bf16).reshape(BLOCKS, 16, 128)


def shards(
    head_input,
    write_vector,
    read_vector,
    log_decay,
    skip_gain,
    out_grad,
    out_master,
    first_moment,
    squared_average,
):
    tokens, width = head_input.shape
    heads = log_decay.shape[0]
    head_width = width // heads

    weight_all = lax.all_gather(out_master.astype(bf16), CTX, axis=0, tiled=True)

    running = jnp.cumsum(log_decay, axis=1)
    last_sum = running[:, -1:]
    gap = running[:, :, None] - running[:, None, :]
    row_index = lax.broadcasted_iota(jnp.int32, gap.shape, 1)
    col_index = lax.broadcasted_iota(jnp.int32, gap.shape, 2)
    lower_decay = jnp.exp(jnp.where(row_index >= col_index, gap, -1e30))
    to_end = jnp.exp(last_sum - running)
    from_start = jnp.exp(running)
    to_end_wide = jnp.repeat(to_end.T, head_width, axis=1)
    from_start_wide = jnp.repeat(from_start.T, head_width, axis=1)
    skip_wide = jnp.repeat(skip_gain, head_width)[None, :]

    head_x = head_input.astype(f32)
    local_state = mm((head_x * to_end_wide).astype(bf16), write_vector, ((0,), (0,)))
    total = last_sum[:, 0]
    high = lax.reduce_precision(total, 8, 7)
    middle = lax.reduce_precision(total - high, 8, 7)
    low = lax.reduce_precision(total - high - middle, 8, 7)
    pieces = jnp.stack([high, middle, low] + [jnp.zeros_like(low)] * 5, axis=1).astype(bf16)
    pieces = jnp.broadcast_to(pieces[:, None, :, None], (heads, BLOCKS // heads, 8, 128))
    packed = jnp.concatenate(
        [local_state.astype(bf16).reshape(BLOCKS, 16, 128), pieces.reshape(BLOCKS, 8, 128)], axis=1
    )
    packed = swap(packed, CTX)
    logs = jnp.sum(packed[:, 16:19, 0].astype(f32), axis=1)
    weights = block_weights(logs)
    start_low = swap(chain(weights, packed[:, :16], False), CTX).reshape(width, 128)

    scores = mm(read_vector, write_vector, ((1,), (1,)))
    mixed = (lower_decay * scores[None]).astype(bf16)
    x_heads = head_input.reshape(tokens, heads, head_width)
    inner = jnp.einsum("hts,shp->thp", mixed, x_heads, preferred_element_type=f32)
    core_y = inner.reshape(tokens, width) + mm(read_vector, start_low, ((1,), (1,))) * from_start_wide
    out_y = (core_y + skip_wide * head_x).astype(bf16)

    partial = mm(out_grad, out_y, ((0,), (0,))).astype(bf16)
    quarter = WIDTH // 4
    partial = swap(partial, "x").reshape(4, quarter, width)
    partial = jnp.sum(partial.astype(f32), axis=0).astype(bf16)
    partial = swap(partial, "z").reshape(8, quarter // 8, width)
    weight_grad = jnp.sum(partial.astype(f32), axis=0)

    grad_low = mm(out_grad, weight_all, ((1,), (0,))).astype(bf16)
    grad = grad_low.astype(f32)
    grad_decayed = (grad * from_start_wide).astype(bf16)
    carried = mm(grad_decayed, read_vector, ((0,), (0,)))
    carried = swap(carried.astype(bf16).reshape(BLOCKS, 16, 128), CTX)
    end_low = swap(chain(weights, carried, True), CTX).reshape(width, 128)

    grad_heads = grad_low.reshape(tokens, heads, head_width)
    inner = jnp.einsum("hst,shp->thp", mixed, grad_heads, preferred_element_type=f32)
    core_grad = inner.reshape(tokens, width) + mm(write_vector, end_low, ((1,), (1,))) * to_end_wide
    input_grad = (core_grad + skip_wide * grad).astype(bf16)
    cross_dots = jnp.einsum("thp,shp->hts", grad_heads, x_heads, preferred_element_type=f32)
    pair_weights = jnp.sum(lower_decay * cross_dots, axis=0).astype(bf16)
    read_grad = mm(pair_weights, write_vector, ((1,), (0,))) + mm(grad_decayed, start_low, ((1,), (0,)))
    write_grad = mm(pair_weights, read_vector, ((0,), (0,))) + mm(
        (head_x * to_end_wide).astype(bf16), end_low, ((1,), (0,))
    )
    both = jnp.concatenate([write_grad, read_grad], axis=0).astype(bf16).reshape(8, -1, 128)
    both = swap(both, TP)
    both = jnp.sum(both.astype(f32), axis=0).astype(bf16)
    both = swap(jnp.broadcast_to(both[None], (8,) + both.shape), TP)
    both = both.reshape(2 * tokens, 128).astype(f32)

    terms = (grad * core_y - head_x * core_grad).reshape(tokens, heads, head_width)
    decay_part = jnp.sum(terms, axis=2).T
    local_tail = jnp.flip(jnp.cumsum(jnp.flip(decay_part, 1), axis=1), 1)
    end_state = start_low.astype(f32).reshape(heads, -1) * jnp.exp(last_sum) + local_state.reshape(
        heads, -1
    )
    above = jnp.sum(end_state * end_low.astype(f32).reshape(heads, -1), axis=1)
    decay_grad = local_tail + above[:, None]

    skip_part = jnp.sum((grad * head_x).reshape(tokens, heads, head_width), axis=(0, 2))
    square_part = jnp.sum((weight_grad * weight_grad).reshape(-1, heads, head_width), axis=(0, 2))
    small = jnp.concatenate([skip_part, square_part])
    small = lax.psum(lax.psum(small, "x"), "z")
    skip_total, square_total = small[:heads], small[heads:]
    mean_square = square_total / float(WIDTH * head_width)
    new_second = beta_two * squared_average + (1.0 - beta_two) * mean_square
    new_first = beta_one * first_moment + (1.0 - beta_one) * weight_grad
    scale = jnp.repeat(jnp.sqrt(new_second / bias_two) + adam_eps, head_width)
    new_master = out_master - learn_rate * (
        new_first / bias_one / scale[None, :] + decoupled_decay * out_master
    )
    return (
        input_grad,
        both[:tokens],
        both[tokens:],
        decay_grad,
        skip_total,
        new_master,
        new_first,
        new_second,
    )


def solution(mesh):
    fine = Mesh(mesh.devices.reshape(4, 8, 4, 2), ("x", "z", "y", "core"))
    in_specs = (
        P(CTX, TP),
        P(CTX, None),
        P(CTX, None),
        P(TP, CTX),
        P(TP),
        P(CTX, None),
        P(CTX, TP),
        P(CTX, TP),
        P(TP),
    )
    out_specs = (
        P(CTX, TP),
        P(CTX, None),
        P(CTX, None),
        P(TP, CTX),
        P(TP),
        P(CTX, TP),
        P(CTX, TP),
        P(TP),
    )
    return jax.shard_map(shards, mesh=fine, in_specs=in_specs, out_specs=out_specs, check_vma=False)
```

time: 655 us -> 266 us (0.41)
  waiting for transfers between devices: 358 us -> 57.9 us
  other arithmetic: 76.2 us -> 18.4 us
  blocking collectives: 146 us -> 91.1 us
  starting transfers between devices: 0.39 us -> 37.5 us
    unnamed x6 -> x1, waiting for transfers between devices: 204 us -> 0.02 us
    all_gather x3 -> x1, waiting for transfers between devices: 154 us -> 0.01 us  [shards(): lax.all_gather(out_master.astype(bf16), CTX, axis=0, tiled=True)]
    unnamed x2 -> x0, blocking collectives: 146 us -> none
    select_n x96 -> x0, other arithmetic: 68.2 us -> none  [hop(): return jax.tree.map(lambda a, b: jnp.where(reached, a, b), new, before)]
    all_to_all x0 -> x1, blocking collectives: none -> 66.9 us  [swap(): return lax.all_to_all(value, axes, 0, 0, tiled=True)]
    all_to_all x0 -> x7, waiting for transfers between devices: none -> 57.9 us  [swap(): return lax.all_to_all(value, axes, 0, 0, tiled=True)]
    all_to_all x0 -> x7, starting transfers between devices: none -> 37.5 us  [swap(): return lax.all_to_all(value, axes, 0, 0, tiled=True)]
    psum x0 -> x2, blocking collectives: none -> 24.3 us  [shards(): small = lax.psum(lax.psum(small, 'x'), 'z')]
  transfers between devices with their start and end apart: 5 -> 8, of which waited for: 4 -> 6; matrix products, arithmetic and copies ran while one was open for 12% -> 17% of each run, Pallas kernels for 0% -> 0%
where the time goes in v1:
time: 266 us; the launch traced here: 263 us
  blocking collectives  91.1 us (34%)
  waiting for transfers between devices  57.9 us (22%)
  starting transfers between devices  37.5 us (14%)
  matrix products  30.6 us (12%)
  other arithmetic  18.4 us (7%)
  between operations  14.4 us (5%)
  local copies, waits for them, and re-layouts  13.4 us (5%)
    all_to_all x1, blocking collectives, swap(): return lax.all_to_all(value, axes, 0, 0, tiled=True)  66.9 us
    all_to_all x7, waiting for transfers between devices, swap(): return lax.all_to_all(value, axes, 0, 0, tiled=True)  57.9 us
    all_to_all x7, starting transfers between devices, swap(): return lax.all_to_all(value, axes, 0, 0, tiled=True)  37.5 us
    psum x2, blocking collectives, shards(): small = lax.psum(lax.psum(small, 'x'), 'z')  24.3 us
    dot_general x11, matrix products, mm(): return lax.dot_general(a, b, (dims, ((), ())), preferred_element_type=f32)  22.4 us
    unnamed x44, local copies, waits for them, and re-layouts  7.68 us
  transfers between devices with their start and end apart: 8, of which 6 were waited for; matrix products, arithmetic and copies ran while one was open for 17% of the time, Pallas kernels for 0%

profile of v1, /device:TPU:8, one launch (start us, length us, event | category | flops | bytes accessed | tf_op | source)
XLA Modules:
  0.0 263.3 jit_solution(7897116591878659787)
XLA Ops:
  7.2 1.7 convert_element_type.86
  8.9 1.3 copy.51
  10.2 2.2 reduce-window.14
  12.7 0.2 exponential_reduce_fusion
  13.2 1.0 fusion.36
  14.3 0.7 pad_maximum_fusion.1
  15.0 11.3 %all-to-all-start = ((bf16[32,24,128]{2,1,0:T(8,128)(2,1)}), bf16[32,24,128]{2,1,0:T(8,128)(2,1)S(1)}, u32[]{:S(2)}, u32[]{:S(2)}) async-start(bf16[32,24,128]{2,1,0:T(8,128)(2,1)} %pad_maximum_fusion.1), calls=%async_computation | async-start | bytes 393216 | tf_op jit(solution)/shard_map/all_to_all | solution.py:37
  26.3 0.3 fusion.37
  26.6 11.8 %all-to-all-done = bf16[32,24,128]{2,1,0:T(8,128)(2,1)S(1)} async-done(((bf16[32,24,128]{2,1,0:T(8,128)(2,1)}), bf16[32,24,128]{2,1,0:T(8,128)(2,1)S(1)}, u32[]{:S(2)}, u32[]{:S(2)}) %all-to-all-start) | async-done | bytes 196640 | tf_op jit(solution)/shard_map/all_to_all | solution.py:37
  38.5 0.3 convert_reduce_fusion.1
  38.8 0.2 select_reduce_fusion
  39.0 0.3 fusion.7
  39.3 0.7 copy.70
  39.9 4.5 %all-to-all-start.3 = ((bf16[32,16,128]{2,1,0:T(8,128)(2,1)}), bf16[32,16,128]{2,1,0:T(8,128)(2,1)S(1)}, u32[]{:S(2)}, u32[]{:S(2)}) async-start(bf16[32,16,128]{2,1,0:T(8,128)(2,1)} %bitcast.40), calls=%async_computation.3 | async-start | bytes 262144 | tf_op jit(solution)/shard_map/all_to_all | solution.py:37
  44.4 3.2 %fusion = f32[8,512,64]{1,2,0:T(8,128)} fusion(bf16[512,8,64]{0,2,1:T(8,128)(2,1)S(1)} %bitcast.108, f32[512,512]{1,0:T(8,128)S(1)} %fusion.37, f32[8,512]{1,0:T(8,128)S(1)} %get-tuple-element.63), kind=kOutput, calls=%fused_computation.6 | convolution fusion | flops 278921216 | bytes 2637824 | tf_op jit(solution)/shard_map/hts,shp->thp/dot_general | solution.py:97
  47.8 7.3 %all-to-all-done.3 = bf16[32,16,128]{2,1,0:T(8,128)(2,1)S(1)} async-done(((bf16[32,16,128]{2,1,0:T(8,128)(2,1)}), bf16[32,16,128]{2,1,0:T(8,128)(2,1)S(1)}, u32[]{:S(2)}, u32[]{:S(2)}) %all-to-all-start.3) | async-done | bytes 131104 | tf_op jit(solution)/shard_map/all_to_all | solution.py:37
  55.1 1.6 fusion.3
  56.7 5.0 %convolution_convert_fusion = bf16[512,4096]{1,0:T(8,128)(2,1)S(1)} fusion(bf16[512,4096]{1,0:T(8,128)(2,1)} %param.14, f32[512,512]{0,1:T(8,128)S(1)} %fusion.3, bf16[512,512]{0,1:T(8,128)(2,1)S(1)} %copy.51, f32[512]{0:T(512)S(1)} %mul.104), kind=kOutput, calls=%fused_computation.4 | convolution fusion | flops 2150629376 | bytes 9963520 | tf_op jit(solution)/shard_map/dot_general | solution.py:23
  61.7 0.6 copy.81
  62.3 66.9 %all_to_all.48 = bf16[4,1024,512]{1,2,0:T(8,128)(2,1)} all-to-all(bf16[4,1024,512]{1,2,0:T(8,128)(2,1)S(1)} %bitcast.107), channel_id=1, replica_groups=mesh['x'=4,'z'=8,'y'=4,'core'=2] {'x'}, dimensions={0} | all-to-all | bytes 8388608 | tf_op jit(solution)/shard_map/all_to_all | solution.py:37
  129.2 3.4 %reduce_sum.128 = bf16[1024,512]{0,1:T(8,128)(2,1)S(1)} reduce(bf16[4,1024,512]{1,2,0:T(8,128)(2,1)} %all_to_all.48, bf16[]{:T(256)} %constant.13.clone.1), dimensions={0}, to_apply=%region_13.14 | reduce | flops 1572864 | bytes 5242882 | tf_op jit(solution)/shard_map/reduce_sum | solution.py:104
  132.6 1.2 copy_bitcast_fusion.1
  133.8 3.6 %all-to-all-start.7 = ((bf16[8,128,512]{1,2,0:T(8,128)(2,1)}), bf16[8,128,512]{1,2,0:T(8,128)(2,1)S(1)}, u32[]{:S(2)}, u32[]{:S(2)}) async-start(bf16[8,128,512]{1,2,0:T(8,128)(2,1)} %copy_bitcast_fusion.1), calls=%async_computation.7 | async-start | bytes 2097152 | tf_op jit(solution)/shard_map/all_to_all | solution.py:37
  137.3 0.8 copy.59
  138.2 0.7 mul.113
  138.9 0.8 copy.57
  139.7 25.3 %all-to-all-done.7 = bf16[8,128,512]{1,2,0:T(8,128)(2,1)S(1)} async-done(((bf16[8,128,512]{1,2,0:T(8,128)(2,1)}), bf16[8,128,512]{1,2,0:T(8,128)(2,1)S(1)}, u32[]{:S(2)}, u32[]{:S(2)}) %all-to-all-start.7) | async-done | bytes 1048608 | tf_op jit(solution)/shard_map/all_to_all | solution.py:37
  165.4 0.6 reduce_sum.132
  166.0 5.8 %fusion.12 = (bf16[512,512]{0,1:T(8,128)(2,1)S(1)}, bf16[512,512]{0,1:T(8,128)(2,1)S(1)}) fusion(f32[512,8]{0,1:T(8,128)S(1)} %get-tuple-element.62, bf16[512,4096]{1,0:T(8,128)(2,1)} %param.14, bf16[4096,512]{1,0:T(8,128)(2,1)} %all-gather.2.cloned.1.call-done), kind=kOutput, calls=%fused_computation.36 | convolution fusion | flops 2148532224 | bytes 9453568 | tf_op jit(solution)/shard_map/dot_general | solution.py:23
  171.9 1.0 convolution_convert_fusion.4
  172.8 4.0 %all-to-all-start.1 = ((bf16[32,16,128]{2,1,0:T(8,128)(2,1)}), bf16[32,16,128]{2,1,0:T(8,128)(2,1)S(1)}, u32[]{:S(2)}, u32[]{:S(2)}) async-start(bf16[32,16,128]{2,1,0:T(8,128)(2,1)} %bitcast.11), calls=%async_computation.1 | async-start | bytes 262144 | tf_op jit(solution)/shard_map/all_to_all | solution.py:37
  176.9 2.0 multiply_reduce_fusion
  178.9 2.4 fusion.1
  181.4 1.0 fusion.38
  182.4 5.1 %all-to-all-done.1 = bf16[32,16,128]{2,1,0:T(8,128)(2,1)S(1)} async-done(((bf16[32,16,128]{2,1,0:T(8,128)(2,1)}), bf16[32,16,128]{2,1,0:T(8,128)(2,1)S(1)}, u32[]{:S(2)}, u32[]{:S(2)}) %all-to-all-start.1) | async-done | bytes 131104 | tf_op jit(solution)/shard_map/all_to_all | solution.py:37
  187.5 0.3 fusion.6
  187.8 0.7 copy.68
  188.5 4.5 %all-to-all-start.2 = ((bf16[32,16,128]{2,1,0:T(8,128)(2,1)}), bf16[32,16,128]{2,1,0:T(8,128)(2,1)S(1)}, u32[]{:S(2)}, u32[]{:S(2)}) async-start(bf16[32,16,128]{2,1,0:T(8,128)(2,1)} %bitcast.36), calls=%async_computation.2 | async-start | bytes 262144 | tf_op jit(solution)/shard_map/all_to_all | solution.py:37
  193.0 1.0 fusion.39
  194.0 1.9 fusion.5
  196.0 7.3 %all-to-all-done.2 = bf16[32,16,128]{2,1,0:T(8,128)(2,1)S(1)} async-done(((bf16[32,16,128]{2,1,0:T(8,128)(2,1)}), bf16[32,16,128]{2,1,0:T(8,128)(2,1)S(1)}, u32[]{:S(2)}, u32[]{:S(2)}) %all-to-all-start.2) | async-done | bytes 131104 | tf_op jit(solution)/shard_map/all_to_all | solution.py:37
  203.3 0.6 copy-done.5
  203.9 2.3 fusion.15
  206.2 1.4 fusion.4
  207.7 0.7 pad_maximum_fusion
  208.4 4.8 %all-to-all-start.4 = ((bf16[8,128,128]{2,1,0:T(8,128)(2,1)}), bf16[8,128,128]{2,1,0:T(8,128)(2,1)}, u32[]{:S(2)}, u32[]{:S(2)}) async-start(bf16[8,128,128]{2,1,0:T(8,128)(2,1)} %bitcast.16), calls=%async_computation.4 | async-start | bytes 524288 | tf_op jit(solution)/shard_map/all_to_all | solution.py:37
  213.2 1.6 bitcast_reduce_fusion
  214.8 0.3 rev.7
  215.1 1.1 reduce-window.16
  216.5 8.9 %psum.14 = f32[16]{0:T(128)S(1)} all-reduce(f32[16]{0:T(128)S(1)} %pad_maximum_fusion.2), channel_id=1, replica_groups=mesh['x'=4,'z'=8,'y'=4,'core'=2] {'x'}, use_global_device_ids=true, to_apply=%region_17.18 | all-reduce | flops 16 | bytes 128 | tf_op jit(solution)/shard_map/psum | solution.py:143
  225.4 15.4 %psum.15 = f32[16]{0:T(128)S(1)} all-reduce(f32[16]{0:T(128)S(1)} %psum.14), channel_id=1, replica_groups=mesh['x'=4,'z'=8,'y'=4,'core'=2] {'z'}, use_global_device_ids=true, to_apply=%region_18.19 | all-reduce | flops 16 | bytes 128 | tf_op jit(solution)/shard_map/psum | solution.py:143
  240.8 0.6 sqrt_add_fusion
  241.5 1.2 multiply_subtract_fusion
  243.0 1.0 reduce_sum.120
  244.0 0.7 broadcast_in_dim.63
  244.7 4.8 %all-to-all-start.5 = ((bf16[8,128,128]{2,1,0:T(8,128)(2,1)}), bf16[8,128,128]{2,1,0:T(8,128)(2,1)S(1)}, u32[]{:S(2)}, u32[]{:S(2)}) async-start(bf16[8,128,128]{2,1,0:T(8,128)(2,1)} %broadcast_in_dim.63), calls=%async_computation.5 | async-start | bytes 524288 | tf_op jit(solution)/shard_map/all_to_all | solution.py:37
  249.5 1.2 multiply_reduce_fusion.2
  250.7 1.0 copy.60
  251.7 0.3 rev.8
  252.2 0.8 copy.61
  253.0 0.8 copy.62
  253.9 0.7 broadcast_add_fusion
  254.5 1.0 all-to-all-done.5
  255.6 0.8 fusion.35
  (68 shorter events, 2.3 us)
Async XLA Ops:
  7.2 6.0 %copy-start = (bf16[512,128]{1,0:T(8,128)(2,1)S(1)}, bf16[512,128]{1,0:T(8,128)(2,1)}, u32[]{:S(2)}) copy-start(bf16[512,128]{1,0:T(8,128)(2,1)} %param.10) | copy-start | bytes 393220
  7.2 19.1 %copy-start.2 = (bf16[512,128]{1,0:T(8,128)(2,1)S(1)}, bf16[512,128]{1,0:T(8,128)(2,1)}, u32[]{:S(2)}) copy-start(bf16[512,128]{1,0:T(8,128)(2,1)} %param.11) | copy-start | bytes 393220
  7.2 158.8 %all-gather.2.cloned.1.call-start = ((), (), s32[]{:S(2)}) async-start(), calls=%async_computation.8 | async-start | bytes 4325376 | tf_op jit(solution)/shard_map/all_gather | solution.py:64
  15.0 23.4 %all-to-all-start = ((bf16[32,24,128]{2,1,0:T(8,128)(2,1)}), bf16[32,24,128]{2,1,0:T(8,128)(2,1)S(1)}, u32[]{:S(2)}, u32[]{:S(2)}) async-start(bf16[32,24,128]{2,1,0:T(8,128)(2,1)} %pad_maximum_fusion.1), calls=%async_computation | async-start | bytes 393216 | tf_op jit(solution)/shard_map/all_to_all | solution.py:37
  26.6 21.0 %copy-start.7 = (f32[512,512]{1,0:T(8,128)}, f32[512,512]{1,0:T(8,128)S(1)}, u32[]{:S(2)}) copy-start(f32[512,512]{1,0:T(8,128)S(1)} %fusion.37) | copy-start | bytes 3145732
  39.9 15.2 %all-to-all-start.3 = ((bf16[32,16,128]{2,1,0:T(8,128)(2,1)}), bf16[32,16,128]{2,1,0:T(8,128)(2,1)S(1)}, u32[]{:S(2)}, u32[]{:S(2)}) async-start(bf16[32,16,128]{2,1,0:T(8,128)(2,1)} %bitcast.40), calls=%async_computation.3 | async-start | bytes 262144 | tf_op jit(solution)/shard_map/all_to_all | solution.py:37
  44.4 3.2 %copy-start.15 = (f32[8]{0:T(128)S(1)}, f32[8]{0:T(128)}, u32[]{:S(2)}) copy-start(f32[8]{0:T(128)} %param.13) | copy-start | bytes 100
  47.8 13.9 %copy-start.13 = (f32[512]{0:T(512)}, f32[512]{0:T(512)S(1)}, u32[]{:S(2)}) copy-start(f32[512]{0:T(512)S(1)} %mul.104) | copy-start | bytes 6148
  55.1 138.9 %copy-start.3 = (bf16[32,16,128]{2,1,0:T(8,128)(2,1)}, bf16[32,16,128]{2,1,0:T(8,128)(2,1)S(1)}, u32[]{:S(2)}) copy-start(bf16[32,16,128]{2,1,0:T(8,128)(2,1)S(1)} %all-to-all-done.3) | copy-start | bytes 393220
  56.7 5.0 %copy-start.1 = (f32[512,512]{0,1:T(8,128)}, f32[512,512]{0,1:T(8,128)S(1)}, u32[]{:S(2)}) copy-start(f32[512,512]{0,1:T(8,128)S(1)} %fusion.3) | copy-start | bytes 3145732
  129.2 8.1 %copy-start.9 = (f32[128,512]{1,0:T(8,128)S(1)}, f32[128,512]{1,0:T(8,128)}, u32[]{:S(2)}) copy-start(f32[128,512]{1,0:T(8,128)} %param.15) | copy-start | bytes 786436
  129.2 9.7 %copy-start.11 = (f32[128,512]{1,0:T(8,128)S(1)}, f32[128,512]{1,0:T(8,128)}, u32[]{:S(2)}) copy-start(f32[128,512]{1,0:T(8,128)} %param.16) | copy-start | bytes 786436
  133.8 31.3 %all-to-all-start.7 = ((bf16[8,128,512]{1,2,0:T(8,128)(2,1)}), bf16[8,128,512]{1,2,0:T(8,128)(2,1)S(1)}, u32[]{:S(2)}, u32[]{:S(2)}) async-start(bf16[8,128,512]{1,2,0:T(8,128)(2,1)} %copy_bitcast_fusion.1), calls=%async_computation.7 | async-start | bytes 2097152 | tf_op jit(solution)/shard_map/all_to_all | solution.py:37
  172.8 14.6 %all-to-all-start.1 = ((bf16[32,16,128]{2,1,0:T(8,128)(2,1)}), bf16[32,16,128]{2,1,0:T(8,128)(2,1)S(1)}, u32[]{:S(2)}, u32[]{:S(2)}) async-start(bf16[32,16,128]{2,1,0:T(8,128)(2,1)} %bitcast.11), calls=%async_computation.1 | async-start | bytes 262144 | tf_op jit(solution)/shard_map/all_to_all | solution.py:37
  176.9 2.0 copy-start.8
  188.5 14.8 %all-to-all-start.2 = ((bf16[32,16,128]{2,1,0:T(8,128)(2,1)}), bf16[32,16,128]{2,1,0:T(8,128)(2,1)S(1)}, u32[]{:S(2)}, u32[]{:S(2)}) async-start(bf16[32,16,128]{2,1,0:T(8,128)(2,1)} %bitcast.36), calls=%async_computation.2 | async-start | bytes 262144 | tf_op jit(solution)/shard_map/all_to_all | solution.py:37
  203.2 0.7 copy-start.5
  203.2 4.4 %copy-start.10 = (bf16[512,128]{1,0:T(8,128)(2,1)S(1)}, bf16[512,128]{1,0:T(8,128)(2,1)}, u32[]{:S(2)}) copy-start(bf16[512,128]{1,0:T(8,128)(2,1)} %fusion.5) | copy-start | bytes 393220
  206.2 10.0 %copy-start.14 = (f32[512]{0:T(512)S(1)}, f32[512]{0:T(512)}, u32[]{:S(2)}) copy-start(f32[512]{0:T(512)} %get-tuple-element.64) | copy-start | bytes 6148
  206.2 10.2 %copy-start.16 = (f32[8]{0:T(128)S(1)}, f32[8]{0:T(128)}, u32[]{:S(2)}) copy-start(f32[8]{0:T(128)} %reduce_sum.132) | copy-start | bytes 100
  206.2 34.5 %copy-start.17 = (f32[8]{0:T(128)S(1)}, f32[8]{0:T(128)}, u32[]{:S(2)}) copy-start(f32[8]{0:T(128)} %param.17) | copy-start | bytes 100
  206.2 43.3 %copy-start.12 = (f32[512]{0:T(512)S(1)}, f32[512]{0:T(512)}, u32[]{:S(2)}) copy-start(f32[512]{0:T(512)} %mul.113) | copy-start | bytes 6148
  207.7 41.9 %copy-start.4 = (bf16[32,16,128]{2,1,0:T(8,128)(2,1)S(1)}, bf16[32,16,128]{2,1,0:T(8,128)(2,1)}, u32[]{:S(2)}) copy-start(bf16[32,16,128]{2,1,0:T(8,128)(2,1)} %copy-done.3) | copy-start | bytes 393220
  207.7 41.9 %copy-start.6 = (bf16[32,16,128]{2,1,0:T(8,128)(2,1)S(1)}, bf16[32,16,128]{2,1,0:T(8,128)(2,1)}, u32[]{:S(2)}) copy-start(bf16[32,16,128]{2,1,0:T(8,128)(2,1)} %copy-done.5) | copy-start | bytes 393220
  208.4 34.6 %all-to-all-start.4 = ((bf16[8,128,128]{2,1,0:T(8,128)(2,1)}), bf16[8,128,128]{2,1,0:T(8,128)(2,1)}, u32[]{:S(2)}, u32[]{:S(2)}) async-start(bf16[8,128,128]{2,1,0:T(8,128)(2,1)} %bitcast.16), calls=%async_computation.4 | async-start | bytes 524288 | tf_op jit(solution)/shard_map/all_to_all | solution.py:37
  244.7 10.9 %all-to-all-start.5 = ((bf16[8,128,128]{2,1,0:T(8,128)(2,1)}), bf16[8,128,128]{2,1,0:T(8,128)(2,1)S(1)}, u32[]{:S(2)}, u32[]{:S(2)}) async-start(bf16[8,128,128]{2,1,0:T(8,128)(2,1)} %broadcast_in_dim.63), calls=%async_computation.5 | async-start | bytes 524288 | tf_op jit(solution)/shard_map/all_to_all | solution.py:37
Sparse Core Ops, SparseCore 0:
  11.2 114.4 all-gather.1

commit v2 on v1

v2 whole, which is shorter than its diff:
```python
import jax
import jax.numpy as jnp
from jax import lax
from jax.sharding import Mesh, PartitionSpec as P

WIDTH = 4096
beta_one = 0.9
beta_two = 0.95
learn_rate = 0.004
decoupled_decay = 0.1
adam_eps = 1e-08
bias_one = 0.9999734386011124
bias_two = 0.994079470779666

f32 = jnp.float32
bf16 = jnp.bfloat16
CTX = ("x", "z")
TP = ("y", "core")
BLOCKS = 32


def mm(a, b, dims):
    return lax.dot_general(a, b, (dims, ((), ())), preferred_element_type=f32)


def block_weights(logs):
    i = lax.broadcasted_iota(jnp.int32, (BLOCKS, BLOCKS, BLOCKS), 0)
    j = lax.broadcasted_iota(jnp.int32, (BLOCKS, BLOCKS, BLOCKS), 1)
    r = lax.broadcasted_iota(jnp.int32, (BLOCKS, BLOCKS, BLOCKS), 2)
    between = jnp.sum(jnp.where((r > j) & (r < i), logs[None, None, :], 0.0), axis=2)
    rows = lax.broadcasted_iota(jnp.int32, (BLOCKS, BLOCKS), 0)
    cols = lax.broadcasted_iota(jnp.int32, (BLOCKS, BLOCKS), 1)
    return jnp.where(rows > cols, jnp.exp(between), 0.0)


def exact(a, b, dims):
    return lax.dot_general(
        a.astype(f32),
        b.astype(f32),
        (dims, ((), ())),
        precision=lax.Precision.HIGHEST,
        preferred_element_type=f32,
    )


def swap(value, axes):
    return lax.all_to_all(value, axes, 0, 0, tiled=True)


def swap_core(value):
    return lax.ppermute(value, "core", [(0, 1), (1, 0)])


def spread(value, axis, count):
    return swap(jnp.broadcast_to(value[None], (count,) + value.shape), axis)


def chain(weights, parts, reverse):
    dims = ((0,), (0,)) if reverse else ((1,), (0,))
    out = exact(weights, parts.reshape(BLOCKS, 16 * 128), dims)
    return out.reshape(BLOCKS, 16, 128)


def shards(
    head_input,
    write_vector,
    read_vector,
    log_decay,
    skip_gain,
    out_grad,
    out_master,
    first_moment,
    squared_average,
):
    tokens, width = head_input.shape
    heads = log_decay.shape[0]
    head_width = width // heads

    core = lax.axis_index("core")
    ring = lax.axis_index("x")
    half = tokens // 2
    quarter = WIDTH // 4

    weight_rows = lax.all_gather(out_master.astype(bf16), "z", axis=0, tiled=True)
    pieces_out = []
    for step in (2, 1, 3, 0):
        to = lax.rem(ring + step, 4)
        piece = lax.dynamic_slice(out_grad, (core * half, to * quarter), (half, quarter))
        if step:
            piece = lax.ppermute(piece, "x", [(i, (i + step) % 4) for i in range(4)])
        pieces_out.append(piece)

    running = jnp.cumsum(log_decay, axis=1)
    last_sum = running[:, -1:]
    gap = running[:, :, None] - running[:, None, :]
    row_index = lax.broadcasted_iota(jnp.int32, gap.shape, 1)
    col_index = lax.broadcasted_iota(jnp.int32, gap.shape, 2)
    lower_decay = jnp.exp(jnp.where(row_index >= col_index, gap, -1e30))
    to_end = jnp.exp(last_sum - running)
    from_start = jnp.exp(running)
    to_end_wide = jnp.repeat(to_end.T, head_width, axis=1)
    from_start_wide = jnp.repeat(from_start.T, head_width, axis=1)
    skip_wide = jnp.repeat(skip_gain, head_width)[None, :]

    head_x = head_input.astype(f32)
    x_decayed = head_x * to_end_wide
    local_state = exact(x_decayed, write_vector, ((0,), (0,)))
    totals = jnp.broadcast_to(last_sum[:, None, :, None], (heads, BLOCKS // heads, 8, 128))
    packed = jnp.concatenate(
        [local_state.reshape(BLOCKS, 16, 128), totals.reshape(BLOCKS, 8, 128)], axis=1
    )
    packed = swap(packed, CTX)
    pieces_out, _ = lax.optimization_barrier((pieces_out, packed))
    ring_grad = jnp.zeros((4, tokens, quarter), bf16)
    for step, piece in zip((2, 1, 3, 0), pieces_out):
        came = lax.rem(ring + 4 - step, 4)
        ring_grad = lax.dynamic_update_slice(ring_grad, piece[None], (came, core * half, 0))
        ring_grad = lax.dynamic_update_slice(
            ring_grad, swap_core(piece)[None], (came, (1 - core) * half, 0)
        )
    ring_grad = ring_grad.reshape(4 * tokens, quarter)
    weights = block_weights(packed[:, 16, 0])
    start = swap(chain(weights, packed[:, :16], False), CTX).reshape(width, 128)

    scores = mm(read_vector, write_vector, ((1,), (1,)))
    mixed = (lower_decay * scores[None]).astype(bf16)
    x_heads = head_input.reshape(tokens, heads, head_width)
    inner = jnp.einsum("hts,shp->thp", mixed, x_heads, preferred_element_type=f32)
    core_y = inner.reshape(tokens, width) + exact(read_vector, start, ((1,), (1,))) * from_start_wide
    out_y = (core_y + skip_wide * head_x).astype(bf16)

    parts = mm(ring_grad, weight_rows, ((1,), (0,))).astype(bf16).reshape(4, tokens, width)
    parts, _ = lax.optimization_barrier((parts, start))
    grad_low = jnp.sum(swap(parts, "x").astype(f32), axis=0).astype(bf16)

    ring_y = lax.all_gather(out_y, "x", axis=0, tiled=True)
    partial = mm(ring_grad, ring_y, ((0,), (0,))).astype(bf16)
    weight_grad = lax.psum_scatter(partial, "z", scatter_dimension=0, tiled=True).astype(f32)

    grad = grad_low.astype(f32)
    grad_decayed = grad * from_start_wide
    carried = exact(grad_decayed, read_vector, ((0,), (0,)))
    carried = swap(carried.reshape(BLOCKS, 16, 128), CTX)
    end = swap(chain(weights, carried, True), CTX).reshape(width, 128)

    grad_heads = grad_low.reshape(tokens, heads, head_width)
    inner = jnp.einsum("hst,shp->thp", mixed, grad_heads, preferred_element_type=f32)
    core_grad = inner.reshape(tokens, width) + exact(write_vector, end, ((1,), (1,))) * to_end_wide
    input_grad = (core_grad + skip_wide * grad).astype(bf16)
    cross_dots = jnp.einsum("thp,shp->hts", grad_heads, x_heads, preferred_element_type=f32)
    pair_weights = jnp.sum(lower_decay * cross_dots, axis=0).astype(bf16)
    read_grad = mm(pair_weights, write_vector, ((1,), (0,))) + mm(
        grad_decayed.astype(bf16), start.astype(bf16), ((1,), (0,))
    )
    write_grad = mm(pair_weights, read_vector, ((0,), (0,))) + mm(
        x_decayed.astype(bf16), end.astype(bf16), ((1,), (0,))
    )
    both = jnp.concatenate([write_grad, read_grad], axis=0)
    keep = lax.dynamic_slice_in_dim(both, core * tokens, tokens, axis=0)
    give = lax.dynamic_slice_in_dim(both, (1 - core) * tokens, tokens, axis=0)
    keep = keep + swap_core(give)
    keep = jnp.sum(spread(keep.astype(bf16), "y", 4).astype(f32), axis=0)
    give = swap_core(keep)
    write_sum = jnp.where(core == 0, keep, give)
    read_sum = jnp.where(core == 0, give, keep)

    terms = (grad * core_y - head_x * core_grad).reshape(tokens, heads, head_width)
    decay_part = jnp.sum(terms, axis=2).T
    local_tail = jnp.flip(jnp.cumsum(jnp.flip(decay_part, 1), axis=1), 1)
    end_state = start.reshape(heads, -1) * jnp.exp(last_sum) + local_state.reshape(
        heads, -1
    )
    above = jnp.sum(end_state * end.reshape(heads, -1), axis=1)
    decay_grad = local_tail + above[:, None]

    skip_part = jnp.sum((grad * head_x).reshape(tokens, heads, head_width), axis=(0, 2))
    square_part = jnp.sum((weight_grad * weight_grad).reshape(-1, heads, head_width), axis=(0, 2))
    small = jnp.concatenate([skip_part, square_part, jnp.zeros((112,), f32)])
    small = spread(jnp.broadcast_to(small[None], (8, 128)), CTX, BLOCKS)
    small = jnp.sum(small, axis=0)[0]
    skip_total, square_total = small[:heads], small[heads : 2 * heads]
    mean_square = square_total / float(WIDTH * head_width)
    new_second = beta_two * squared_average + (1.0 - beta_two) * mean_square
    new_first = beta_one * first_moment + (1.0 - beta_one) * weight_grad
    scale = jnp.repeat(jnp.sqrt(new_second / bias_two) + adam_eps, head_width)
    new_master = out_master - learn_rate * (
        new_first / bias_one / scale[None, :] + decoupled_decay * out_master
    )
    return (
        input_grad,
        write_sum,
        read_sum,
        decay_grad,
        skip_total,
        new_master,
        new_first,
        new_second,
    )


def solution(mesh):
    fine = Mesh(mesh.devices.reshape(4, 8, 4, 2), ("x", "z", "y", "core"))
    in_specs = (
        P(CTX, TP),
        P(CTX, None),
        P(CTX, None),
        P(TP, CTX),
        P(TP),
        P(CTX, None),
        P(CTX, TP),
        P(CTX, TP),
        P(TP),
    )
    out_specs = (
        P(CTX, TP),
        P(CTX, None),
        P(CTX, None),
        P(TP, CTX),
        P(TP),
        P(CTX, TP),
        P(CTX, TP),
        P(TP),
    )
    return jax.shard_map(shards, mesh=fine, in_specs=in_specs, out_specs=out_specs, check_vma=False)
```

time: 266 us -> 277 us (1.041)
  blocking collectives: 91.1 us -> 31.1 us
  waiting for transfers between devices: 57.9 us -> 93.1 us
  local copies, waits for them, and re-layouts: 13.4 us -> 32.2 us
  starting transfers between devices: 37.5 us -> 51.5 us
  matrix products: 30.6 us -> 35.5 us
    all_to_all x1, blocking collectives: 66.9 us -> 31.1 us  [swap(): return lax.all_to_all(value, axes, 0, 0, tiled=True)]
    all_to_all x7 -> x6, waiting for transfers between devices: 57.9 us -> 24.7 us  [swap(): return lax.all_to_all(value, axes, 0, 0, tiled=True)]
    all_gather x1 -> x2, waiting for transfers between devices: 0.01 us -> 27.3 us  [the longest x1 27.3 us: shards(): ring_y = lax.all_gather(out_y, 'x', axis=0, tiled=True)]
    psum x2 -> x0, blocking collectives: 24.3 us -> none  [shards(): small = lax.psum(lax.psum(small, 'x'), 'z')]
    ppermute x0 -> x9, waiting for transfers between devices: none -> 23.6 us  [the longest x3 22.1 us: shards(): piece = lax.ppermute(piece, 'x', [(i, (i + step) % 4) for i in range(4)])]
    reduce_scatter x0 -> x1, waiting for transfers between devices: none -> 17.3 us  [shards(): lax.psum_scatter(partial, 'z', scatter_dimension=0, tiled=True).astype(f32)]
    dynamic_update_slice x0 -> x8, local copies, waits for them, and re-layouts: none -> 13 us  [the longest x4 7.55 us: shards(): lax.dynamic_update_slice(ring_grad, swap_core(piece)[None], (came, (1 - c...]
    dot_general x2 -> x6, matrix products: 0.58 us -> 9.69 us  [exact(): lax.dot_general(a.astype(f32), b.astype(f32), (dims, ((), ())), precision...]
  transfers between devices with their start and end apart: 8 -> 18, of which waited for: 6 -> 8; matrix products, arithmetic and copies ran while one was open for 17% -> 21% of each run, Pallas kernels for 0% -> 0%
where the time goes in v2:
time: 277 us; the launch traced here: 275 us
  waiting for transfers between devices  93.1 us (34%)
  starting transfers between devices  51.5 us (19%)
  matrix products  35.5 us (13%)
  local copies, waits for them, and re-layouts  32.2 us (12%)
  blocking collectives  31.1 us (11%)
  other arithmetic  17.8 us (6%)
  between operations  14.2 us (5%)
    all_to_all x6, starting transfers between devices, swap(): return lax.all_to_all(value, axes, 0, 0, tiled=True)  43.4 us
    all_to_all x1, blocking collectives, swap(): return lax.all_to_all(value, axes, 0, 0, tiled=True)  31.1 us
    all_gather x1, waiting for transfers between devices, shards(): ring_y = lax.all_gather(out_y, 'x', axis=0, tiled=True)  27.3 us
    all_to_all x6, waiting for transfers between devices, swap(): return lax.all_to_all(value, axes, 0, 0, tiled=True)  24.7 us
    ppermute x3, waiting for transfers between devices, shards(): piece = lax.ppermute(piece, 'x', [(i, (i + step) % 4) for i in range(4)])  22.1 us
    reduce_scatter x1, waiting for transfers between devices, shards(): lax.psum_scatter(partial, 'z', scatter_dimension=0, tiled=True).astype(f32)  17.3 us
    dot_general x7, matrix products, mm(): return lax.dot_general(a, b, (dims, ((), ())), preferred_element_type=f32)  15.4 us
    dot_general x6, matrix products, exact(): lax.dot_general(a.astype(f32), b.astype(f32), (dims, ((), ())), precision...  9.69 us
  transfers between devices with their start and end apart: 18, of which 8 were waited for; matrix products, arithmetic and copies ran while one was open for 21% of the time, Pallas kernels for 0%

profile of v2, /device:TPU:8, one launch (start us, length us, event | category | flops | bytes accessed | tf_op | source)
XLA Modules:
  0.0 275.4 jit_solution(4467924727664810374)
XLA Ops:
  7.2 1.3 copy.74
  8.5 2.2 reduce-window.14
  11.0 0.7 exponential_reduce_fusion
  12.1 0.6 fusion.41
  12.8 0.6 copy-done.2
  13.4 0.8 pad_maximum_fusion
  14.1 11.3 %all-to-all-start = ((f32[32,24,128]{2,1,0:T(8,128)}), f32[32,24,128]{2,1,0:T(8,128)S(1)}, u32[]{:S(2)}, u32[]{:S(2)}) async-start(f32[32,24,128]{2,1,0:T(8,128)} %pad_maximum_fusion), calls=%async_computation | async-start | bytes 786432 | tf_op jit(solution)/shard_map/all_to_all | solution.py:47
  25.6 2.7 fusion.40
  28.3 3.3 %collective-permute-start = (bf16[256,1024]{1,0:T(8,128)(2,1)}, bf16[256,1024]{1,0:T(8,128)(2,1)}, u32[]{:S(2)}, u32[]{:S(2)}) collective-permute-start(bf16[256,1024]{1,0:T(8,128)(2,1)} %get-tuple-element.76), channel_id=1, source_target_pairs={{0,128},{64,192},{128,0},{192,64},{1,129},{65,193},{129,1},{193,65... | collective-permute-start | bytes 1572872 | tf_op jit(solution)/shard_map/ppermute | solution.py:90
  31.6 0.6 collective-permute-start.1
  32.2 2.6 collective-permute-start.2
  34.8 0.7 convert_element_type.76
  35.6 12.1 %collective-permute-done = bf16[256,1024]{1,0:T(8,128)(2,1)} collective-permute-done((bf16[256,1024]{1,0:T(8,128)(2,1)}, bf16[256,1024]{1,0:T(8,128)(2,1)}, u32[]{:S(2)}, u32[]{:S(2)}) %collective-permute-start) | collective-permute-done | bytes 524320 | tf_op jit(solution)/shard_map/ppermute | solution.py:90
  47.7 10.0 %collective-permute-done.1 = bf16[256,1024]{1,0:T(8,128)(2,1)} collective-permute-done((bf16[256,1024]{1,0:T(8,128)(2,1)}, bf16[256,1024]{1,0:T(8,128)(2,1)}, u32[]{:S(2)}, u32[]{:S(2)}) %collective-permute-start.1) | collective-permute-done | bytes 524320 | tf_op jit(solution)/shard_map/ppermute | solution.py:90
  59.7 0.9 copy.76
  60.6 7.9 %all-to-all-start.1 = ((f32[32,16,128]{2,1,0:T(8,128)}), f32[32,16,128]{2,1,0:T(8,128)S(1)}, u32[]{:S(2)}, u32[]{:S(2)}) async-start(f32[32,16,128]{2,1,0:T(8,128)} %copy.76), calls=%async_computation.1 | async-start | bytes 524288 | tf_op jit(solution)/shard_map/all_to_all | solution.py:47
  68.5 2.5 broadcast_in_dim.85
  70.9 1.9 bitcast_dynamic-update-slice_fusion.7
  72.8 1.9 bitcast_dynamic-update-slice_fusion.6
  74.7 1.9 bitcast_dynamic-update-slice_fusion.5
  76.6 1.9 bitcast_dynamic-update-slice_fusion.4
  78.4 0.9 bitcast_dynamic-update-slice_fusion.3
  79.3 1.9 bitcast_dynamic-update-slice_fusion.2
  81.2 0.8 bitcast_dynamic-update-slice_fusion.1
  82.0 1.9 bitcast_dynamic-update-slice_fusion
  83.9 6.2 %convolution_convert_fusion = bf16[2048,512]{1,0:T(8,128)(2,1)} fusion(bf16[2048,1024]{1,0:T(8,128)(2,1)} %bitcast.13, bf16[1024,512]{1,0:T(8,128)(2,1)} %all-gather.3.cloned.1.call-done), kind=kOutput, calls=%fused_computation.6 | convolution fusion | flops 2148532224 | bytes 7340032 | tf_op jit(solution)/shard_map/dot_general | solution.py:23
  90.1 31.1 %all_to_all.35 = bf16[4,512,512]{2,1,0:T(8,128)(2,1)} all-to-all(bf16[4,512,512]{2,1,0:T(8,128)(2,1)} %bitcast.145), channel_id=1, replica_groups=mesh['x'=4,'z'=8,'y'=4,'core'=2] {'x'}, dimensions={0} | all-to-all | bytes 4194304 | tf_op jit(solution)/shard_map/all_to_all | solution.py:47
  121.2 2.2 reduce_sum.106
  123.7 1.3 fusion.28
  125.0 7.8 %all-to-all-start.3 = ((f32[32,16,128]{2,1,0:T(8,128)}), f32[32,16,128]{2,1,0:T(8,128)}, u32[]{:S(2)}, u32[]{:S(2)}) async-start(f32[32,16,128]{2,1,0:T(8,128)} %fusion.28), calls=%async_computation.3 | async-start | bytes 524288 | tf_op jit(solution)/shard_map/all_to_all | solution.py:47
  133.2 11.0 %all-to-all-done.3 = f32[32,16,128]{2,1,0:T(8,128)} async-done(((f32[32,16,128]{2,1,0:T(8,128)}), f32[32,16,128]{2,1,0:T(8,128)}, u32[]{:S(2)}, u32[]{:S(2)}) %all-to-all-start.3) | async-done | bytes 262176 | tf_op jit(solution)/shard_map/all_to_all | solution.py:47
  144.2 1.4 fusion.18
  145.6 0.9 copy.81
  146.4 4.2 %all-to-all-start.4 = ((f32[32,16,128]{2,1,0:T(8,128)}), f32[32,16,128]{2,1,0:T(8,128)S(1)}, u32[]{:S(2)}, u32[]{:S(2)}) async-start(f32[32,16,128]{2,1,0:T(8,128)} %copy.81), calls=%async_computation.4 | async-start | bytes 524288 | tf_op jit(solution)/shard_map/all_to_all | solution.py:47
  150.7 4.0 %fusion = f32[8,512,64]{1,2,0:T(8,128)} fusion(bf16[512,8,64]{0,2,1:T(8,128)(2,1)S(1)} %bitcast.134, f32[512,512]{1,0:T(8,128)S(1)} %fusion.42, f32[8,512]{1,0:T(8,128)} %copy-done.14), kind=kOutput, calls=%fused_computation.4 | convolution fusion | flops 278921216 | bytes 2637824 | tf_op jit(solution)/shard_map/hts,shp->thp/dot_general | solution.py:128
  154.7 0.7 broadcast_in_dim.104
  155.4 1.3 mul.153
  156.7 2.0 fusion.3
  158.7 3.6 %fusion.1 = f32[8,64,512]{2,1,0:T(8,128)} fusion(bf16[512,8,64]{0,2,1:T(8,128)(2,1)S(1)} %bitcast.136, f32[512,512]{1,0:T(8,128)} %copy-done.7, f32[8,512]{1,0:T(8,128)} %copy-done.14), kind=kOutput, calls=%fused_computation.5 | convolution fusion | flops 278921216 | bytes 2637824 | tf_op jit(solution)/shard_map/hst,shp->thp/dot_general | solution.py:147
  162.3 4.0 %fusion.9 = (f32[512]{0:T(512)}, bf16[512,512]{0,1:T(8,128)(2,1)}, bf16[512,512]{0,1:T(8,128)(2,1)}, f32[512,512]{0,1:T(8,128)}) fusion(bf16[512,512]{0,1:T(8,128)(2,1)S(1)} %copy.74, bf16[512,512]{0,1:T(8,128)(2,1)S(1)} %copy.77, f32[512]{0:T(512)} %mul.153, f32[512,512]{0,1:T(8,128)S(1)} %fusion.3, f32[512,512]{0,1:T(8,128)} %bitcast.146, ...), kind=kOutput, calls=%fused_computation.28 | convolution fusion | flops 405798400 | bytes 5656576 | tf_op jit(solution)/shard_map/dot_general | solution.py:37
  166.4 1.3 mul.164
  167.7 1.3 mul.165
  169.0 2.8 %multiply_reduce_fusion = bf16[512,512]{1,0:T(8,128)(2,1)S(1)} fusion(f32[8,512]{1,0:T(8,128)} %copy-done.14, bf16[512,8,64]{0,2,1:T(8,128)(2,1)S(1)} %bitcast.137, bf16[512,8,64]{0,2,1:T(8,128)(2,1)S(1)} %bitcast.135), kind=kOutput, calls=%fused_computation | convolution fusion | flops 278659072 | bytes 1589248 | tf_op jit(solution)/shard_map/thp,shp->hts/dot_general | solution.py:150
  171.8 1.0 fusion.44
  172.8 1.0 fusion.43
  173.8 27.3 %all-gather.5.cloned.1.call-done = bf16[2048,512]{0,1:T(8,128)(2,1)} async-done(((bf16[512,512]{0,1:T(8,128)(2,1)}), bf16[2048,512]{0,1:T(8,128)(2,1)}) %all-gather.5.cloned.1.call-update) | async-done | bytes 2097168 | tf_op jit(solution)/shard_map/all_gather | solution.py:136
  201.2 6.2 %convolution_convert_fusion.1 = bf16[1024,512]{1,0:T(8,128)(2,1)} fusion(bf16[2048,1024]{1,0:T(8,128)(2,1)} %bitcast.13, bf16[2048,512]{0,1:T(8,128)(2,1)} %all-gather.5.cloned.1.call-done), kind=kOutput, calls=%fused_computation.16 | convolution fusion | flops 2148007936 | bytes 7340032 | tf_op jit(solution)/shard_map/dot_general | solution.py:23
  207.4 2.2 multiply_reduce_fusion.1
  209.6 2.2 bitcast_reduce_fusion
  213.1 1.5 collective-permute-done.7
  214.8 0.9 broadcast_in_dim.105
  215.6 4.8 %all-to-all-start.5 = ((bf16[4,512,128]{2,1,0:T(8,128)(2,1)}), bf16[4,512,128]{2,1,0:T(8,128)(2,1)S(1)}, u32[]{:S(2)}, u32[]{:S(2)}) async-start(bf16[4,512,128]{2,1,0:T(8,128)(2,1)} %broadcast_in_dim.105), calls=%async_computation.5 | async-start | bytes 1048576 | tf_op jit(solution)/shard_map/all_to_all | solution.py:47
  220.7 1.1 reduce-window.16
  222.8 5.9 %all-to-all-done.5 = bf16[4,512,128]{2,1,0:T(8,128)(2,1)S(1)} async-done(((bf16[4,512,128]{2,1,0:T(8,128)(2,1)}), bf16[4,512,128]{2,1,0:T(8,128)(2,1)S(1)}, u32[]{:S(2)}, u32[]{:S(2)}) %all-to-all-start.5) | async-done | bytes 524320 | tf_op jit(solution)/shard_map/all_to_all | solution.py:47
  228.9 17.3 %reduce-scatter.2.cloned.1.call-done = bf16[128,512]{1,0:T(8,128)(2,1)} async-done(((bf16[1024,512]{1,0:T(8,128)(2,1)}), bf16[128,512]{1,0:T(8,128)(2,1)}) %reduce-scatter.2.cloned.1.call-update) | async-done | bytes 131088 | tf_op jit(solution)/shard_map/reduce_scatter | solution.py:138
  246.2 1.0 fusion.12
  247.5 0.7 broadcast_in_dim_broadcast_in_dim_broadcast_in_dim.2
  248.2 7.4 %all-to-all-start.6 = ((f32[32,8,128]{2,1,0:T(8,128)}), f32[32,8,128]{2,1,0:T(8,128)S(1)}, u32[]{:S(2)}, u32[]{:S(2)}) async-start(f32[32,8,128]{2,1,0:T(8,128)} %broadcast_in_dim_broadcast_in_dim_broadcast_in_dim.2), calls=%async_computation.7 | async-start | bytes 262144 | tf_op jit(solution)/shard_map/all_to_all | solution.py:47
  255.5 0.7 broadcast_add_fusion
  256.2 1.0 copy.83
  257.2 0.8 broadcast_select_fusion
  258.0 7.8 %all-to-all-done.6 = f32[32,8,128]{2,1,0:T(8,128)S(1)} async-done(((f32[32,8,128]{2,1,0:T(8,128)}), f32[32,8,128]{2,1,0:T(8,128)S(1)}, u32[]{:S(2)}, u32[]{:S(2)}) %all-to-all-start.6) | async-done | bytes 131104 | tf_op jit(solution)/shard_map/all_to_all | solution.py:47
  266.4 0.6 sqrt_add_fusion
  267.1 1.8 multiply_subtract_fusion
  (100 shorter events, 7.3 us)
Async XLA Ops:
  7.2 4.9 %copy-start = (bf16[512,128]{1,0:T(8,128)(2,1)S(1)}, bf16[512,128]{1,0:T(8,128)(2,1)}, u32[]{:S(2)}) copy-start(bf16[512,128]{1,0:T(8,128)(2,1)} %param.10) | copy-start | bytes 393220
  11.0 0.9 copy-start.14
  11.8 13.8 %copy-start.12 = (f32[512,8]{0,1:T(8,128)}, f32[512,8]{0,1:T(8,128)S(1)}, u32[]{:S(2)}) copy-start(f32[512,8]{0,1:T(8,128)S(1)} %exponential_bitcast_fusion.1) | copy-start | bytes 49156
  11.9 22.9 %copy-start.9 = (f32[128,512]{1,0:T(8,128)S(1)}, f32[128,512]{1,0:T(8,128)}, u32[]{:S(2)}) copy-start(f32[128,512]{1,0:T(8,128)} %param.15) | copy-start | bytes 786436
  12.7 0.7 copy-start.2
  14.1 43.5 %all-to-all-start = ((f32[32,24,128]{2,1,0:T(8,128)}), f32[32,24,128]{2,1,0:T(8,128)S(1)}, u32[]{:S(2)}, u32[]{:S(2)}) async-start(f32[32,24,128]{2,1,0:T(8,128)} %pad_maximum_fusion), calls=%async_computation | async-start | bytes 786432 | tf_op jit(solution)/shard_map/all_to_all | solution.py:47
  25.5 58.4 %all-gather.3.cloned.1.call-start = ((), (), s32[]{:S(2)}) async-start(), calls=%async_computation.8 | async-start | bytes 1179648 | tf_op jit(solution)/shard_map/all_gather | solution.py:84
  28.3 19.4 %collective-permute-start = (bf16[256,1024]{1,0:T(8,128)(2,1)}, bf16[256,1024]{1,0:T(8,128)(2,1)}, u32[]{:S(2)}, u32[]{:S(2)}) collective-permute-start(bf16[256,1024]{1,0:T(8,128)(2,1)} %get-tuple-element.76), channel_id=1, source_target_pairs={{0,128},{64,192},{128,0},{192,64},{1,129},{65,193},{129,1},{193,65... | collective-permute-start | bytes 1572872 | tf_op jit(solution)/shard_map/ppermute | solution.py:90
  31.6 26.1 %collective-permute-start.1 = (bf16[256,1024]{1,0:T(8,128)(2,1)}, bf16[256,1024]{1,0:T(8,128)(2,1)}, u32[]{:S(2)}, u32[]{:S(2)}) collective-permute-start(bf16[256,1024]{1,0:T(8,128)(2,1)} %get-tuple-element.75), channel_id=1, source_target_pairs={{0,64},{64,128},{128,192},{192,0},{1,65},{65,129},{129,193},{193,1... | collective-permute-start | bytes 1572872 | tf_op jit(solution)/shard_map/ppermute | solution.py:90
  32.2 25.5 %collective-permute-start.2 = (bf16[256,1024]{1,0:T(8,128)(2,1)}, bf16[256,1024]{1,0:T(8,128)(2,1)S(1)}, u32[]{:S(2)}, u32[]{:S(2)}) collective-permute-start(bf16[256,1024]{1,0:T(8,128)(2,1)} %get-tuple-element.77), channel_id=1, source_target_pairs={{0,192},{64,0},{128,64},{192,128},{1,193},{65,1},{129,65},{193,129... | collective-permute-start | bytes 1572872 | tf_op jit(solution)/shard_map/ppermute | solution.py:90
  57.7 15.1 %collective-permute-start.3 = (bf16[256,1024]{1,0:T(8,128)(2,1)}, bf16[256,1024]{1,0:T(8,128)(2,1)}, u32[]{:S(2)}, u32[]{:S(2)}) collective-permute-start(bf16[256,1024]{1,0:T(8,128)(2,1)} %collective-permute-done), channel_id=1, source_target_pairs={{0,1},{1,0},{2,3},{3,2},{4,5},{5,4},{6,7},{7,6},{8,9},{9,8},{10,11... | collective-permute-start | bytes 1572872 | tf_op jit(solution)/shard_map/ppermute | solution.py:51
  57.7 18.8 %collective-permute-start.4 = (bf16[256,1024]{1,0:T(8,128)(2,1)}, bf16[256,1024]{1,0:T(8,128)(2,1)}, u32[]{:S(2)}, u32[]{:S(2)}) collective-permute-start(bf16[256,1024]{1,0:T(8,128)(2,1)} %collective-permute-done.1), channel_id=1, source_target_pairs={{0,1},{1,0},{2,3},{3,2},{4,5},{5,4},{6,7},{7,6},{8,9},{9,8},{10,11... | collective-permute-start | bytes 1572872 | tf_op jit(solution)/shard_map/ppermute | solution.py:51
  58.2 21.1 %collective-permute-start.5 = (bf16[256,1024]{1,0:T(8,128)(2,1)S(1)}, bf16[256,1024]{1,0:T(8,128)(2,1)}, u32[]{:S(2)}, u32[]{:S(2)}) collective-permute-start(bf16[256,1024]{1,0:T(8,128)(2,1)S(1)} %collective-permute-done.2), channel_id=1, source_target_pairs={{0,1},{1,0},{2,3},{3,2},{4,5},{5,4},{6,7},{7,6},{8,9},{9,8},{10,11... | collective-permute-start | bytes 1572872 | tf_op jit(solution)/shard_map/ppermute | solution.py:51
  58.3 23.7 %collective-permute-start.6 = (bf16[256,1024]{1,0:T(8,128)(2,1)S(1)}, bf16[256,1024]{1,0:T(8,128)(2,1)}, u32[]{:S(2)}, u32[]{:S(2)}) collective-permute-start(bf16[256,1024]{1,0:T(8,128)(2,1)S(1)} %get-tuple-element.16), channel_id=1, source_target_pairs={{0,1},{1,0},{2,3},{3,2},{4,5},{5,4},{6,7},{7,6},{8,9},{9,8},{10,11... | collective-permute-start | bytes 1572872 | tf_op jit(solution)/shard_map/ppermute | solution.py:51
  59.2 15.4 %copy-start.13 = (f32[32,32]{1,0:T(8,128)}, f32[32,32]{1,0:T(8,128)S(1)}, u32[]{:S(2)}) copy-start(f32[32,32]{1,0:T(8,128)S(1)} %select_reduce_fusion) | copy-start | bytes 12292
  60.6 29.5 %all-to-all-start.1 = ((f32[32,16,128]{2,1,0:T(8,128)}), f32[32,16,128]{2,1,0:T(8,128)S(1)}, u32[]{:S(2)}, u32[]{:S(2)}) async-start(f32[32,16,128]{2,1,0:T(8,128)} %copy.76), calls=%async_computation.1 | async-start | bytes 524288 | tf_op jit(solution)/shard_map/all_to_all | solution.py:47
  90.1 31.1 %copy-start.1 = (f32[32,16,128]{2,1,0:T(8,128)}, f32[32,16,128]{2,1,0:T(8,128)S(1)}, u32[]{:S(2)}) copy-start(f32[32,16,128]{2,1,0:T(8,128)S(1)} %all-to-all-done.1) | copy-start | bytes 786436
  90.1 33.6 %copy-start.4 = (bf16[512,128]{1,0:T(8,128)(2,1)S(1)}, bf16[512,128]{1,0:T(8,128)(2,1)}, u32[]{:S(2)}) copy-start(bf16[512,128]{1,0:T(8,128)(2,1)} %param.11) | copy-start | bytes 393220
  125.0 19.1 %all-to-all-start.3 = ((f32[32,16,128]{2,1,0:T(8,128)}), f32[32,16,128]{2,1,0:T(8,128)}, u32[]{:S(2)}, u32[]{:S(2)}) async-start(f32[32,16,128]{2,1,0:T(8,128)} %fusion.28), calls=%async_computation.3 | async-start | bytes 524288 | tf_op jit(solution)/shard_map/all_to_all | solution.py:47
  133.1 21.6 %copy-start.7 = (f32[512,512]{1,0:T(8,128)}, f32[512,512]{1,0:T(8,128)S(1)}, u32[]{:S(2)}) copy-start(f32[512,512]{1,0:T(8,128)S(1)} %fusion.42) | copy-start | bytes 3145732
  146.4 15.9 %all-to-all-start.4 = ((f32[32,16,128]{2,1,0:T(8,128)}), f32[32,16,128]{2,1,0:T(8,128)S(1)}, u32[]{:S(2)}, u32[]{:S(2)}) async-start(f32[32,16,128]{2,1,0:T(8,128)} %copy.81), calls=%async_computation.4 | async-start | bytes 524288 | tf_op jit(solution)/shard_map/all_to_all | solution.py:47
  150.6 50.6 %all-gather.5.cloned.1.call-start = ((), (), s32[]{:S(2)}) async-start(), calls=%async_computation.9 | async-start | bytes 2621440 | tf_op jit(solution)/shard_map/all_gather | solution.py:136
  150.7 4.0 %copy-start.18 = (f32[8]{0:T(128)S(1)}, f32[8]{0:T(128)}, u32[]{:S(2)}) copy-start(f32[8]{0:T(128)} %param.13) | copy-start | bytes 100
  166.3 79.9 %reduce-scatter.2.cloned.1.call-start = ((), (), s32[]{:S(2)}) async-start(), calls=%async_computation.10 | async-start | bytes 1179648 | tf_op jit(solution)/shard_map/reduce_scatter | solution.py:138
  169.0 2.8 %copy-start.5 = (bf16[512,128]{1,0:T(8,128)(2,1)S(1)}, bf16[512,128]{1,0:T(8,128)(2,1)}, u32[]{:S(2)}) copy-start(bf16[512,128]{1,0:T(8,128)(2,1)} %param.11) | copy-start | bytes 393220
  207.4 4.4 %copy-start.8 = (f32[512,128]{1,0:T(8,128)S(1)}, f32[512,128]{1,0:T(8,128)}, u32[]{:S(2)}) copy-start(f32[512,128]{1,0:T(8,128)} %fusion.43) | copy-start | bytes 786436
  207.4 4.8 %copy-start.6 = (f32[512,128]{1,0:T(8,128)S(1)}, f32[512,128]{1,0:T(8,128)}, u32[]{:S(2)}) copy-start(f32[512,128]{1,0:T(8,128)} %fusion.44) | copy-start | bytes 786436
  211.8 8.6 %copy-start.15 = (f32[512,8]{0,1:T(8,128)S(1)}, f32[512,8]{0,1:T(8,128)}, u32[]{:S(2)}) copy-start(f32[512,8]{0,1:T(8,128)} %get-tuple-element.81) | copy-start | bytes 49156
  211.8 10.6 %copy-start.17 = (f32[32]{0:T(128)S(1)}, f32[32]{0:T(128)}, u32[]{:S(2)}) copy-start(f32[32]{0:T(128)} %get-tuple-element.85) | copy-start | bytes 388
  211.8 10.8 %copy-start.16 = (f32[512]{0:T(512)S(1)}, f32[512]{0:T(512)}, u32[]{:S(2)}) copy-start(f32[512]{0:T(512)} %get-tuple-element.78) | copy-start | bytes 6148
  211.8 44.4 %copy-start.3 = (bf16[512,512]{0,1:T(8,128)(2,1)S(1)}, bf16[512,512]{0,1:T(8,128)(2,1)}, u32[]{:S(2)}) copy-start(bf16[512,512]{0,1:T(8,128)(2,1)} %get-tuple-element.79) | copy-start | bytes 1572868
  212.2 54.2 %copy-start.19 = (f32[8]{0:T(128)S(1)}, f32[8]{0:T(128)}, u32[]{:S(2)}) copy-start(f32[8]{0:T(128)} %param.17) | copy-start | bytes 100
  212.2 54.9 %copy-start.10 = (f32[128,512]{1,0:T(8,128)S(1)}, f32[128,512]{1,0:T(8,128)}, u32[]{:S(2)}) copy-start(f32[128,512]{1,0:T(8,128)} %param.15) | copy-start | bytes 786436
  212.2 54.9 %copy-start.11 = (f32[128,512]{1,0:T(8,128)S(1)}, f32[128,512]{1,0:T(8,128)}, u32[]{:S(2)}) copy-start(f32[128,512]{1,0:T(8,128)} %param.16) | copy-start | bytes 786436
  212.7 1.8 collective-permute-start.7
  215.6 13.1 %all-to-all-start.5 = ((bf16[4,512,128]{2,1,0:T(8,128)(2,1)}), bf16[4,512,128]{2,1,0:T(8,128)(2,1)S(1)}, u32[]{:S(2)}, u32[]{:S(2)}) async-start(bf16[4,512,128]{2,1,0:T(8,128)(2,1)} %broadcast_in_dim.105), calls=%async_computation.5 | async-start | bytes 1048576 | tf_op jit(solution)/shard_map/all_to_all | solution.py:47
  228.8 28.4 %collective-permute-start.8 = (f32[512,128]{1,0:T(8,128)S(1)}, f32[512,128]{1,0:T(8,128)S(1)}, u32[]{:S(2)}, u32[]{:S(2)}) collective-permute-start(f32[512,128]{1,0:T(8,128)S(1)} %convert_reduce_fusion), channel_id=1, source_target_pairs={{0,1},{1,0},{2,3},{3,2},{4,5},{5,4},{6,7},{7,6},{8,9},{9,8},{10,11... | collective-permute-start | bytes 786440 | tf_op jit(solution)/shard_map/ppermute | solution.py:51
  248.2 17.7 %all-to-all-start.6 = ((f32[32,8,128]{2,1,0:T(8,128)}), f32[32,8,128]{2,1,0:T(8,128)S(1)}, u32[]{:S(2)}, u32[]{:S(2)}) async-start(f32[32,8,128]{2,1,0:T(8,128)} %broadcast_in_dim_broadcast_in_dim_broadcast_in_dim.2), calls=%async_computation.7 | async-start | bytes 262144 | tf_op jit(solution)/shard_map/all_to_all | solution.py:47
Sparse Core Ops, SparseCore 0:
  35.6 37.3 all-gather.2
  166.4 34.6 all-gather.4
  207.5 38.6 reduce-scatter.1

commit v3 on v2

--- a/solution.py
+++ b/solution.py
@@ -1,6 +1,8 @@
 import jax
 import jax.numpy as jnp
 from jax import lax
+from jax.experimental import pallas as pl
+from jax.experimental.pallas import tpu as pltpu
 from jax.sharding import Mesh, PartitionSpec as P
 
 WIDTH = 4096
@@ -51,8 +53,80 @@
     return lax.ppermute(value, "core", [(0, 1), (1, 0)])
 
 
+def ring_shift(value, step):
+    return lax.ppermute(value, "x", [(i, (i + step) % 4) for i in range(4)]) if step else value
+
+
 def spread(value, axis, count):
     return swap(jnp.broadcast_to(value[None], (count,) + value.shape), axis)
+
+
+def ring_grad_kernel(core_ref, own_ref, other_ref, weight_ref, out_ref):
+    half = own_ref.shape[0]
+    core = core_ref[0]
+    for ref, at in ((own_ref, core), (other_ref, 1 - core)):
+        out_ref[pl.ds(pl.multiple_of(at * half, half), half), :] = jnp.dot(
+            ref[...], weight_ref[...], preferred_element_type=f32
+        ).astype(bf16)
+
+
+def ring_grad_part(core, own, other, weight_rows):
+    half, quarter = own.shape
+    width = weight_rows.shape[1]
+    return pl.pallas_call(
+        ring_grad_kernel,
+        out_shape=jax.ShapeDtypeStruct((2 * half, width), bf16),
+        grid=(2,),
+        in_specs=[
+            pl.BlockSpec(memory_space=pltpu.SMEM),
+            pl.BlockSpec((half, quarter), lambda j: (0, 0)),
+            pl.BlockSpec((half, quarter), lambda j: (0, 0)),
+            pl.BlockSpec((quarter, width // 2), lambda j: (0, j)),
+        ],
+        out_specs=pl.BlockSpec((2 * half, width // 2), lambda j: (0, j)),
+        cost_estimate=pl.CostEstimate(
+            flops=4 * half * quarter * width, bytes_accessed=3 << 20, transcendentals=0
+        ),
+        compiler_params=pltpu.CompilerParams(vmem_limit_bytes=24 << 20),
+        name="ring_grad",
+    )(core, own, other, weight_rows)
+
+
+def weight_grad_kernel(core_ref, *refs):
+    owns, others, ys, out_ref = refs[:4], refs[4:8], refs[8:12], refs[12]
+    half = owns[0].shape[0]
+    core = core_ref[0]
+    total = None
+    for own, other, y in zip(owns, others, ys):
+        for ref, at in ((own, core), (other, 1 - core)):
+            part = lax.dot_general(
+                ref[...],
+                y[pl.ds(pl.multiple_of(at * half, half), half), :],
+                (((0,), (0,)), ((), ())),
+                preferred_element_type=f32,
+            )
+            total = part if total is None else total + part
+    out_ref[...] = total.astype(bf16)
+
+
+def weight_grad_part(core, owns, others, ys):
+    half, quarter = owns[0].shape
+    width = ys[0].shape[1]
+    tile = 256
+    return pl.pallas_call(
+        weight_grad_kernel,
+        out_shape=jax.ShapeDtypeStruct((quarter, width), bf16),
+        grid=(quarter // tile,),
+        in_specs=[pl.BlockSpec(memory_space=pltpu.SMEM)]
+        + [pl.BlockSpec((half, tile), lambda j: (0, j))] * 8
+        + [pl.BlockSpec((2 * half, width), lambda j: (0, 0))] * 4,
+        out_specs=pl.BlockSpec((tile, width), lambda j: (j, 0)),
+        cost_estimate=pl.CostEstimate(
+            flops=16 * half * quarter * width, bytes_accessed=8 << 20, transcendentals=0
+        ),
+        compiler_params=pltpu.CompilerParams(vmem_limit_bytes=24 << 20),
+        name="weight_grad",
+    )(core, *owns, *others, *ys)
 
 
 def chain(weights, parts, reverse):
@@ -82,13 +156,11 @@
     quarter = WIDTH // 4
 
     weight_rows = lax.all_gather(out_master.astype(bf16), "z", axis=0, tiled=True)
-    pieces_out = []
-    for step in (2, 1, 3, 0):
+    owns = []
+    for step in range(4):
         to = lax.rem(ring + step, 4)
         piece = lax.dynamic_slice(out_grad, (core * half, to * quarter), (half, quarter))
-        if step:
-            piece = lax.ppermute(piece, "x", [(i, (i + step) % 4) for i in range(4)])
-        pieces_out.append(piece)
+        owns.append(ring_shift(piece, step))
 
     running = jnp.cumsum(log_decay, axis=1)
     last_sum = running[:, -1:]
@@ -110,15 +182,6 @@
         [local_state.reshape(BLOCKS, 16, 128), totals.reshape(BLOCKS, 8, 128)], axis=1
     )
     packed = swap(packed, CTX)
-    pieces_out, _ = lax.optimization_barrier((pieces_out, packed))
-    ring_grad = jnp.zeros((4, tokens, quarter), bf16)
-    for step, piece in zip((2, 1, 3, 0), pieces_out):
-        came = lax.rem(ring + 4 - step, 4)
-        ring_grad = lax.dynamic_update_slice(ring_grad, piece[None], (came, core * half, 0))
-        ring_grad = lax.dynamic_update_slice(
-            ring_grad, swap_core(piece)[None], (came, (1 - core) * half, 0)
-        )
-    ring_grad = ring_grad.reshape(4 * tokens, quarter)
     weights = block_weights(packed[:, 16, 0])
     start = swap(chain(weights, packed[:, :16], False), CTX).reshape(width, 128)
 
@@ -129,12 +192,19 @@
     core_y = inner.reshape(tokens, width) + exact(read_vector, start, ((1,), (1,))) * from_start_wide
     out_y = (core_y + skip_wide * head_x).astype(bf16)
 
-    parts = mm(ring_grad, weight_rows, ((1,), (0,))).astype(bf16).reshape(4, tokens, width)
-    parts, _ = lax.optimization_barrier((parts, start))
-    grad_low = jnp.sum(swap(parts, "x").astype(f32), axis=0).astype(bf16)
-
-    ring_y = lax.all_gather(out_y, "x", axis=0, tiled=True)
-    partial = mm(ring_grad, ring_y, ((0,), (0,))).astype(bf16)
+    owns, _ = lax.optimization_barrier((owns, start))
+    others = [swap_core(piece) for piece in owns]
+    core_one = jnp.full((1,), core, jnp.int32)
+    parts = [
+        ring_shift(ring_grad_part(core_one, owns[step], others[step], weight_rows), 4 - step)
+        for step in (2, 1, 3)
+    ]
+    parts.append(ring_grad_part(core_one, owns[0], others[0], weight_rows))
+    ring_y = [ring_shift(out_y, step) for step in range(4)]
+    parts, _ = lax.optimization_barrier((parts, out_y))
+    grad_low = sum(part.astype(f32) for part in parts).astype(bf16)
+
+    partial = weight_grad_part(core_one, owns, others, ring_y)
     weight_grad = lax.psum_scatter(partial, "z", scatter_dimension=0, tiled=True).astype(f32)
 
     grad = grad_low.astype(f32)

time: 277 us -> 216 us (0.78)
  waiting for transfers between devices: 93.1 us -> 52.9 us
  blocking collectives: 31.1 us -> 0 us
  Pallas kernels: 0 us -> 12 us
  starting transfers between devices: 51.5 us -> 57.4 us
  matrix products: 35.5 us -> 30.2 us
    all_to_all x1 -> x0, blocking collectives: 31.1 us -> none  [swap(): return lax.all_to_all(value, axes, 0, 0, tiled=True)]
    all_gather x1 -> x0, waiting for transfers between devices: 27.3 us -> none  [shards(): ring_y = lax.all_gather(out_y, 'x', axis=0, tiled=True)]
    reduce_scatter x1, waiting for transfers between devices: 17.3 us -> 0.01 us  [shards(): lax.psum_scatter(partial, 'z', scatter_dimension=0, tiled=True).astype(f32)]
    dynamic_update_slice x8 -> x0, local copies, waits for them, and re-layouts: 13 us -> none  [the longest x4 7.55 us: shards(): lax.dynamic_update_slice(ring_grad, swap_core(piece)[None], (came, (1 - c...]
    pallas_call x0 -> x5, Pallas kernels: none -> 12 us  [the longest x4 6.26 us: ring_grad_part(): pl.pallas_call(ring_grad_kernel, out_shape=jax.ShapeDtypeStruct((2 * half...]
    unnamed x42 -> x69, local copies, waits for them, and re-layouts: 2.99 us -> 12.8 us
    ppermute x3 -> x9, starting transfers between devices: 6.54 us -> 16.1 us  [ring_shift(): lax.ppermute(value, 'x', [(i, (i + step) % 4) for i in range(4)])]
    dot_general x7 -> x5, matrix products: 15.4 us -> 7.68 us  [mm(): return lax.dot_general(a, b, (dims, ((), ())), preferred_element_type=f32)]
  transfers between devices with their start and end apart: 18 -> 23, of which waited for: 8 -> 11; matrix products, arithmetic and copies ran while one was open for 21% -> 26% of each run, Pallas kernels for 0% -> 6%
where the time goes in v3:
time: 216 us; the launch traced here: 214 us
  starting transfers between devices  57.4 us (27%)
  waiting for transfers between devices  52.9 us (24%)
  local copies, waits for them, and re-layouts  31.6 us (15%)
  matrix products  30.2 us (14%)
  other arithmetic  15.7 us (7%)
  between operations  14.5 us (7%)
  Pallas kernels  12 us (6%)
    all_to_all x6, starting transfers between devices, swap(): return lax.all_to_all(value, axes, 0, 0, tiled=True)  40 us
    all_to_all x6, waiting for transfers between devices, swap(): return lax.all_to_all(value, axes, 0, 0, tiled=True)  32.1 us
    ppermute x9, waiting for transfers between devices, ring_shift(): lax.ppermute(value, 'x', [(i, (i + step) % 4) for i in range(4)])  19.1 us
    ppermute x9, starting transfers between devices, ring_shift(): lax.ppermute(value, 'x', [(i, (i + step) % 4) for i in range(4)])  16.1 us
    dot_general x6, matrix products, exact(): lax.dot_general(a.astype(f32), b.astype(f32), (dims, ((), ())), precision...  14.4 us
    unnamed x69, local copies, waits for them, and re-layouts  12.8 us
    dot_general x5, matrix products, mm(): return lax.dot_general(a, b, (dims, ((), ())), preferred_element_type=f32)  7.68 us
    pallas_call x4, Pallas kernels, ring_grad_part(): pl.pallas_call(ring_grad_kernel, out_shape=jax.ShapeDtypeStruct((2 * half...  6.26 us
  transfers between devices with their start and end apart: 23, of which 11 were waited for; matrix products, arithmetic and copies ran while one was open for 26% of the time, Pallas kernels for 6%

profile of v3, /device:TPU:8, one launch (start us, length us, event | category | flops | bytes accessed | tf_op | source)
XLA Modules:
  0.0 214.4 jit_solution(2233519862784070875)
XLA Ops:
  7.2 2.2 %reduce-window.14 = f32[8,4,128]{2,0,1:T(8,128)S(1)} reduce-window(f32[8,4,128]{2,0,1:T(8,128)} %bitcast.109, f32[]{:T(128)} %constant.55.clone.1), window={size=1x1x128 pad=0_0x0_0x127_0}, to_apply=%region_0.0 | reduce-window | flops 520192 | bytes 32772 | tf_op jit(solution)/shard_map/reduce-window
  11.8 2.4 %fusion.13 = f32[512,128]{1,0:T(8,128)S(1)} fusion(bf16[512,128]{1,0:T(8,128)(2,1)} %param.10, f32[512,512]{1,0:T(8,128)S(1)} %copy.100, bf16[512,512]{1,0:T(8,128)(2,1)} %param.9), kind=kOutput, calls=%fused_computation.33 | convolution fusion | flops 403177472 | bytes 1966080 | tf_op jit(solution)/shard_map/dot_general | solution.py:39
  15.0 11.3 %all-to-all-start = ((f32[32,24,128]{2,1,0:T(8,128)}), f32[32,24,128]{2,1,0:T(8,128)S(1)}, u32[]{:S(2)}, u32[]{:S(2)}) async-start(f32[32,24,128]{2,1,0:T(8,128)} %pad_maximum_fusion), calls=%async_computation | async-start | bytes 786432 | tf_op jit(solution)/shard_map/all_to_all | solution.py:49
  26.4 2.7 %fusion.46 = (bf16[256,1024]{1,0:T(8,128)(2,1)}, bf16[256,1024]{1,0:T(8,128)(2,1)}, bf16[256,1024]{1,0:T(8,128)(2,1)S(1)}, bf16[256,1024]{1,0:T(8,128)(2,1)}) fusion(bf16[512,4096]{1,0:T(8,128)(2,1)} %param.14, s32[]{:T(128)S(6)} %select_n.48, s32[]{:T(128)S(6)} %select_n.52, s32[]{:T(128)S(6)} %select_n.50, s32[]{:T(128)S(6)} %select_n.49, s32[]{:T(128)S(6)} %select_n.51), kind=kLoop, calls=%fused_computation.93 | loop fusion | bytes 4194324 | tf_op jit(solution)/shard_map/dynamic_slice | solution.py:162
  29.1 1.8 collective-permute-start
  30.9 2.7 %collective-permute-start.1 = (bf16[256,1024]{1,0:T(8,128)(2,1)}, bf16[256,1024]{1,0:T(8,128)(2,1)S(1)}, u32[]{:S(2)}, u32[]{:S(2)}) collective-permute-start(bf16[256,1024]{1,0:T(8,128)(2,1)} %get-tuple-element.37), channel_id=1, source_target_pairs={{0,128},{64,192},{128,0},{192,64},{1,129},{65,193},{129,1},{193,65... | collective-permute-start | bytes 1572872 | tf_op jit(solution)/shard_map/ppermute | solution.py:57
  33.7 1.4 collective-permute-start.2
  35.8 1.3 fusion.47
  37.1 1.0 copy.103
  38.1 2.8 %all-to-all-done = f32[32,24,128]{2,1,0:T(8,128)S(1)} async-done(((f32[32,24,128]{2,1,0:T(8,128)}), f32[32,24,128]{2,1,0:T(8,128)S(1)}, u32[]{:S(2)}, u32[]{:S(2)}) %all-to-all-start) | async-done | bytes 393248 | tf_op jit(solution)/shard_map/all_to_all | solution.py:49
  42.7 5.2 %all-to-all-start.1 = ((f32[32,16,128]{2,1,0:T(8,128)}), f32[32,16,128]{2,1,0:T(8,128)S(1)}, u32[]{:S(2)}, u32[]{:S(2)}) async-start(f32[32,16,128]{2,1,0:T(8,128)} %copy.102), calls=%async_computation.1 | async-start | bytes 524288 | tf_op jit(solution)/shard_map/all_to_all | solution.py:49
  48.0 2.9 %fusion.1 = f32[8,512,64]{1,2,0:T(8,128)S(1)} fusion(bf16[512,8,64]{0,2,1:T(8,128)(2,1)} %bitcast.103, f32[512,512]{1,0:T(8,128)} %fusion.47, f32[8,512]{1,0:T(8,128)} %copy-done.29), kind=kOutput, calls=%fused_computation.5 | convolution fusion | flops 278921216 | bytes 2637824 | tf_op jit(solution)/shard_map/hts,shp->thp/dot_general | solution.py:191
  50.9 1.3 copy.106
  53.1 1.3 copy.105
  55.8 5.9 %collective-permute-done.1.own_ref.refs_2_ = bf16[256,1024]{1,0:T(8,128)(2,1)S(1)} collective-permute-done((bf16[256,1024]{1,0:T(8,128)(2,1)}, bf16[256,1024]{1,0:T(8,128)(2,1)S(1)}, u32[]{:S(2)}, u32[]{:S(2)}) %collective-permute-start.1) | collective-permute-done | bytes 524320 | tf_op jit(solution)/shard_map/ppermute | solution.py:57
  62.9 3.6 %fusion.7 = (bf16[512,512]{1,0:T(8,128)(2,1)}, f32[512,512]{1,0:T(8,128)}) fusion(bf16[512,512]{1,0:T(8,128)(2,1)} %param.9, f32[512]{0:T(512)} %mul.132, f32[512,512]{1,0:T(8,128)} %copy.106, f32[512,512]{1,0:T(8,128)} %copy.105, f32[512,128]{1,0:T(8,128)S(1)} %bitcast.94, bf16[512,128]{1,0:T(8,128)(2,1)S(1)} %copy-done), kind=kOutput, calls=%fused_computation.22 | convolution fusion | flops 404226048 | bytes 4589568 | tf_op jit(solution)/shard_map/dot_general | solution.py:39
  66.6 1.7 collective-permute-start.12
  69.1 1.8 collective-permute-start.13
  71.6 1.4 collective-permute-start.14
  73.0 1.7 all-gather.2.cloned.1.call-done.weight_ref
  74.8 1.2 copy-done.1
  76.0 1.0 copy-done.12
  77.0 1.7 ring_grad.6
  78.7 1.0 copy-done.9
  79.8 1.8 ring_grad.5
  81.5 1.8 collective-permute-start.8
  83.4 1.7 ring_grad.4
  85.9 1.4 collective-permute-start.6
  87.3 2.1 collective-permute-start.4
  90.8 3.6 %collective-permute-done.13.refs_10_ = bf16[512,512]{1,0:T(8,128)(2,1)} collective-permute-done((bf16[512,512]{1,0:T(8,128)(2,1)}, bf16[512,512]{1,0:T(8,128)(2,1)}, u32[]{:S(2)}, u32[]{:S(2)}) %collective-permute-start.13) | collective-permute-done | bytes 524320 | tf_op jit(solution)/shard_map/ppermute | solution.py:57
  94.4 1.5 collective-permute-done.14.refs_11_
  95.9 1.0 copy-done.4
  96.9 1.0 copy-done.7
  98.0 1.0 copy-done.10
  99.0 1.0 copy-done.13
  100.0 5.7 %weight_grad.1 = bf16[1024,512]{1,0:T(8,128)(2,1)} custom-call(s32[1]{0:T(128)} %bitcast.core_ref, bf16[256,1024]{1,0:T(8,128)(2,1)S(1)} %get-tuple-element.19.own_ref.refs_0_, bf16[256,1024]{1,0:T(8,128)(2,1)S(1)} %collective-permute-done.own_ref.refs_1_, bf16[256,1024]{1,0:T(8,128)(2,1)S(1)} %collective-permute-done.1.own_ref.refs_2_, ...), custom_call_target="tpu_custom_call" | custom-call | flops 2147483648 | bytes 8388608 | tf_op jit(solution)/shard_map/weight_grad/pallas_call | solution.py:116
  105.8 1.0 copy-done.5
  106.8 1.0 ring_grad.7
  107.9 8.0 %collective-permute-done.4 = bf16[512,512]{1,0:T(8,128)(2,1)} collective-permute-done((bf16[512,512]{1,0:T(8,128)(2,1)}, bf16[512,512]{1,0:T(8,128)(2,1)}, u32[]{:S(2)}, u32[]{:S(2)}) %collective-permute-start.4) | collective-permute-done | bytes 524320 | tf_op jit(solution)/shard_map/ppermute | solution.py:57
  115.9 1.9 fusion.11
  117.9 2.9 %fusion.15 = f32[512,128]{1,0:T(8,128)} fusion(bf16[512,128]{1,0:T(8,128)(2,1)S(1)} %copy-done, f32[512,512]{1,0:T(8,128)} %copy.105, bf16[512,512]{1,0:T(8,128)(2,1)S(1)} %get-tuple-element.31), kind=kOutput, calls=%fused_computation.35 | convolution fusion | flops 403177472 | bytes 1966080 | tf_op jit(solution)/shard_map/dot_general | solution.py:39
  121.7 9.5 %all-to-all-start.2 = ((f32[32,16,128]{2,1,0:T(8,128)}), f32[32,16,128]{2,1,0:T(8,128)}, u32[]{:S(2)}, u32[]{:S(2)}) async-start(f32[32,16,128]{2,1,0:T(8,128)} %bitcast.19), calls=%async_computation.2 | async-start | bytes 524288 | tf_op jit(solution)/shard_map/all_to_all | solution.py:49
  131.2 2.1 fusion
  133.3 1.3 copy.114
  134.7 3.1 %multiply_reduce_fusion = bf16[512,512]{1,0:T(8,128)(2,1)S(1)} fusion(f32[8,512]{1,0:T(8,128)} %copy-done.29, bf16[512,8,64]{0,2,1:T(8,128)(2,1)} %bitcast.106, bf16[512,8,64]{0,2,1:T(8,128)(2,1)} %bitcast.104), kind=kOutput, calls=%fused_computation | convolution fusion | flops 278659072 | bytes 1589248 | tf_op jit(solution)/shard_map/thp,shp->hts/dot_general | solution.py:220
  138.6 1.0 fusion.48
  139.6 5.3 %all-to-all-done.2 = f32[32,16,128]{2,1,0:T(8,128)} async-done(((f32[32,16,128]{2,1,0:T(8,128)}), f32[32,16,128]{2,1,0:T(8,128)}, u32[]{:S(2)}, u32[]{:S(2)}) %all-to-all-start.2) | async-done | bytes 262176 | tf_op jit(solution)/shard_map/all_to_all | solution.py:49
  144.9 1.4 fusion.25
  147.2 5.0 %all-to-all-start.3 = ((f32[32,16,128]{2,1,0:T(8,128)}), f32[32,16,128]{2,1,0:T(8,128)}, u32[]{:S(2)}, u32[]{:S(2)}) async-start(f32[32,16,128]{2,1,0:T(8,128)} %copy.111), calls=%async_computation.3 | async-start | bytes 524288 | tf_op jit(solution)/shard_map/all_to_all | solution.py:49
  152.2 2.1 fusion.49
  154.3 2.0 convolution_add_fusion
  156.3 7.2 %all-to-all-done.3 = f32[32,16,128]{2,1,0:T(8,128)} async-done(((f32[32,16,128]{2,1,0:T(8,128)}), f32[32,16,128]{2,1,0:T(8,128)}, u32[]{:S(2)}, u32[]{:S(2)}) %all-to-all-start.3) | async-done | bytes 262176 | tf_op jit(solution)/shard_map/all_to_all | solution.py:49
  163.5 1.5 multiply_reduce_fusion.1
  165.2 3.7 %fusion.8 = (f32[512,512]{1,0:T(8,128)}, bf16[512,512]{1,0:T(8,128)(2,1)}) fusion(bf16[512,512]{1,0:T(8,128)(2,1)S(1)} %copy-done.15, f32[512,512]{1,0:T(8,128)} %get-tuple-element.43, bf16[512,512]{1,0:T(8,128)(2,1)S(1)} %get-tuple-element.31, f32[512]{0:T(512)S(1)} %copy-done.30, f32[512,512]{1,0:T(8,128)} %copy.114, f32[512,512]{1,0:T(8,128)S(1)} %copy-done.17, ...), kind=kOutput, calls=%fused_computation.23 | convolution fusion | flops 405274624 | bytes 6162432 | tf_op jit(solution)/shard_map/dot_general | solution.py:39
  169.0 1.6 copy.115
  170.6 1.4 convolution_add_fusion.1
  172.7 1.1 reduce-window.16
  174.2 0.9 broadcast_in_dim.73
  175.0 4.6 %all-to-all-start.4 = ((bf16[4,512,128]{2,1,0:T(8,128)(2,1)}), bf16[4,512,128]{2,1,0:T(8,128)(2,1)S(1)}, u32[]{:S(2)}, u32[]{:S(2)}) async-start(bf16[4,512,128]{2,1,0:T(8,128)(2,1)} %broadcast_in_dim.73), calls=%async_computation.4 | async-start | bytes 1048576 | tf_op jit(solution)/shard_map/all_to_all | solution.py:49
  180.0 1.0 fusion.19
  181.3 7.1 %all-to-all-done.4 = bf16[4,512,128]{2,1,0:T(8,128)(2,1)S(1)} async-done(((bf16[4,512,128]{2,1,0:T(8,128)(2,1)}), bf16[4,512,128]{2,1,0:T(8,128)(2,1)S(1)}, u32[]{:S(2)}, u32[]{:S(2)}) %all-to-all-start.4) | async-done | bytes 524320 | tf_op jit(solution)/shard_map/all_to_all | solution.py:49
  189.0 4.3 %all-to-all-start.5 = ((f32[32,8,128]{2,1,0:T(8,128)}), f32[32,8,128]{2,1,0:T(8,128)S(1)}, u32[]{:S(2)}, u32[]{:S(2)}) async-start(f32[32,8,128]{2,1,0:T(8,128)} %broadcast_in_dim_broadcast_in_dim_broadcast_in_dim.2), calls=%async_computation.6 | async-start | bytes 262144 | tf_op jit(solution)/shard_map/all_to_all | solution.py:49
  194.2 9.5 %all-to-all-done.5 = f32[32,8,128]{2,1,0:T(8,128)S(1)} async-done(((f32[32,8,128]{2,1,0:T(8,128)}), f32[32,8,128]{2,1,0:T(8,128)S(1)}, u32[]{:S(2)}, u32[]{:S(2)}) %all-to-all-start.5) | async-done | bytes 131104 | tf_op jit(solution)/shard_map/all_to_all | solution.py:49
  205.0 1.8 multiply_subtract_fusion
  (134 shorter events, 21.1 us)
Async XLA Ops:
  7.2 28.6 %copy-start = (bf16[512,128]{1,0:T(8,128)(2,1)S(1)}, bf16[512,128]{1,0:T(8,128)(2,1)}, u32[]{:S(2)}) copy-start(bf16[512,128]{1,0:T(8,128)(2,1)} %param.11) | copy-start | bytes 393220
  10.3 0.7 copy-start.29
  11.6 14.8 %copy-start.16 = (f32[512,512]{1,0:T(8,128)}, f32[512,512]{1,0:T(8,128)S(1)}, u32[]{:S(2)}) copy-start(f32[512,512]{1,0:T(8,128)S(1)} %copy.100) | copy-start | bytes 3145732
  11.6 23.5 %copy-start.25 = (f32[128,512]{1,0:T(8,128)S(1)}, f32[128,512]{1,0:T(8,128)}, u32[]{:S(2)}) copy-start(f32[128,512]{1,0:T(8,128)} %param.15) | copy-start | bytes 786436
  11.7 24.0 %copy-start.22 = (bf16[512,128]{1,0:T(8,128)(2,1)S(1)}, bf16[512,128]{1,0:T(8,128)(2,1)}, u32[]{:S(2)}) copy-start(bf16[512,128]{1,0:T(8,128)(2,1)} %param.10) | copy-start | bytes 393220
  14.1 16.8 %copy-start.19 = (f32[512,128]{1,0:T(8,128)}, f32[512,128]{1,0:T(8,128)S(1)}, u32[]{:S(2)}) copy-start(f32[512,128]{1,0:T(8,128)S(1)} %fusion.13) | copy-start | bytes 786436
  14.1 23.0 %copy-start.14 = (bf16[512,512]{1,0:T(8,128)(2,1)S(1)}, bf16[512,512]{1,0:T(8,128)(2,1)}, u32[]{:S(2)}) copy-start(bf16[512,512]{1,0:T(8,128)(2,1)} %param.9) | copy-start | bytes 1572868
  15.0 25.9 %all-to-all-start = ((f32[32,24,128]{2,1,0:T(8,128)}), f32[32,24,128]{2,1,0:T(8,128)S(1)}, u32[]{:S(2)}, u32[]{:S(2)}) async-start(f32[32,24,128]{2,1,0:T(8,128)} %pad_maximum_fusion), calls=%async_computation | async-start | bytes 786432 | tf_op jit(solution)/shard_map/all_to_all | solution.py:49
  26.3 48.4 %all-gather.2.cloned.1.call-start = ((), (), s32[]{:S(2)}) async-start(), calls=%async_computation.7 | async-start | bytes 1179648 | tf_op jit(solution)/shard_map/all_gather | solution.py:158
  29.1 26.7 %collective-permute-start = (bf16[256,1024]{1,0:T(8,128)(2,1)}, bf16[256,1024]{1,0:T(8,128)(2,1)S(1)}, u32[]{:S(2)}, u32[]{:S(2)}) collective-permute-start(bf16[256,1024]{1,0:T(8,128)(2,1)} %get-tuple-element.35), channel_id=1, source_target_pairs={{0,64},{64,128},{128,192},{192,0},{1,65},{65,129},{129,193},{193,1... | collective-permute-start | bytes 1572872 | tf_op jit(solution)/shard_map/ppermute | solution.py:57
  30.9 30.8 %collective-permute-start.1 = (bf16[256,1024]{1,0:T(8,128)(2,1)}, bf16[256,1024]{1,0:T(8,128)(2,1)S(1)}, u32[]{:S(2)}, u32[]{:S(2)}) collective-permute-start(bf16[256,1024]{1,0:T(8,128)(2,1)} %get-tuple-element.37), channel_id=1, source_target_pairs={{0,128},{64,192},{128,0},{192,64},{1,129},{65,193},{129,1},{193,65... | collective-permute-start | bytes 1572872 | tf_op jit(solution)/shard_map/ppermute | solution.py:57
  33.7 28.1 %collective-permute-start.2 = (bf16[256,1024]{1,0:T(8,128)(2,1)}, bf16[256,1024]{1,0:T(8,128)(2,1)S(1)}, u32[]{:S(2)}, u32[]{:S(2)}) collective-permute-start(bf16[256,1024]{1,0:T(8,128)(2,1)} %get-tuple-element.34), channel_id=1, source_target_pairs={{0,192},{64,0},{128,64},{192,128},{1,193},{65,1},{129,65},{193,129... | collective-permute-start | bytes 1572872 | tf_op jit(solution)/shard_map/ppermute | solution.py:57
  42.7 19.2 %all-to-all-start.1 = ((f32[32,16,128]{2,1,0:T(8,128)}), f32[32,16,128]{2,1,0:T(8,128)S(1)}, u32[]{:S(2)}, u32[]{:S(2)}) async-start(f32[32,16,128]{2,1,0:T(8,128)} %copy.102), calls=%async_computation.1 | async-start | bytes 524288 | tf_op jit(solution)/shard_map/all_to_all | solution.py:49
  47.9 132.1 %reduce-scatter.2.cloned.1.call-start = ((), (), s32[]{:S(2)}) async-start(), calls=%async_computation.8 | async-start | bytes 1179648 | tf_op jit(solution)/shard_map/reduce_scatter | solution.py:208
  61.9 19.6 %collective-permute-start.3 = (bf16[256,1024]{1,0:T(8,128)(2,1)S(1)}, bf16[256,1024]{1,0:T(8,128)(2,1)S(1)}, u32[]{:S(2)}, u32[]{:S(2)}) collective-permute-start(bf16[256,1024]{1,0:T(8,128)(2,1)S(1)} %collective-permute-done.1.own_ref.refs_2_), channel_id=1, source_target_pairs={{0,1},{1,0},{2,3},{3,2},{4,5},{5,4},{6,7},{7,6},{8,9},{9,8},{10,11... | collective-permute-start | bytes 1572872 | tf_op jit(solution)/shard_map/ppermute | solution.py:53
  61.9 6.3 %collective-permute-start.5 = (bf16[256,1024]{1,0:T(8,128)(2,1)S(1)}, bf16[256,1024]{1,0:T(8,128)(2,1)S(1)}, u32[]{:S(2)}, u32[]{:S(2)}) collective-permute-start(bf16[256,1024]{1,0:T(8,128)(2,1)S(1)} %collective-permute-done.own_ref.refs_1_), channel_id=1, source_target_pairs={{0,1},{1,0},{2,3},{3,2},{4,5},{5,4},{6,7},{7,6},{8,9},{9,8},{10,11... | collective-permute-start | bytes 1572872 | tf_op jit(solution)/shard_map/ppermute | solution.py:53
  62.4 8.4 %collective-permute-start.7 = (bf16[256,1024]{1,0:T(8,128)(2,1)S(1)}, bf16[256,1024]{1,0:T(8,128)(2,1)S(1)}, u32[]{:S(2)}, u32[]{:S(2)}) collective-permute-start(bf16[256,1024]{1,0:T(8,128)(2,1)S(1)} %collective-permute-done.2.own_ref.refs_3_), channel_id=1, source_target_pairs={{0,1},{1,0},{2,3},{3,2},{4,5},{5,4},{6,7},{7,6},{8,9},{9,8},{10,11... | collective-permute-start | bytes 1572872 | tf_op jit(solution)/shard_map/ppermute | solution.py:53
  62.4 22.7 %collective-permute-start.9 = (bf16[256,1024]{1,0:T(8,128)(2,1)S(1)}, bf16[256,1024]{1,0:T(8,128)(2,1)S(1)}, u32[]{:S(2)}, u32[]{:S(2)}) collective-permute-start(bf16[256,1024]{1,0:T(8,128)(2,1)S(1)} %get-tuple-element.19.own_ref.refs_0_), channel_id=1, source_target_pairs={{0,1},{1,0},{2,3},{3,2},{4,5},{5,4},{6,7},{7,6},{8,9},{9,8},{10,11... | collective-permute-start | bytes 1572872 | tf_op jit(solution)/shard_map/ppermute | solution.py:53
  66.6 20.8 %collective-permute-start.12 = (bf16[512,512]{1,0:T(8,128)(2,1)}, bf16[512,512]{1,0:T(8,128)(2,1)}, u32[]{:S(2)}, u32[]{:S(2)}) collective-permute-start(bf16[512,512]{1,0:T(8,128)(2,1)} %get-tuple-element.42.refs_8_), channel_id=1, source_target_pairs={{0,64},{64,128},{128,192},{192,0},{1,65},{65,129},{129,193},{193,1... | collective-permute-start | bytes 1572872 | tf_op jit(solution)/shard_map/ppermute | solution.py:57
  68.3 0.8 copy-start.8
  69.1 25.4 %collective-permute-start.13 = (bf16[512,512]{1,0:T(8,128)(2,1)}, bf16[512,512]{1,0:T(8,128)(2,1)}, u32[]{:S(2)}, u32[]{:S(2)}) collective-permute-start(bf16[512,512]{1,0:T(8,128)(2,1)} %get-tuple-element.42.refs_8_), channel_id=1, source_target_pairs={{0,128},{64,192},{128,0},{192,64},{1,129},{65,193},{129,1},{193,65... | collective-permute-start | bytes 1572872 | tf_op jit(solution)/shard_map/ppermute | solution.py:57
  70.9 0.8 copy-start.11
  71.6 24.2 %collective-permute-start.14 = (bf16[512,512]{1,0:T(8,128)(2,1)}, bf16[512,512]{1,0:T(8,128)(2,1)}, u32[]{:S(2)}, u32[]{:S(2)}) collective-permute-start(bf16[512,512]{1,0:T(8,128)(2,1)} %get-tuple-element.42.refs_8_), channel_id=1, source_target_pairs={{0,192},{64,0},{128,64},{192,128},{1,193},{65,1},{129,65},{193,129... | collective-permute-start | bytes 1572872 | tf_op jit(solution)/shard_map/ppermute | solution.py:57
  74.7 1.2 copy-start.1
  76.0 1.0 copy-start.12
  78.7 1.0 copy-start.9
  81.5 9.2 %copy-start.6 = (bf16[256,1024]{1,0:T(8,128)(2,1)}, bf16[256,1024]{1,0:T(8,128)(2,1)S(1)}, u32[]{:S(2)}) copy-start(bf16[256,1024]{1,0:T(8,128)(2,1)S(1)} %collective-permute-done.3.other_ref.refs_6_) | copy-start | bytes 1572868
  81.5 26.4 %collective-permute-start.8 = (bf16[512,512]{1,0:T(8,128)(2,1)}, bf16[512,512]{1,0:T(8,128)(2,1)}, u32[]{:S(2)}, u32[]{:S(2)}) collective-permute-start(bf16[512,512]{1,0:T(8,128)(2,1)} %ring_grad.6), channel_id=1, source_target_pairs={{0,64},{64,128},{128,192},{192,0},{1,65},{65,129},{129,193},{193,1... | collective-permute-start | bytes 1572872 | tf_op jit(solution)/shard_map/ppermute | solution.py:57
  85.1 0.8 copy-start.3
  85.9 22.0 %collective-permute-start.6 = (bf16[512,512]{1,0:T(8,128)(2,1)}, bf16[512,512]{1,0:T(8,128)(2,1)}, u32[]{:S(2)}, u32[]{:S(2)}) collective-permute-start(bf16[512,512]{1,0:T(8,128)(2,1)} %ring_grad.5), channel_id=1, source_target_pairs={{0,192},{64,0},{128,64},{192,128},{1,193},{65,1},{129,65},{193,129... | collective-permute-start | bytes 1572872 | tf_op jit(solution)/shard_map/ppermute | solution.py:57
  87.3 28.6 %collective-permute-start.4 = (bf16[512,512]{1,0:T(8,128)(2,1)}, bf16[512,512]{1,0:T(8,128)(2,1)}, u32[]{:S(2)}, u32[]{:S(2)}) collective-permute-start(bf16[512,512]{1,0:T(8,128)(2,1)} %ring_grad.4), channel_id=1, source_target_pairs={{0,128},{64,192},{128,0},{192,64},{1,129},{65,193},{129,1},{193,65... | collective-permute-start | bytes 1572872 | tf_op jit(solution)/shard_map/ppermute | solution.py:57
  90.8 15.0 %copy-start.2 = (bf16[1024,512]{1,0:T(8,128)(2,1)S(1)}, bf16[1024,512]{1,0:T(8,128)(2,1)}, u32[]{:S(2)}) copy-start(bf16[1024,512]{1,0:T(8,128)(2,1)} %all-gather.2.cloned.1.call-done.weight_ref) | copy-start | bytes 3145732
  95.9 1.0 copy-start.4
  96.9 1.0 copy-start.7
  98.0 1.0 copy-start.10
  99.0 1.0 copy-start.13
  105.8 1.0 copy-start.5
  107.9 23.3 %copy-start.24 = (f32[512,512]{1,0:T(8,128)S(1)}, f32[512,512]{1,0:T(8,128)}, u32[]{:S(2)}) copy-start(f32[512,512]{1,0:T(8,128)} %fusion.47) | copy-start | bytes 3145732
  121.0 12.3 %copy-start.27 = (bf16[512,512]{0,1:T(8,128)(2,1)}, bf16[512,512]{0,1:T(8,128)(2,1)S(1)}, u32[]{:S(2)}) copy-start(bf16[512,512]{0,1:T(8,128)(2,1)S(1)} %copy.107) | copy-start | bytes 1572868
  121.7 23.2 %all-to-all-start.2 = ((f32[32,16,128]{2,1,0:T(8,128)}), f32[32,16,128]{2,1,0:T(8,128)}, u32[]{:S(2)}, u32[]{:S(2)}) async-start(f32[32,16,128]{2,1,0:T(8,128)} %bitcast.19), calls=%async_computation.2 | async-start | bytes 524288 | tf_op jit(solution)/shard_map/all_to_all | solution.py:49
  134.7 4.0 %copy-start.23 = (bf16[512,128]{1,0:T(8,128)(2,1)S(1)}, bf16[512,128]{1,0:T(8,128)(2,1)}, u32[]{:S(2)}) copy-start(bf16[512,128]{1,0:T(8,128)(2,1)} %param.10) | copy-start | bytes 393220
  134.7 19.7 %copy-start.18 = (f32[512,512]{1,0:T(8,128)S(1)}, f32[512,512]{1,0:T(8,128)}, u32[]{:S(2)}) copy-start(f32[512,512]{1,0:T(8,128)} %copy.105) | copy-start | bytes 3145732
  137.8 0.8 copy-start.21
  138.6 26.6 %copy-start.15 = (bf16[512,512]{1,0:T(8,128)(2,1)S(1)}, bf16[512,512]{1,0:T(8,128)(2,1)}, u32[]{:S(2)}) copy-start(bf16[512,512]{1,0:T(8,128)(2,1)} %param.9) | copy-start | bytes 1572868
  138.6 26.6 %copy-start.17 = (f32[512,512]{1,0:T(8,128)S(1)}, f32[512,512]{1,0:T(8,128)}, u32[]{:S(2)}) copy-start(f32[512,512]{1,0:T(8,128)} %copy-done.16) | copy-start | bytes 3145732
  146.3 17.2 %copy-start.31 = (f32[32]{0:T(128)S(1)}, f32[32]{0:T(128)}, u32[]{:S(2)}) copy-start(f32[32]{0:T(128)} %mul.145) | copy-start | bytes 388
  146.3 18.9 %copy-start.30 = (f32[512]{0:T(512)S(1)}, f32[512]{0:T(512)}, u32[]{:S(2)}) copy-start(f32[512]{0:T(512)} %mul.132) | copy-start | bytes 6148
  147.2 16.3 %all-to-all-start.3 = ((f32[32,16,128]{2,1,0:T(8,128)}), f32[32,16,128]{2,1,0:T(8,128)}, u32[]{:S(2)}, u32[]{:S(2)}) async-start(f32[32,16,128]{2,1,0:T(8,128)} %copy.111), calls=%async_computation.3 | async-start | bytes 524288 | tf_op jit(solution)/shard_map/all_to_all | solution.py:49
  165.2 6.7 %copy-start.20 = (f32[512,128]{1,0:T(8,128)S(1)}, f32[512,128]{1,0:T(8,128)}, u32[]{:S(2)}) copy-start(f32[512,128]{1,0:T(8,128)} %convolution_add_fusion) | copy-start | bytes 786436
  169.0 12.2 %copy-start.32 = (f32[8]{0:T(128)S(1)}, f32[8]{0:T(128)}, u32[]{:S(2)}) copy-start(f32[8]{0:T(128)} %reduce_sum.102) | copy-start | bytes 100
  170.6 33.2 %copy-start.33 = (f32[8]{0:T(128)S(1)}, f32[8]{0:T(128)}, u32[]{:S(2)}) copy-start(f32[8]{0:T(128)} %param.17) | copy-start | bytes 100
  170.6 34.4 %copy-start.26 = (f32[128,512]{1,0:T(8,128)S(1)}, f32[128,512]{1,0:T(8,128)}, u32[]{:S(2)}) copy-start(f32[128,512]{1,0:T(8,128)} %param.15) | copy-start | bytes 786436
  172.0 33.0 %copy-start.28 = (f32[128,512]{1,0:T(8,128)S(1)}, f32[128,512]{1,0:T(8,128)}, u32[]{:S(2)}) copy-start(f32[128,512]{1,0:T(8,128)} %param.16) | copy-start | bytes 786436
  172.1 1.9 collective-permute-start.10
  175.0 13.3 %all-to-all-start.4 = ((bf16[4,512,128]{2,1,0:T(8,128)(2,1)}), bf16[4,512,128]{2,1,0:T(8,128)(2,1)S(1)}, u32[]{:S(2)}, u32[]{:S(2)}) async-start(bf16[4,512,128]{2,1,0:T(8,128)(2,1)} %broadcast_in_dim.73), calls=%async_computation.4 | async-start | bytes 1048576 | tf_op jit(solution)/shard_map/all_to_all | solution.py:49
  189.0 14.7 %all-to-all-start.5 = ((f32[32,8,128]{2,1,0:T(8,128)}), f32[32,8,128]{2,1,0:T(8,128)S(1)}, u32[]{:S(2)}, u32[]{:S(2)}) async-start(f32[32,8,128]{2,1,0:T(8,128)} %broadcast_in_dim_broadcast_in_dim_broadcast_in_dim.2), calls=%async_computation.6 | async-start | bytes 262144 | tf_op jit(solution)/shard_map/all_to_all | solution.py:49
  194.1 12.7 %collective-permute-start.11 = (f32[512,128]{1,0:T(8,128)S(1)}, f32[512,128]{1,0:T(8,128)S(1)}, u32[]{:S(2)}, u32[]{:S(2)}) collective-permute-start(f32[512,128]{1,0:T(8,128)S(1)} %convert_reduce_fusion), channel_id=1, source_target_pairs={{0,1},{1,0},{2,3},{3,2},{4,5},{5,4},{6,7},{7,6},{8,9},{9,8},{10,11... | collective-permute-start | bytes 786440 | tf_op jit(solution)/shard_map/ppermute | solution.py:53
Sparse Core Ops, SparseCore 0:
  35.9 38.8 all-gather.1
  105.9 39.6 reduce-scatter.1

commit v4 on v3

--- a/solution.py
+++ b/solution.py
@@ -61,10 +61,37 @@
     return swap(jnp.broadcast_to(value[None], (count,) + value.shape), axis)
 
 
-def ring_grad_kernel(core_ref, own_ref, other_ref, weight_ref, out_ref):
+TILE = 256
+ANYWHERE = pl.BlockSpec(memory_space=pl.ANY)
+IN_SMEM = pl.BlockSpec(memory_space=pltpu.SMEM)
+IN_VMEM = pl.BlockSpec(memory_space=pltpu.VMEM)
+
+
+def tile_of(j):
+    return pl.ds(pl.multiple_of(j * TILE, TILE), TILE)
+
+
+def fetch(refs, buffers, sems):
+    copies = [
+        pltpu.make_async_copy(ref, buffer, sems.at[i])
+        for i, (ref, buffer) in enumerate(zip(refs, buffers))
+    ]
+    for copy in copies:
+        copy.start()
+    return copies
+
+
+def like(arrays):
+    return [pltpu.VMEM(a.shape, a.dtype) for a in arrays] + [pltpu.SemaphoreType.DMA((len(arrays),))]
+
+
+def ring_grad_kernel(core_ref, own_in, other_in, weight_in, out_ref, own_ref, other_ref, weight_ref, sems):
+    copies = fetch((weight_in, own_in, other_in), (weight_ref, own_ref, other_ref), sems)
     half = own_ref.shape[0]
     core = core_ref[0]
-    for ref, at in ((own_ref, core), (other_ref, 1 - core)):
+    copies[0].wait()
+    for copy, ref, at in zip(copies[1:], (own_ref, other_ref), (core, 1 - core)):
+        copy.wait()
         out_ref[pl.ds(pl.multiple_of(at * half, half), half), :] = jnp.dot(
             ref[...], weight_ref[...], preferred_element_type=f32
         ).astype(bf16)
@@ -76,51 +103,49 @@
     return pl.pallas_call(
         ring_grad_kernel,
         out_shape=jax.ShapeDtypeStruct((2 * half, width), bf16),
-        grid=(2,),
-        in_specs=[
-            pl.BlockSpec(memory_space=pltpu.SMEM),
-            pl.BlockSpec((half, quarter), lambda j: (0, 0)),
-            pl.BlockSpec((half, quarter), lambda j: (0, 0)),
-            pl.BlockSpec((quarter, width // 2), lambda j: (0, j)),
-        ],
-        out_specs=pl.BlockSpec((2 * half, width // 2), lambda j: (0, j)),
+        in_specs=[IN_SMEM] + [ANYWHERE] * 3,
+        out_specs=IN_VMEM,
+        scratch_shapes=like((own, other, weight_rows)),
         cost_estimate=pl.CostEstimate(
             flops=4 * half * quarter * width, bytes_accessed=3 << 20, transcendentals=0
         ),
-        compiler_params=pltpu.CompilerParams(vmem_limit_bytes=24 << 20),
+        compiler_params=pltpu.CompilerParams(vmem_limit_bytes=16 << 20),
         name="ring_grad",
     )(core, own, other, weight_rows)
 
 
 def weight_grad_kernel(core_ref, *refs):
-    owns, others, ys, out_ref = refs[:4], refs[4:8], refs[8:12], refs[12]
+    out_ref, sems = refs[12], refs[25]
+    for copy in fetch(refs[:12], refs[13:25], sems):
+        copy.wait()
+    owns, others, ys = refs[13:17], refs[17:21], refs[21:25]
     half = owns[0].shape[0]
     core = core_ref[0]
-    total = None
-    for own, other, y in zip(owns, others, ys):
-        for ref, at in ((own, core), (other, 1 - core)):
-            part = lax.dot_general(
-                ref[...],
-                y[pl.ds(pl.multiple_of(at * half, half), half), :],
-                (((0,), (0,)), ((), ())),
-                preferred_element_type=f32,
-            )
-            total = part if total is None else total + part
-    out_ref[...] = total.astype(bf16)
+
+    @pl.loop(0, out_ref.shape[0] // TILE)
+    def _(j):
+        total = None
+        for own, other, y in zip(owns, others, ys):
+            for ref, at in ((own, core), (other, 1 - core)):
+                part = lax.dot_general(
+                    ref[:, tile_of(j)],
+                    y[pl.ds(pl.multiple_of(at * half, half), half), :],
+                    (((0,), (0,)), ((), ())),
+                    preferred_element_type=f32,
+                )
+                total = part if total is None else total + part
+        out_ref[tile_of(j), :] = total.astype(bf16)
 
 
 def weight_grad_part(core, owns, others, ys):
     half, quarter = owns[0].shape
     width = ys[0].shape[1]
-    tile = 256
     return pl.pallas_call(
         weight_grad_kernel,
         out_shape=jax.ShapeDtypeStruct((quarter, width), bf16),
-        grid=(quarter // tile,),
-        in_specs=[pl.BlockSpec(memory_space=pltpu.SMEM)]
-        + [pl.BlockSpec((half, tile), lambda j: (0, j))] * 8
-        + [pl.BlockSpec((2 * half, width), lambda j: (0, 0))] * 4,
-        out_specs=pl.BlockSpec((tile, width), lambda j: (j, 0)),
+        in_specs=[IN_SMEM] + [ANYWHERE] * 12,
+        out_specs=IN_VMEM,
+        scratch_shapes=like((*owns, *others, *ys)),
         cost_estimate=pl.CostEstimate(
             flops=16 * half * quarter * width, bytes_accessed=8 << 20, transcendentals=0
         ),
@@ -181,9 +206,12 @@
     packed = jnp.concatenate(
         [local_state.reshape(BLOCKS, 16, 128), totals.reshape(BLOCKS, 8, 128)], axis=1
     )
+    packed, owns[1] = lax.optimization_barrier((packed, owns[1]))
     packed = swap(packed, CTX)
     weights = block_weights(packed[:, 16, 0])
-    start = swap(chain(weights, packed[:, :16], False), CTX).reshape(width, 128)
+    start = chain(weights, packed[:, :16], False)
+    start, weight_rows, owns = lax.optimization_barrier((start, weight_rows, owns))
+    start = swap(start, CTX).reshape(width, 128)
 
     scores = mm(read_vector, write_vector, ((1,), (1,)))
     mixed = (lower_decay * scores[None]).astype(bf16)
@@ -192,7 +220,6 @@
     core_y = inner.reshape(tokens, width) + exact(read_vector, start, ((1,), (1,))) * from_start_wide
     out_y = (core_y + skip_wide * head_x).astype(bf16)
 
-    owns, _ = lax.optimization_barrier((owns, start))
     others = [swap_core(piece) for piece in owns]
     core_one = jnp.full((1,), core, jnp.int32)
     parts = [
@@ -225,7 +252,23 @@
     write_grad = mm(pair_weights, read_vector, ((0,), (0,))) + mm(
         x_decayed.astype(bf16), end.astype(bf16), ((1,), (0,))
     )
+    terms = (grad * core_y - head_x * core_grad).reshape(tokens, heads, head_width)
+    decay_part = jnp.sum(terms, axis=2).T
+    local_tail = jnp.flip(jnp.cumsum(jnp.flip(decay_part, 1), axis=1), 1)
+    end_state = start.reshape(heads, -1) * jnp.exp(last_sum) + local_state.reshape(
+        heads, -1
+    )
+    above = jnp.sum(end_state * end.reshape(heads, -1), axis=1)
+    decay_grad = local_tail + above[:, None]
+
+    skip_part = jnp.sum((grad * head_x).reshape(tokens, heads, head_width), axis=(0, 2))
+    square_part = jnp.sum((weight_grad * weight_grad).reshape(-1, heads, head_width), axis=(0, 2))
+    small = jnp.concatenate([skip_part, square_part, jnp.zeros((112,), f32)])
+    small = spread(jnp.broadcast_to(small[None], (8, 128)), CTX, BLOCKS)
+    small = jnp.sum(small, axis=0)[0]
+
     both = jnp.concatenate([write_grad, read_grad], axis=0)
+    both, small = lax.optimization_barrier((both, small))
     keep = lax.dynamic_slice_in_dim(both, core * tokens, tokens, axis=0)
     give = lax.dynamic_slice_in_dim(both, (1 - core) * tokens, tokens, axis=0)
     keep = keep + swap_core(give)
@@ -234,20 +277,6 @@
     write_sum = jnp.where(core == 0, keep, give)
     read_sum = jnp.where(core == 0, give, keep)
 
-    terms = (grad * core_y - head_x * core_grad).reshape(tokens, heads, head_width)
-    decay_part = jnp.sum(terms, axis=2).T
-    local_tail = jnp.flip(jnp.cumsum(jnp.flip(decay_part, 1), axis=1), 1)
-    end_state = start.reshape(heads, -1) * jnp.exp(last_sum) + local_state.reshape(
-        heads, -1
-    )
-    above = jnp.sum(end_state * end.reshape(heads, -1), axis=1)
-    decay_grad = local_tail + above[:, None]
-
-    skip_part = jnp.sum((grad * head_x).reshape(tokens, heads, head_width), axis=(0, 2))
-    square_part = jnp.sum((weight_grad * weight_grad).reshape(-1, heads, head_width), axis=(0, 2))
-    small = jnp.concatenate([skip_part, square_part, jnp.zeros((112,), f32)])
-    small = spread(jnp.broadcast_to(small[None], (8, 128)), CTX, BLOCKS)
-    small = jnp.sum(small, axis=0)[0]
     skip_total, square_total = small[:heads], small[heads : 2 * heads]
     mean_square = square_total / float(WIDTH * head_width)
     new_second = beta_two * squared_average + (1.0 - beta_two) * mean_square

time: 216 us -> 242 us (1.12)
  waiting for transfers between devices: 52.9 us -> 75.8 us
  Pallas kernels: 12 us -> 15.2 us
    ppermute x9, waiting for transfers between devices: 19.1 us -> 35.9 us  [ring_shift(): lax.ppermute(value, 'x', [(i, (i + step) % 4) for i in range(4)])]
    all_to_all x6, waiting for transfers between devices: 32.1 us -> 39.8 us  [swap(): return lax.all_to_all(value, axes, 0, 0, tiled=True)]
    unnamed x69 -> x63, local copies, waits for them, and re-layouts: 12.8 us -> 5.4 us
    dot_general x6, matrix products: 14.4 us -> 11.4 us  [exact(): lax.dot_general(a.astype(f32), b.astype(f32), (dims, ((), ())), precision...]
    pallas_call x4, Pallas kernels: 6.26 us -> 8.88 us  [ring_grad_part(): pl.pallas_call(ring_grad_kernel, out_shape=jax.ShapeDtypeStruct((2 * half...]
  transfers between devices with their start and end apart: 23 -> 23, of which waited for: 11 -> 14; matrix products, arithmetic and copies ran while one was open for 26% -> 26% of each run, Pallas kernels for 6% -> 6%
where the time goes in v4:
time: 242 us; the launch traced here: 239 us
  waiting for transfers between devices  75.8 us (31%)
  starting transfers between devices  57.8 us (24%)
  local copies, waits for them, and re-layouts  29.9 us (12%)
  matrix products  29 us (12%)
  other arithmetic  16.4 us (7%)
  Pallas kernels  15.2 us (6%)
  between operations  14.5 us (6%)
    all_to_all x6, starting transfers between devices, swap(): return lax.all_to_all(value, axes, 0, 0, tiled=True)  42.1 us
    all_to_all x6, waiting for transfers between devices, swap(): return lax.all_to_all(value, axes, 0, 0, tiled=True)  39.8 us
    ppermute x9, waiting for transfers between devices, ring_shift(): lax.ppermute(value, 'x', [(i, (i + step) % 4) for i in range(4)])  35.9 us
    ppermute x9, starting transfers between devices, ring_shift(): lax.ppermute(value, 'x', [(i, (i + step) % 4) for i in range(4)])  14.4 us
    dot_general x6, matrix products, exact(): lax.dot_general(a.astype(f32), b.astype(f32), (dims, ((), ())), precision...  11.4 us
    pallas_call x4, Pallas kernels, ring_grad_part(): pl.pallas_call(ring_grad_kernel, out_shape=jax.ShapeDtypeStruct((2 * half...  8.88 us
    dot_general x5, matrix products, mm(): return lax.dot_general(a, b, (dims, ((), ())), preferred_element_type=f32)  8.39 us
    pallas_call x1, Pallas kernels, weight_grad_part(): pl.pallas_call(weight_grad_kernel, out_shape=jax.ShapeDtypeStruct((quarte...  6.29 us
  transfers between devices with their start and end apart: 23, of which 14 were waited for; matrix products, arithmetic and copies ran while one was open for 26% of the time, Pallas kernels for 6%

profile of v4, /device:TPU:8, one launch (start us, length us, event | category | flops | bytes accessed | tf_op | source)
XLA Modules:
  0.0 238.5 jit_solution(5919371398296513675)
XLA Ops:
  7.3 2.9 %fusion.42 = (bf16[256,1024]{1,0:T(8,128)(2,1)}, bf16[256,1024]{1,0:T(8,128)(2,1)S(1)}, bf16[256,1024]{1,0:T(8,128)(2,1)S(1)}, bf16[256,1024]{1,0:T(8,128)(2,1)}) fusion(bf16[512,4096]{1,0:T(8,128)(2,1)} %param.14, s32[]{:T(128)S(6)} %select_n.48, s32[]{:T(128)S(6)} %select_n.54, s32[]{:T(128)S(6)} %select_n.52, s32[]{:T(128)S(6)} %select_n.49, s32[]{:T(128)S(6)} %select_n.53), kind=kLoop, calls=%fused_computation.88 | loop fusion | bytes 4194324 | tf_op jit(solution)/shard_map/dynamic_slice | solution.py:187
  10.2 1.5 collective-permute-start
  12.4 1.1 reduce-window.14
  15.3 1.1 broadcast_in_dim.62
  16.5 1.6 copy.100
  18.1 1.0 fusion.13
  20.5 4.5 %collective-permute-done.own_in.refs_1_ = bf16[256,1024]{1,0:T(8,128)(2,1)S(1)} collective-permute-done((bf16[256,1024]{1,0:T(8,128)(2,1)S(1)}, bf16[256,1024]{1,0:T(8,128)(2,1)S(1)}, u32[]{:S(2)}, u32[]{:S(2)}) %collective-permute-start) | collective-permute-done | bytes 524320 | tf_op jit(solution)/shard_map/ppermute | solution.py:57
  25.0 10.1 %all-to-all-start = ((f32[32,24,128]{2,1,0:T(8,128)}), f32[32,24,128]{2,1,0:T(8,128)S(1)}, u32[]{:S(2)}, u32[]{:S(2)}) async-start(f32[32,24,128]{2,1,0:T(8,128)} %pad_maximum_fusion.1), calls=%async_computation | async-start | bytes 786432 | tf_op jit(solution)/shard_map/all_to_all | solution.py:49
  35.2 3.4 %collective-permute-start.1 = (bf16[256,1024]{1,0:T(8,128)(2,1)}, bf16[256,1024]{1,0:T(8,128)(2,1)S(1)}, u32[]{:S(2)}, u32[]{:S(2)}) collective-permute-start(bf16[256,1024]{1,0:T(8,128)(2,1)} %get-tuple-element.49), channel_id=1, source_target_pairs={{0,128},{64,192},{128,0},{192,64},{1,129},{65,193},{129,1},{193,65... | collective-permute-start | bytes 1572872 | tf_op jit(solution)/shard_map/ppermute | solution.py:57
  38.6 1.2 collective-permute-start.2
  39.7 1.3 fusion.43
  41.0 1.0 copy.102
  42.7 9.5 %all-to-all-done = f32[32,24,128]{2,1,0:T(8,128)S(1)} async-done(((f32[32,24,128]{2,1,0:T(8,128)}), f32[32,24,128]{2,1,0:T(8,128)S(1)}, u32[]{:S(2)}, u32[]{:S(2)}) %all-to-all-start) | async-done | bytes 393248 | tf_op jit(solution)/shard_map/all_to_all | solution.py:49
  53.5 11.5 %collective-permute-done.2.own_in.refs_3_ = bf16[256,1024]{1,0:T(8,128)(2,1)S(1)} collective-permute-done((bf16[256,1024]{1,0:T(8,128)(2,1)}, bf16[256,1024]{1,0:T(8,128)(2,1)S(1)}, u32[]{:S(2)}, u32[]{:S(2)}) %collective-permute-start.2) | collective-permute-done | bytes 524320 | tf_op jit(solution)/shard_map/ppermute | solution.py:57
  65.8 8.5 %all-to-all-start.1 = ((f32[32,16,128]{2,1,0:T(8,128)}), f32[32,16,128]{2,1,0:T(8,128)S(1)}, u32[]{:S(2)}, u32[]{:S(2)}) async-start(f32[32,16,128]{2,1,0:T(8,128)} %copy.103), calls=%async_computation.1 | async-start | bytes 524288 | tf_op jit(solution)/shard_map/all_to_all | solution.py:49
  74.4 2.9 %fusion.1 = f32[8,512,64]{1,2,0:T(8,128)S(1)} fusion(bf16[512,8,64]{0,2,1:T(8,128)(2,1)} %bitcast.100, f32[512,512]{1,0:T(8,128)} %fusion.43, f32[8,512]{1,0:T(8,128)} %copy-done.24), kind=kOutput, calls=%fused_computation.5 | convolution fusion | flops 278921216 | bytes 2637824 | tf_op jit(solution)/shard_map/hts,shp->thp/dot_general | solution.py:219
  77.3 1.3 copy.106
  78.6 1.9 broadcast_in_dim.71
  80.5 2.5 %copy.105 = f32[512,512]{1,0:T(8,128)} copy(f32[512,512]{0,1:T(8,128)} %bitcast.94) | data formatting | bytes 2097152 | tf_op jit(solution)/shard_map/reshape | solution.py:199
  84.1 2.8 %all-to-all-done.1 = f32[32,16,128]{2,1,0:T(8,128)S(1)} async-done(((f32[32,16,128]{2,1,0:T(8,128)}), f32[32,16,128]{2,1,0:T(8,128)S(1)}, u32[]{:S(2)}, u32[]{:S(2)}) %all-to-all-start.1) | async-done | bytes 262176 | tf_op jit(solution)/shard_map/all_to_all | solution.py:49
  86.9 3.6 %fusion.7 = (bf16[512,512]{1,0:T(8,128)(2,1)}, f32[512,512]{1,0:T(8,128)}) fusion(bf16[512,512]{1,0:T(8,128)(2,1)} %param.9, f32[512]{0:T(512)} %mul.129, f32[512,512]{1,0:T(8,128)} %copy.106, f32[512,512]{1,0:T(8,128)} %copy.105, f32[512,128]{1,0:T(8,128)S(1)} %bitcast.91, bf16[512,128]{1,0:T(8,128)(2,1)S(1)} %copy-done), kind=kOutput, calls=%fused_computation.22 | convolution fusion | flops 404226048 | bytes 4589568 | tf_op jit(solution)/shard_map/dot_general | solution.py:39
  91.1 2.0 collective-permute-start.11
  93.1 1.6 collective-permute-start.12
  94.7 2.4 %ring_grad.4 = bf16[512,512]{1,0:T(8,128)(2,1)} custom-call(s32[1]{0:T(128)} %bitcast.core_ref, bf16[256,1024]{1,0:T(8,128)(2,1)S(1)} %collective-permute-done.1.own_in.refs_2_, bf16[256,1024]{1,0:T(8,128)(2,1)} %collective-permute-done.3.other_in.refs_6_, bf16[1024,512]{1,0:T(8,128)(2,1)S(1)} %copy-done.1), custom_call_target="tpu_custom_call" | custom-call | flops 536870912 | bytes 3145728 | tf_op jit(solution)/shard_map/ring_grad/pallas_call | solution.py:103
  97.1 2.5 %ring_grad.5 = bf16[512,512]{1,0:T(8,128)(2,1)} custom-call(s32[1]{0:T(128)} %bitcast.core_ref, bf16[256,1024]{1,0:T(8,128)(2,1)S(1)} %collective-permute-done.own_in.refs_1_, bf16[256,1024]{1,0:T(8,128)(2,1)} %collective-permute-done.5.other_in.refs_5_, bf16[1024,512]{1,0:T(8,128)(2,1)S(1)} %copy-done.1), custom_call_target="tpu_custom_call" | custom-call | flops 536870912 | bytes 3145728 | tf_op jit(solution)/shard_map/ring_grad/pallas_call | solution.py:103
  99.6 2.0 collective-permute-start.4
  101.6 2.4 %ring_grad.6 = bf16[512,512]{1,0:T(8,128)(2,1)} custom-call(s32[1]{0:T(128)} %bitcast.core_ref, bf16[256,1024]{1,0:T(8,128)(2,1)S(1)} %collective-permute-done.2.own_in.refs_3_, bf16[256,1024]{1,0:T(8,128)(2,1)} %collective-permute-done.7.other_in.refs_7_, bf16[1024,512]{1,0:T(8,128)(2,1)S(1)} %copy-done.1), custom_call_target="tpu_custom_call" | custom-call | flops 536870912 | bytes 3145728 | tf_op jit(solution)/shard_map/ring_grad/pallas_call | solution.py:103
  104.0 1.2 collective-permute-start.6
  108.3 1.6 ring_grad.7
  109.9 7.7 %collective-permute-done.11.refs_10_ = bf16[512,512]{1,0:T(8,128)(2,1)} collective-permute-done((bf16[512,512]{1,0:T(8,128)(2,1)}, bf16[512,512]{1,0:T(8,128)(2,1)}, u32[]{:S(2)}, u32[]{:S(2)}) %collective-permute-start.11) | collective-permute-done | bytes 524320 | tf_op jit(solution)/shard_map/ppermute | solution.py:57
  117.6 1.4 collective-permute-done.12.refs_11_
  118.9 1.0 copy-done.3
  120.0 1.0 copy-done.5
  121.0 6.3 %weight_grad.1 = bf16[1024,512]{1,0:T(8,128)(2,1)} custom-call(s32[1]{0:T(128)} %bitcast.core_ref, bf16[256,1024]{1,0:T(8,128)(2,1)S(1)} %get-tuple-element.28.own_in.refs_0_, bf16[256,1024]{1,0:T(8,128)(2,1)S(1)} %collective-permute-done.own_in.refs_1_, bf16[256,1024]{1,0:T(8,128)(2,1)S(1)} %collective-permute-done.1.own_in.refs_2_, ...), custom_call_target="tpu_custom_call" | custom-call | flops 2147483648 | bytes 8388608 | tf_op jit(solution)/shard_map/weight_grad/pallas_call | solution.py:143
  127.4 1.4 collective-permute-done.4
  128.7 9.0 %collective-permute-done.6 = bf16[512,512]{1,0:T(8,128)(2,1)} collective-permute-done((bf16[512,512]{1,0:T(8,128)(2,1)}, bf16[512,512]{1,0:T(8,128)(2,1)}, u32[]{:S(2)}, u32[]{:S(2)}) %collective-permute-start.6) | collective-permute-done | bytes 524320 | tf_op jit(solution)/shard_map/ppermute | solution.py:57
  138.0 2.3 fusion.11
  140.3 1.0 copy.107
  141.4 3.4 %fusion = f32[8,64,512]{2,1,0:T(8,128)} fusion(bf16[512,8,64]{0,2,1:T(8,128)(2,1)} %bitcast.102, f32[512,512]{1,0:T(8,128)S(1)} %copy-done.16, f32[8,512]{1,0:T(8,128)} %copy-done.24), kind=kOutput, calls=%fused_computation.4 | convolution fusion | flops 278921216 | bytes 2637824 | tf_op jit(solution)/shard_map/hst,shp->thp/dot_general | solution.py:244
  144.8 2.7 %copy.114 = f32[512,512]{1,0:T(8,128)} copy(f32[512,512]{0,1:T(8,128)} %bitcast.97) | data formatting | bytes 2097152 | tf_op jit(solution)/shard_map/reshape | solution.py:245
  147.5 1.7 fusion.15
  149.2 9.3 %all-to-all-start.2 = ((f32[32,16,128]{2,1,0:T(8,128)}), f32[32,16,128]{2,1,0:T(8,128)}, u32[]{:S(2)}, u32[]{:S(2)}) async-start(f32[32,16,128]{2,1,0:T(8,128)} %bitcast.19), calls=%async_computation.2 | async-start | bytes 524288 | tf_op jit(solution)/shard_map/all_to_all | solution.py:49
  158.5 1.4 reduce_sum.96
  159.9 1.3 reduce_sum.97
  161.2 2.8 %multiply_reduce_fusion = bf16[512,512]{1,0:T(8,128)(2,1)S(1)} fusion(f32[8,512]{1,0:T(8,128)} %copy-done.24, bf16[512,8,64]{0,2,1:T(8,128)(2,1)S(1)} %bitcast.103, bf16[512,8,64]{0,2,1:T(8,128)(2,1)S(1)} %bitcast.101), kind=kOutput, calls=%fused_computation | convolution fusion | flops 278659072 | bytes 1589248 | tf_op jit(solution)/shard_map/thp,shp->hts/dot_general | solution.py:247
  164.8 1.0 fusion.44
  165.8 7.6 %all-to-all-done.2 = f32[32,16,128]{2,1,0:T(8,128)} async-done(((f32[32,16,128]{2,1,0:T(8,128)}), f32[32,16,128]{2,1,0:T(8,128)}, u32[]{:S(2)}, u32[]{:S(2)}) %all-to-all-start.2) | async-done | bytes 262176 | tf_op jit(solution)/shard_map/all_to_all | solution.py:49
  173.4 1.4 fusion.21
  175.7 4.8 %all-to-all-start.3 = ((f32[32,16,128]{2,1,0:T(8,128)}), f32[32,16,128]{2,1,0:T(8,128)}, u32[]{:S(2)}, u32[]{:S(2)}) async-start(f32[32,16,128]{2,1,0:T(8,128)} %copy.111), calls=%async_computation.3 | async-start | bytes 524288 | tf_op jit(solution)/shard_map/all_to_all | solution.py:49
  180.5 2.1 fusion.45
  182.6 2.0 convolution_add_fusion
  184.6 7.0 %all-to-all-done.3 = f32[32,16,128]{2,1,0:T(8,128)} async-done(((f32[32,16,128]{2,1,0:T(8,128)}), f32[32,16,128]{2,1,0:T(8,128)}, u32[]{:S(2)}, u32[]{:S(2)}) %all-to-all-start.3) | async-done | bytes 262176 | tf_op jit(solution)/shard_map/all_to_all | solution.py:49
  191.6 3.3 %fusion.8 = (f32[512,512]{1,0:T(8,128)S(1)}, bf16[512,512]{1,0:T(8,128)(2,1)}) fusion(bf16[512,512]{1,0:T(8,128)(2,1)S(1)} %copy-done.7, f32[512,512]{1,0:T(8,128)} %get-tuple-element.56, bf16[512,512]{1,0:T(8,128)(2,1)S(1)} %get-tuple-element.43, f32[512]{0:T(512)S(1)} %copy-done.25, f32[512,512]{1,0:T(8,128)} %copy.114, f32[512,512]{1,0:T(8,128)S(1)} %copy-done.9, ...), kind=kOutput, calls=%fused_computation.23 | convolution fusion | flops 405274624 | bytes 6162432 | tf_op jit(solution)/shard_map/dot_general | solution.py:39
  194.9 1.0 fusion.19
  196.9 4.6 %all-to-all-start.4 = ((f32[32,8,128]{2,1,0:T(8,128)}), f32[32,8,128]{2,1,0:T(8,128)}, u32[]{:S(2)}, u32[]{:S(2)}) async-start(f32[32,8,128]{2,1,0:T(8,128)} %broadcast_in_dim_broadcast_in_dim_broadcast_in_dim.2), calls=%async_computation.5 | async-start | bytes 262144 | tf_op jit(solution)/shard_map/all_to_all | solution.py:49
  201.5 2.0 convolution_add_fusion.1
  203.9 1.0 pad_maximum_fusion
  205.0 6.9 %all-to-all-done.4 = f32[32,8,128]{2,1,0:T(8,128)} async-done(((f32[32,8,128]{2,1,0:T(8,128)}), f32[32,8,128]{2,1,0:T(8,128)}, u32[]{:S(2)}, u32[]{:S(2)}) %all-to-all-start.4) | async-done | bytes 131104 | tf_op jit(solution)/shard_map/all_to_all | solution.py:49
  211.9 0.9 reduce_sum.101
  213.4 1.1 reduce-window.16
  215.6 4.8 %all-to-all-start.5 = ((bf16[4,512,128]{2,1,0:T(8,128)(2,1)}), bf16[4,512,128]{2,1,0:T(8,128)(2,1)S(1)}, u32[]{:S(2)}, u32[]{:S(2)}) async-start(bf16[4,512,128]{2,1,0:T(8,128)(2,1)} %broadcast_in_dim.74), calls=%async_computation.6 | async-start | bytes 1048576 | tf_op jit(solution)/shard_map/all_to_all | solution.py:49
  220.7 1.4 multiply_reduce_fusion.1
  223.1 6.0 %all-to-all-done.5 = bf16[4,512,128]{2,1,0:T(8,128)(2,1)S(1)} async-done(((bf16[4,512,128]{2,1,0:T(8,128)(2,1)}), bf16[4,512,128]{2,1,0:T(8,128)(2,1)S(1)}, u32[]{:S(2)}, u32[]{:S(2)}) %all-to-all-start.5) | async-done | bytes 524320 | tf_op jit(solution)/shard_map/all_to_all | solution.py:49
  230.0 0.9 multiply_subtract_fusion
  (129 shorter events, 19.3 us)
Async XLA Ops:
  7.2 32.6 %copy-start = (bf16[512,128]{1,0:T(8,128)(2,1)S(1)}, bf16[512,128]{1,0:T(8,128)(2,1)}, u32[]{:S(2)}) copy-start(bf16[512,128]{1,0:T(8,128)(2,1)} %param.11) | copy-start | bytes 393220
  7.2 4.5 %copy-start.18 = (f32[128,512]{1,0:T(8,128)S(1)}, f32[128,512]{1,0:T(8,128)}, u32[]{:S(2)}) copy-start(f32[128,512]{1,0:T(8,128)} %param.15) | copy-start | bytes 786436
  7.2 5.2 %copy-start.26 = (f32[8,512]{1,0:T(8,128)S(1)}, f32[8,512]{1,0:T(8,128)}, u32[]{:S(2)}) copy-start(f32[8,512]{1,0:T(8,128)} %param.12) | copy-start | bytes 49156
  7.2 10.8 %copy-start.6 = (bf16[512,512]{1,0:T(8,128)(2,1)S(1)}, bf16[512,512]{1,0:T(8,128)(2,1)}, u32[]{:S(2)}) copy-start(bf16[512,512]{1,0:T(8,128)(2,1)} %param.9) | copy-start | bytes 1572868
  7.2 10.8 %copy-start.14 = (bf16[512,128]{1,0:T(8,128)(2,1)S(1)}, bf16[512,128]{1,0:T(8,128)(2,1)}, u32[]{:S(2)}) copy-start(bf16[512,128]{1,0:T(8,128)(2,1)} %param.10) | copy-start | bytes 393220
  7.2 57.7 %all-gather.2.cloned.1.call-start = ((), (), s32[]{:S(2)}) async-start(), calls=%async_computation.7 | async-start | bytes 1179648 | tf_op jit(solution)/shard_map/all_gather | solution.py:183
  10.2 14.9 %collective-permute-start = (bf16[256,1024]{1,0:T(8,128)(2,1)S(1)}, bf16[256,1024]{1,0:T(8,128)(2,1)S(1)}, u32[]{:S(2)}, u32[]{:S(2)}) collective-permute-start(bf16[256,1024]{1,0:T(8,128)(2,1)S(1)} %get-tuple-element.48), channel_id=1, source_target_pairs={{0,64},{64,128},{128,192},{192,0},{1,65},{65,129},{129,193},{193,1... | collective-permute-start | bytes 1572872 | tf_op jit(solution)/shard_map/ppermute | solution.py:57
  14.4 2.0 copy-start.24
  16.5 25.6 %copy-start.29 = (f32[8]{0:T(128)S(1)}, f32[8]{0:T(128)}, u32[]{:S(2)}) copy-start(f32[8]{0:T(128)} %param.13) | copy-start | bytes 100
  18.1 17.1 %copy-start.8 = (f32[512,512]{1,0:T(8,128)}, f32[512,512]{1,0:T(8,128)S(1)}, u32[]{:S(2)}) copy-start(f32[512,512]{1,0:T(8,128)S(1)} %copy.100) | copy-start | bytes 3145732
  19.1 0.7 copy-start.11
  25.0 27.2 %all-to-all-start = ((f32[32,24,128]{2,1,0:T(8,128)}), f32[32,24,128]{2,1,0:T(8,128)S(1)}, u32[]{:S(2)}, u32[]{:S(2)}) async-start(f32[32,24,128]{2,1,0:T(8,128)} %pad_maximum_fusion.1), calls=%async_computation | async-start | bytes 786432 | tf_op jit(solution)/shard_map/all_to_all | solution.py:49
  35.2 18.3 %collective-permute-start.1 = (bf16[256,1024]{1,0:T(8,128)(2,1)}, bf16[256,1024]{1,0:T(8,128)(2,1)S(1)}, u32[]{:S(2)}, u32[]{:S(2)}) collective-permute-start(bf16[256,1024]{1,0:T(8,128)(2,1)} %get-tuple-element.49), channel_id=1, source_target_pairs={{0,128},{64,192},{128,0},{192,64},{1,129},{65,193},{129,1},{193,65... | collective-permute-start | bytes 1572872 | tf_op jit(solution)/shard_map/ppermute | solution.py:57
  38.6 26.4 %collective-permute-start.2 = (bf16[256,1024]{1,0:T(8,128)(2,1)}, bf16[256,1024]{1,0:T(8,128)(2,1)S(1)}, u32[]{:S(2)}, u32[]{:S(2)}) collective-permute-start(bf16[256,1024]{1,0:T(8,128)(2,1)} %get-tuple-element.46), channel_id=1, source_target_pairs={{0,192},{64,0},{128,64},{192,128},{1,193},{65,1},{129,65},{193,129... | collective-permute-start | bytes 1572872 | tf_op jit(solution)/shard_map/ppermute | solution.py:57
  65.0 36.7 %copy-start.2 = (bf16[256,1024]{1,0:T(8,128)(2,1)}, bf16[256,1024]{1,0:T(8,128)(2,1)S(1)}, u32[]{:S(2)}) copy-start(bf16[256,1024]{1,0:T(8,128)(2,1)S(1)} %collective-permute-done.2.own_in.refs_3_) | copy-start | bytes 1572868
  65.8 21.0 %all-to-all-start.1 = ((f32[32,16,128]{2,1,0:T(8,128)}), f32[32,16,128]{2,1,0:T(8,128)S(1)}, u32[]{:S(2)}, u32[]{:S(2)}) async-start(f32[32,16,128]{2,1,0:T(8,128)} %copy.103), calls=%async_computation.1 | async-start | bytes 524288 | tf_op jit(solution)/shard_map/all_to_all | solution.py:49
  74.3 120.6 %reduce-scatter.2.cloned.1.call-start = ((), (), s32[]{:S(2)}) async-start(), calls=%async_computation.8 | async-start | bytes 1179648 | tf_op jit(solution)/shard_map/reduce_scatter | solution.py:235
  78.6 16.1 %copy-start.1 = (bf16[1024,512]{1,0:T(8,128)(2,1)S(1)}, bf16[1024,512]{1,0:T(8,128)(2,1)}, u32[]{:S(2)}) copy-start(bf16[1024,512]{1,0:T(8,128)(2,1)} %all-gather.2.cloned.1.call-done.weight_in) | copy-start | bytes 3145732
  83.1 8.0 %collective-permute-start.3 = (bf16[256,1024]{1,0:T(8,128)(2,1)S(1)}, bf16[256,1024]{1,0:T(8,128)(2,1)}, u32[]{:S(2)}, u32[]{:S(2)}) collective-permute-start(bf16[256,1024]{1,0:T(8,128)(2,1)S(1)} %collective-permute-done.1.own_in.refs_2_), channel_id=1, source_target_pairs={{0,1},{1,0},{2,3},{3,2},{4,5},{5,4},{6,7},{7,6},{8,9},{9,8},{10,11... | collective-permute-start | bytes 1572872 | tf_op jit(solution)/shard_map/ppermute | solution.py:53
  83.1 10.0 %collective-permute-start.5 = (bf16[256,1024]{1,0:T(8,128)(2,1)S(1)}, bf16[256,1024]{1,0:T(8,128)(2,1)}, u32[]{:S(2)}, u32[]{:S(2)}) collective-permute-start(bf16[256,1024]{1,0:T(8,128)(2,1)S(1)} %collective-permute-done.own_in.refs_1_), channel_id=1, source_target_pairs={{0,1},{1,0},{2,3},{3,2},{4,5},{5,4},{6,7},{7,6},{8,9},{9,8},{10,11... | collective-permute-start | bytes 1572872 | tf_op jit(solution)/shard_map/ppermute | solution.py:53
  83.6 16.0 %collective-permute-start.7 = (bf16[256,1024]{1,0:T(8,128)(2,1)S(1)}, bf16[256,1024]{1,0:T(8,128)(2,1)}, u32[]{:S(2)}, u32[]{:S(2)}) collective-permute-start(bf16[256,1024]{1,0:T(8,128)(2,1)S(1)} %collective-permute-done.2.own_in.refs_3_), channel_id=1, source_target_pairs={{0,1},{1,0},{2,3},{3,2},{4,5},{5,4},{6,7},{7,6},{8,9},{9,8},{10,11... | collective-permute-start | bytes 1572872 | tf_op jit(solution)/shard_map/ppermute | solution.py:53
  83.6 20.4 %collective-permute-start.9 = (bf16[256,1024]{1,0:T(8,128)(2,1)S(1)}, bf16[256,1024]{1,0:T(8,128)(2,1)}, u32[]{:S(2)}, u32[]{:S(2)}) collective-permute-start(bf16[256,1024]{1,0:T(8,128)(2,1)S(1)} %get-tuple-element.28.own_in.refs_0_), channel_id=1, source_target_pairs={{0,1},{1,0},{2,3},{3,2},{4,5},{5,4},{6,7},{7,6},{8,9},{9,8},{10,11... | collective-permute-start | bytes 1572872 | tf_op jit(solution)/shard_map/ppermute | solution.py:53
  90.5 14.8 %collective-permute-start.10 = (bf16[512,512]{1,0:T(8,128)(2,1)}, bf16[512,512]{1,0:T(8,128)(2,1)S(1)}, u32[]{:S(2)}, u32[]{:S(2)}) collective-permute-start(bf16[512,512]{1,0:T(8,128)(2,1)} %get-tuple-element.55.refs_8_), channel_id=1, source_target_pairs={{0,64},{64,128},{128,192},{192,0},{1,65},{65,129},{129,193},{193,1... | collective-permute-start | bytes 1572872 | tf_op jit(solution)/shard_map/ppermute | solution.py:57
  91.1 26.5 %collective-permute-start.11 = (bf16[512,512]{1,0:T(8,128)(2,1)}, bf16[512,512]{1,0:T(8,128)(2,1)}, u32[]{:S(2)}, u32[]{:S(2)}) collective-permute-start(bf16[512,512]{1,0:T(8,128)(2,1)} %get-tuple-element.55.refs_8_), channel_id=1, source_target_pairs={{0,128},{64,192},{128,0},{192,64},{1,129},{65,193},{129,1},{193,65... | collective-permute-start | bytes 1572872 | tf_op jit(solution)/shard_map/ppermute | solution.py:57
  93.1 25.9 %collective-permute-start.12 = (bf16[512,512]{1,0:T(8,128)(2,1)}, bf16[512,512]{1,0:T(8,128)(2,1)}, u32[]{:S(2)}, u32[]{:S(2)}) collective-permute-start(bf16[512,512]{1,0:T(8,128)(2,1)} %get-tuple-element.55.refs_8_), channel_id=1, source_target_pairs={{0,192},{64,0},{128,64},{192,128},{1,193},{65,1},{129,65},{193,129... | collective-permute-start | bytes 1572872 | tf_op jit(solution)/shard_map/ppermute | solution.py:57
  99.6 29.2 %collective-permute-start.4 = (bf16[512,512]{1,0:T(8,128)(2,1)}, bf16[512,512]{1,0:T(8,128)(2,1)}, u32[]{:S(2)}, u32[]{:S(2)}) collective-permute-start(bf16[512,512]{1,0:T(8,128)(2,1)} %ring_grad.4), channel_id=1, source_target_pairs={{0,128},{64,192},{128,0},{192,64},{1,129},{65,193},{129,1},{193,65... | collective-permute-start | bytes 1572872 | tf_op jit(solution)/shard_map/ppermute | solution.py:57
  104.0 33.7 %collective-permute-start.6 = (bf16[512,512]{1,0:T(8,128)(2,1)}, bf16[512,512]{1,0:T(8,128)(2,1)}, u32[]{:S(2)}, u32[]{:S(2)}) collective-permute-start(bf16[512,512]{1,0:T(8,128)(2,1)} %ring_grad.5), channel_id=1, source_target_pairs={{0,192},{64,0},{128,64},{192,128},{1,193},{65,1},{129,65},{193,129... | collective-permute-start | bytes 1572872 | tf_op jit(solution)/shard_map/ppermute | solution.py:57
  105.3 0.8 copy-start.4
  106.1 31.9 %collective-permute-start.8 = (bf16[512,512]{1,0:T(8,128)(2,1)}, bf16[512,512]{1,0:T(8,128)(2,1)}, u32[]{:S(2)}, u32[]{:S(2)}) collective-permute-start(bf16[512,512]{1,0:T(8,128)(2,1)} %ring_grad.6), channel_id=1, source_target_pairs={{0,64},{64,128},{128,192},{192,0},{1,65},{65,129},{129,193},{193,1... | collective-permute-start | bytes 1572872 | tf_op jit(solution)/shard_map/ppermute | solution.py:57
  118.9 1.0 copy-start.3
  120.0 1.0 copy-start.5
  121.0 17.0 %copy-start.7 = (bf16[512,512]{1,0:T(8,128)(2,1)S(1)}, bf16[512,512]{1,0:T(8,128)(2,1)}, u32[]{:S(2)}) copy-start(bf16[512,512]{1,0:T(8,128)(2,1)} %param.9) | copy-start | bytes 1572868
  127.3 14.0 %copy-start.16 = (f32[512,512]{1,0:T(8,128)S(1)}, f32[512,512]{1,0:T(8,128)}, u32[]{:S(2)}) copy-start(f32[512,512]{1,0:T(8,128)} %fusion.43) | copy-start | bytes 3145732
  141.4 6.1 %copy-start.10 = (f32[512,512]{1,0:T(8,128)S(1)}, f32[512,512]{1,0:T(8,128)}, u32[]{:S(2)}) copy-start(f32[512,512]{1,0:T(8,128)} %copy.105) | copy-start | bytes 3145732
  144.8 16.4 %copy-start.21 = (bf16[512,512]{0,1:T(8,128)(2,1)S(1)}, bf16[512,512]{0,1:T(8,128)(2,1)}, u32[]{:S(2)}) copy-start(bf16[512,512]{0,1:T(8,128)(2,1)} %copy.102) | copy-start | bytes 1572868
  144.8 16.4 %copy-start.22 = (bf16[512,512]{0,1:T(8,128)(2,1)S(1)}, bf16[512,512]{0,1:T(8,128)(2,1)}, u32[]{:S(2)}) copy-start(bf16[512,512]{0,1:T(8,128)(2,1)} %copy.107) | copy-start | bytes 1572868
  149.2 24.3 %all-to-all-start.2 = ((f32[32,16,128]{2,1,0:T(8,128)}), f32[32,16,128]{2,1,0:T(8,128)}, u32[]{:S(2)}, u32[]{:S(2)}) async-start(f32[32,16,128]{2,1,0:T(8,128)} %bitcast.19), calls=%async_computation.2 | async-start | bytes 524288 | tf_op jit(solution)/shard_map/all_to_all | solution.py:49
  161.2 3.6 %copy-start.15 = (bf16[512,128]{1,0:T(8,128)(2,1)S(1)}, bf16[512,128]{1,0:T(8,128)(2,1)}, u32[]{:S(2)}) copy-start(bf16[512,128]{1,0:T(8,128)(2,1)} %param.10) | copy-start | bytes 393220
  164.0 0.8 copy-start.13
  164.8 26.8 %copy-start.9 = (f32[512,512]{1,0:T(8,128)S(1)}, f32[512,512]{1,0:T(8,128)}, u32[]{:S(2)}) copy-start(f32[512,512]{1,0:T(8,128)} %copy-done.8) | copy-start | bytes 3145732
  174.8 16.8 %copy-start.25 = (f32[512]{0:T(512)S(1)}, f32[512]{0:T(512)}, u32[]{:S(2)}) copy-start(f32[512]{0:T(512)} %mul.129) | copy-start | bytes 6148
  175.7 15.9 %all-to-all-start.3 = ((f32[32,16,128]{2,1,0:T(8,128)}), f32[32,16,128]{2,1,0:T(8,128)}, u32[]{:S(2)}, u32[]{:S(2)}) async-start(f32[32,16,128]{2,1,0:T(8,128)} %copy.111), calls=%async_computation.3 | async-start | bytes 524288 | tf_op jit(solution)/shard_map/all_to_all | solution.py:49
  182.6 13.6 %copy-start.28 = (f32[8]{0:T(128)S(1)}, f32[8]{0:T(128)}, u32[]{:S(2)}) copy-start(f32[8]{0:T(128)} %reduce_sum.97) | copy-start | bytes 100
  194.9 9.0 %copy-start.17 = (f32[512,128]{1,0:T(8,128)S(1)}, f32[512,128]{1,0:T(8,128)}, u32[]{:S(2)}) copy-start(f32[512,128]{1,0:T(8,128)} %convolution_add_fusion) | copy-start | bytes 786436
  196.9 15.0 %all-to-all-start.4 = ((f32[32,8,128]{2,1,0:T(8,128)}), f32[32,8,128]{2,1,0:T(8,128)}, u32[]{:S(2)}, u32[]{:S(2)}) async-start(f32[32,8,128]{2,1,0:T(8,128)} %broadcast_in_dim_broadcast_in_dim_broadcast_in_dim.2), calls=%async_computation.5 | async-start | bytes 262144 | tf_op jit(solution)/shard_map/all_to_all | solution.py:49
  203.6 17.2 %copy-start.12 = (f32[512,128]{1,0:T(8,128)S(1)}, f32[512,128]{1,0:T(8,128)}, u32[]{:S(2)}) copy-start(f32[512,128]{1,0:T(8,128)} %copy-done.11) | copy-start | bytes 786436
  203.6 17.2 %copy-start.27 = (f32[32]{0:T(128)S(1)}, f32[32]{0:T(128)}, u32[]{:S(2)}) copy-start(f32[32]{0:T(128)} %mul.144) | copy-start | bytes 388
  203.6 25.6 %copy-start.30 = (f32[8]{0:T(128)S(1)}, f32[8]{0:T(128)}, u32[]{:S(2)}) copy-start(f32[8]{0:T(128)} %param.17) | copy-start | bytes 100
  203.9 26.0 %copy-start.19 = (f32[128,512]{1,0:T(8,128)S(1)}, f32[128,512]{1,0:T(8,128)}, u32[]{:S(2)}) copy-start(f32[128,512]{1,0:T(8,128)} %param.15) | copy-start | bytes 786436
  203.9 26.0 %copy-start.20 = (bf16[128,512]{1,0:T(8,128)(2,1)S(1)}, bf16[128,512]{1,0:T(8,128)(2,1)}, u32[]{:S(2)}) copy-start(bf16[128,512]{1,0:T(8,128)(2,1)} %reduce-scatter.2.cloned.1.call-done) | copy-start | bytes 393220
  203.9 26.0 %copy-start.23 = (f32[128,512]{1,0:T(8,128)S(1)}, f32[128,512]{1,0:T(8,128)}, u32[]{:S(2)}) copy-start(f32[128,512]{1,0:T(8,128)} %param.16) | copy-start | bytes 786436
  212.8 1.9 collective-permute-start.13
  215.6 13.4 %all-to-all-start.5 = ((bf16[4,512,128]{2,1,0:T(8,128)(2,1)}), bf16[4,512,128]{2,1,0:T(8,128)(2,1)S(1)}, u32[]{:S(2)}, u32[]{:S(2)}) async-start(bf16[4,512,128]{2,1,0:T(8,128)(2,1)} %broadcast_in_dim.74), calls=%async_computation.6 | async-start | bytes 1048576 | tf_op jit(solution)/shard_map/all_to_all | solution.py:49
  229.1 1.7 collective-permute-start.14
Sparse Core Ops, SparseCore 0:
  12.5 44.8 all-gather.1
  127.5 49.8 reduce-scatter.1

commit v5 on v4

--- a/solution.py
+++ b/solution.py
@@ -181,11 +181,13 @@
     quarter = WIDTH // 4
 
     weight_rows = lax.all_gather(out_master.astype(bf16), "z", axis=0, tiled=True)
-    owns = []
-    for step in range(4):
+    def piece(step, start, rows):
         to = lax.rem(ring + step, 4)
-        piece = lax.dynamic_slice(out_grad, (core * half, to * quarter), (half, quarter))
-        owns.append(ring_shift(piece, step))
+        return lax.dynamic_slice(out_grad, (core * half + start, to * quarter), (rows, quarter))
+
+    near = half // 2
+    up = ring_shift(jnp.concatenate([piece(1, 0, half), piece(2, 0, near)]), 1)
+    down = ring_shift(jnp.concatenate([piece(3, 0, half), piece(2, near, near)]), 3)
 
     running = jnp.cumsum(log_decay, axis=1)
     last_sum = running[:, -1:]
@@ -206,12 +208,14 @@
     packed = jnp.concatenate(
         [local_state.reshape(BLOCKS, 16, 128), totals.reshape(BLOCKS, 8, 128)], axis=1
     )
-    packed, owns[1] = lax.optimization_barrier((packed, owns[1]))
+    packed, up, down = lax.optimization_barrier((packed, up, down))
+    far = jnp.concatenate([ring_shift(up[half:], 1), ring_shift(down[half:], 3)])
+    owns = [piece(0, 0, half), up[:half], far, down[:half]]
     packed = swap(packed, CTX)
     weights = block_weights(packed[:, 16, 0])
-    start = chain(weights, packed[:, :16], False)
-    start, weight_rows, owns = lax.optimization_barrier((start, weight_rows, owns))
-    start = swap(start, CTX).reshape(width, 128)
+    start = swap(chain(weights, packed[:, :16], False), CTX).reshape(width, 128)
+    others = [swap_core(piece) for piece in owns]
+    start, weight_rows = lax.optimization_barrier((start, weight_rows))
 
     scores = mm(read_vector, write_vector, ((1,), (1,)))
     mixed = (lower_decay * scores[None]).astype(bf16)
@@ -220,14 +224,20 @@
     core_y = inner.reshape(tokens, width) + exact(read_vector, start, ((1,), (1,))) * from_start_wide
     out_y = (core_y + skip_wide * head_x).astype(bf16)
 
-    others = [swap_core(piece) for piece in owns]
     core_one = jnp.full((1,), core, jnp.int32)
+    part_far, part_down, part_up, part_own = (
+        ring_grad_part(core_one, owns[step], others[step], weight_rows) for step in (2, 3, 1, 0)
+    )
+    from_up = ring_shift(part_far[:half], 1).astype(f32) + part_down[:half].astype(f32)
+    from_down = ring_shift(part_far[half:], 3).astype(f32) + part_up[half:].astype(f32)
     parts = [
-        ring_shift(ring_grad_part(core_one, owns[step], others[step], weight_rows), 4 - step)
-        for step in (2, 1, 3)
+        part_own,
+        ring_shift(jnp.concatenate([from_up.astype(bf16), part_down[half:]]), 1),
+        ring_shift(jnp.concatenate([part_up[:half], from_down.astype(bf16)]), 3),
     ]
-    parts.append(ring_grad_part(core_one, owns[0], others[0], weight_rows))
-    ring_y = [ring_shift(out_y, step) for step in range(4)]
+    y_up, y_down = ring_shift(out_y, 1), ring_shift(out_y, 3)
+    y_far = jnp.concatenate([ring_shift(y_up[:half], 1), ring_shift(y_down[half:], 3)])
+    ring_y = [out_y, y_up, y_far, y_down]
     parts, _ = lax.optimization_barrier((parts, out_y))
     grad_low = sum(part.astype(f32) for part in parts).astype(bf16)
 
@@ -242,8 +252,6 @@
 
     grad_heads = grad_low.reshape(tokens, heads, head_width)
     inner = jnp.einsum("hst,shp->thp", mixed, grad_heads, preferred_element_type=f32)
-    core_grad = inner.reshape(tokens, width) + exact(write_vector, end, ((1,), (1,))) * to_end_wide
-    input_grad = (core_grad + skip_wide * grad).astype(bf16)
     cross_dots = jnp.einsum("thp,shp->hts", grad_heads, x_heads, preferred_element_type=f32)
     pair_weights = jnp.sum(lower_decay * cross_dots, axis=0).astype(bf16)
     read_grad = mm(pair_weights, write_vector, ((1,), (0,))) + mm(
@@ -252,6 +260,26 @@
     write_grad = mm(pair_weights, read_vector, ((0,), (0,))) + mm(
         x_decayed.astype(bf16), end.astype(bf16), ((1,), (0,))
     )
+
+    both = jnp.concatenate([write_grad, read_grad], axis=0)
+    both, end = lax.optimization_barrier((both, end))
+    keep = lax.dynamic_slice_in_dim(both, core * tokens, tokens, axis=0)
+    give = lax.dynamic_slice_in_dim(both, (1 - core) * tokens, tokens, axis=0)
+    mine = (keep + swap_core(give)).astype(bf16)
+    column = lax.axis_index("y")
+    terms = [mine] + [
+        lax.ppermute(mine, "y", [(i, (i + step) % 4) for i in range(4)]) for step in range(1, 4)
+    ]
+    keep = 0.0
+    for y in range(4):
+        keep = keep + lax.select_n(lax.rem(column + 4 - y, 4), *terms).astype(f32)
+    give = swap_core(keep)
+    write_sum = jnp.where(core == 0, keep, give)
+    read_sum = jnp.where(core == 0, give, keep)
+
+    core_grad = inner.reshape(tokens, width) + exact(write_vector, end, ((1,), (1,))) * to_end_wide
+    input_grad = (core_grad + skip_wide * grad).astype(bf16)
+
     terms = (grad * core_y - head_x * core_grad).reshape(tokens, heads, head_width)
     decay_part = jnp.sum(terms, axis=2).T
     local_tail = jnp.flip(jnp.cumsum(jnp.flip(decay_part, 1), axis=1), 1)
@@ -266,16 +294,6 @@
     small = jnp.concatenate([skip_part, square_part, jnp.zeros((112,), f32)])
     small = spread(jnp.broadcast_to(small[None], (8, 128)), CTX, BLOCKS)
     small = jnp.sum(small, axis=0)[0]
-
-    both = jnp.concatenate([write_grad, read_grad], axis=0)
-    both, small = lax.optimization_barrier((both, small))
-    keep = lax.dynamic_slice_in_dim(both, core * tokens, tokens, axis=0)
-    give = lax.dynamic_slice_in_dim(both, (1 - core) * tokens, tokens, axis=0)
-    keep = keep + swap_core(give)
-    keep = jnp.sum(spread(keep.astype(bf16), "y", 4).astype(f32), axis=0)
-    give = swap_core(keep)
-    write_sum = jnp.where(core == 0, keep, give)
-    read_sum = jnp.where(core == 0, give, keep)
 
     skip_total, square_total = small[:heads], small[heads : 2 * heads]
     mean_square = square_total / float(WIDTH * head_width)

time: 242 us -> 235 us (0.971)
  waiting for transfers between devices: 75.8 us -> 52.8 us
  starting transfers between devices: 57.8 us -> 69.5 us
  other arithmetic: 16.4 us -> 21.7 us
  Pallas kernels: 15.2 us -> 12 us
    all_to_all x6 -> x5, waiting for transfers between devices: 39.8 us -> 20.6 us  [swap(): return lax.all_to_all(value, axes, 0, 0, tiled=True)]
    ppermute x9 -> x12, waiting for transfers between devices: 35.9 us -> 27.6 us  [ring_shift(): lax.ppermute(value, 'x', [(i, (i + step) % 4) for i in range(4)])]
    slice x2 -> x12, local copies, waits for them, and re-layouts: 0.18 us -> 8.26 us  [the longest x2 2.15 us: shards(): owns = [piece(0, 0, half), up[:half], far, down[:half]]]
    concatenate x0 -> x5, other arithmetic: none -> 4.68 us  [the longest x1 1.07 us: shards(): jnp.concatenate([ring_shift(y_up[:half], 1), ring_shift(y_down[half:], 3)])]
    ppermute x0 -> x3, waiting for transfers between devices: none -> 4.59 us  [shards(): lax.ppermute(mine, 'y', [(i, (i + step) % 4) for i in range(4)])]
    ppermute x0 -> x3, starting transfers between devices: none -> 4.28 us  [shards(): lax.ppermute(mine, 'y', [(i, (i + step) % 4) for i in range(4)])]
    all_to_all x6 -> x5, starting transfers between devices: 42.1 us -> 46.1 us  [swap(): return lax.all_to_all(value, axes, 0, 0, tiled=True)]
    ppermute x9 -> x12, starting transfers between devices: 14.4 us -> 18.2 us  [ring_shift(): lax.ppermute(value, 'x', [(i, (i + step) % 4) for i in range(4)])]
  transfers between devices with their start and end apart: 23 -> 28, of which waited for: 14 -> 11; matrix products, arithmetic and copies ran while one was open for 26% -> 32% of each run, Pallas kernels for 6% -> 5%
where the time goes in v5:
time: 235 us; the launch traced here: 233 us
  starting transfers between devices  69.5 us (30%)
  waiting for transfers between devices  52.8 us (22%)
  local copies, waits for them, and re-layouts  32.2 us (14%)
  matrix products  30.6 us (13%)
  other arithmetic  21.7 us (9%)
  between operations  14.6 us (6%)
  Pallas kernels  12 us (5%)
    all_to_all x5, starting transfers between devices, swap(): return lax.all_to_all(value, axes, 0, 0, tiled=True)  46.1 us
    ppermute x12, waiting for transfers between devices, ring_shift(): lax.ppermute(value, 'x', [(i, (i + step) % 4) for i in range(4)])  27.6 us
    all_to_all x5, waiting for transfers between devices, swap(): return lax.all_to_all(value, axes, 0, 0, tiled=True)  20.6 us
    ppermute x12, starting transfers between devices, ring_shift(): lax.ppermute(value, 'x', [(i, (i + step) % 4) for i in range(4)])  18.2 us
    dot_general x6, matrix products, exact(): lax.dot_general(a.astype(f32), b.astype(f32), (dims, ((), ())), precision...  11.3 us
    dot_general x5, matrix products, mm(): return lax.dot_general(a, b, (dims, ((), ())), preferred_element_type=f32)  8.78 us
    pallas_call x1, Pallas kernels, weight_grad_part(): pl.pallas_call(weight_grad_kernel, out_shape=jax.ShapeDtypeStruct((quarte...  6.1 us
    pallas_call x4, Pallas kernels, ring_grad_part(): pl.pallas_call(ring_grad_kernel, out_shape=jax.ShapeDtypeStruct((2 * half...  5.87 us
  transfers between devices with their start and end apart: 28, of which 11 were waited for; matrix products, arithmetic and copies ran while one was open for 32% of the time, Pallas kernels for 5%

profile of v5, /device:TPU:8, one launch (start us, length us, event | category | flops | bytes accessed | tf_op | source)
XLA Modules:
  0.0 233.4 jit_solution(16829707890590968256)
XLA Ops:
  7.3 1.1 fusion.43
  8.4 1.5 fusion.42
  10.9 1.5 collective-permute-start.1
  13.4 1.7 collective-permute-start.2
  15.8 1.1 reduce-window.14
  19.3 1.7 fusion.13
  21.1 1.8 pad_maximum_fusion.6
  22.8 8.9 %collective-permute-done.1 = bf16[384,1024]{1,0:T(8,128)(2,1)} collective-permute-done((bf16[384,1024]{1,0:T(8,128)(2,1)}, bf16[384,1024]{1,0:T(8,128)(2,1)}, u32[]{:S(2)}, u32[]{:S(2)}) %collective-permute-start.1) | collective-permute-done | bytes 786464 | tf_op jit(solution)/shard_map/ppermute | solution.py:57
  32.7 11.2 %all-to-all-start = ((f32[32,24,128]{2,1,0:T(8,128)}), f32[32,24,128]{2,1,0:T(8,128)S(1)}, u32[]{:S(2)}, u32[]{:S(2)}) async-start(f32[32,24,128]{2,1,0:T(8,128)} %pad_maximum_fusion.6), calls=%async_computation | async-start | bytes 786432 | tf_op jit(solution)/shard_map/all_to_all | solution.py:49
  44.9 1.9 collective-permute-start.3
  49.4 1.5 collective-permute-start.4
  51.0 1.3 fusion.45
  52.2 3.1 %collective-permute-done.3 = bf16[128,1024]{1,0:T(8,128)(2,1)S(1)} collective-permute-done((bf16[128,1024]{1,0:T(8,128)(2,1)S(1)}, bf16[128,1024]{1,0:T(8,128)(2,1)S(1)}, u32[]{:S(2)}, u32[]{:S(2)}) %collective-permute-start.3) | collective-permute-done | bytes 262176 | tf_op jit(solution)/shard_map/ppermute | solution.py:57
  55.4 4.8 %collective-permute-done.4 = bf16[128,1024]{1,0:T(8,128)(2,1)S(1)} collective-permute-done((bf16[128,1024]{1,0:T(8,128)(2,1)S(1)}, bf16[128,1024]{1,0:T(8,128)(2,1)S(1)}, u32[]{:S(2)}, u32[]{:S(2)}) %collective-permute-start.4) | collective-permute-done | bytes 262176 | tf_op jit(solution)/shard_map/ppermute | solution.py:57
  62.2 8.9 %all-to-all-start.1 = ((f32[32,16,128]{2,1,0:T(8,128)}), f32[32,16,128]{2,1,0:T(8,128)S(1)}, u32[]{:S(2)}, u32[]{:S(2)}) async-start(f32[32,16,128]{2,1,0:T(8,128)} %copy.101), calls=%async_computation.1 | async-start | bytes 524288 | tf_op jit(solution)/shard_map/all_to_all | solution.py:49
  71.2 2.9 %fusion.1 = f32[8,512,64]{1,2,0:T(8,128)S(1)} fusion(bf16[512,8,64]{0,2,1:T(8,128)(2,1)} %bitcast.103, f32[512,512]{1,0:T(8,128)} %fusion.45, f32[8,512]{1,0:T(8,128)S(1)} %copy-done.22), kind=kOutput, calls=%fused_computation.5 | convolution fusion | flops 278921216 | bytes 2637824 | tf_op jit(solution)/shard_map/hts,shp->thp/dot_general | solution.py:223
  74.1 1.3 copy.105
  75.5 1.3 copy.104
  76.9 1.1 slice.78.own_in.refs_3_
  78.0 1.1 slice.81.own_in.refs_1_
  79.6 3.9 %all-to-all-done.1 = f32[32,16,128]{2,1,0:T(8,128)S(1)} async-done(((f32[32,16,128]{2,1,0:T(8,128)}), f32[32,16,128]{2,1,0:T(8,128)S(1)}, u32[]{:S(2)}, u32[]{:S(2)}) %all-to-all-start.1) | async-done | bytes 262176 | tf_op jit(solution)/shard_map/all_to_all | solution.py:49
  84.4 1.2 copy-done.1
  87.8 1.2 collective-permute-start.6
  88.9 3.0 %fusion.7 = (bf16[512,512]{1,0:T(8,128)(2,1)}, f32[512,512]{1,0:T(8,128)}) fusion(bf16[512,512]{1,0:T(8,128)(2,1)} %param.9, f32[512]{0:T(512)} %mul.134, f32[512,512]{1,0:T(8,128)S(1)} %copy-done.13, f32[512,512]{1,0:T(8,128)S(1)} %copy-done.10, f32[512,128]{1,0:T(8,128)S(1)} %bitcast.94, bf16[512,128]{1,0:T(8,128)(2,1)S(1)} %copy-done), kind=kOutput, calls=%fused_computation.22 | convolution fusion | flops 404226048 | bytes 4589568 | tf_op jit(solution)/shard_map/dot_general | solution.py:39
  91.9 1.2 collective-permute-start.17
  93.1 2.0 collective-permute-start.19
  95.2 1.6 ring_grad.6
  97.9 1.6 ring_grad.7
  100.4 1.1 collective-permute-start.8
  101.5 8.6 %collective-permute-done.10 = bf16[256,512]{1,0:T(8,128)(2,1)S(1)} collective-permute-done((bf16[256,512]{1,0:T(8,128)(2,1)S(1)}, bf16[256,512]{1,0:T(8,128)(2,1)S(1)}, u32[]{:S(2)}, u32[]{:S(2)}) %collective-permute-start.10) | collective-permute-done | bytes 262176 | tf_op jit(solution)/shard_map/ppermute | solution.py:57
  111.0 3.0 %collective-permute-start.11 = (bf16[512,512]{1,0:T(8,128)(2,1)}, bf16[512,512]{1,0:T(8,128)(2,1)}, u32[]{:S(2)}, u32[]{:S(2)}) collective-permute-start(bf16[512,512]{1,0:T(8,128)(2,1)} %pad_maximum_fusion.3), channel_id=1, source_target_pairs={{0,192},{64,0},{128,64},{192,128},{1,193},{65,1},{129,65},{193,129... | collective-permute-start | bytes 1572872 | tf_op jit(solution)/shard_map/ppermute | solution.py:57
  114.1 1.3 mul.146
  115.4 1.3 mul.147
  116.7 1.6 ring_grad.4
  118.3 1.7 slice.104
  120.2 1.7 slice.103
  121.9 1.8 collective-permute-start.18
  123.8 1.1 collective-permute-done.11
  124.9 2.2 fusion.11
  128.1 3.9 %multiply_reduce_fusion = bf16[512,512]{1,0:T(8,128)(2,1)} fusion(f32[8,512]{1,0:T(8,128)} %copy-done.21, bf16[512,8,64]{0,2,1:T(8,128)(2,1)} %bitcast.105, bf16[512,8,64]{0,2,1:T(8,128)(2,1)S(1)} %bitcast.104), kind=kOutput, calls=%fused_computation | convolution fusion | flops 278659072 | bytes 1589248 | tf_op jit(solution)/shard_map/thp,shp->hts/dot_general | solution.py:255
  132.0 1.7 fusion.15
  133.7 11.6 %all-to-all-start.2 = ((f32[32,16,128]{2,1,0:T(8,128)}), f32[32,16,128]{2,1,0:T(8,128)}, u32[]{:S(2)}, u32[]{:S(2)}) async-start(f32[32,16,128]{2,1,0:T(8,128)} %bitcast.99), calls=%async_computation.2 | async-start | bytes 524288 | tf_op jit(solution)/shard_map/all_to_all | solution.py:49
  145.4 2.1 fusion.46
  148.5 6.1 %weight_grad.1 = bf16[1024,512]{1,0:T(8,128)(2,1)} custom-call(s32[1]{0:T(128)} %bitcast.core_ref, bf16[256,1024]{1,0:T(8,128)(2,1)S(1)} %get-tuple-element.40.own_in.refs_0_, bf16[256,1024]{1,0:T(8,128)(2,1)S(1)} %slice.81.own_in.refs_1_, bf16[256,1024]{1,0:T(8,128)(2,1)S(1)} %constant_dynamic-update-slice_fusion.own_in.refs_2_, ...), custom_call_target="tpu_custom_call" | custom-call | flops 2147483648 | bytes 8388608 | tf_op jit(solution)/shard_map/weight_grad/pallas_call | solution.py:143
  154.7 3.7 %fusion = f32[8,64,512]{2,1,0:T(8,128)} fusion(bf16[512,8,64]{0,2,1:T(8,128)(2,1)} %bitcast.106, f32[512,512]{1,0:T(8,128)} %fusion.45, f32[8,512]{1,0:T(8,128)} %copy-done.21), kind=kOutput, calls=%fused_computation.4 | convolution fusion | flops 278921216 | bytes 2637824 | tf_op jit(solution)/shard_map/hst,shp->thp/dot_general | solution.py:254
  158.4 1.5 fusion.21
  160.8 9.8 %all-to-all-start.3 = ((f32[32,16,128]{2,1,0:T(8,128)}), f32[32,16,128]{2,1,0:T(8,128)}, u32[]{:S(2)}, u32[]{:S(2)}) async-start(f32[32,16,128]{2,1,0:T(8,128)} %copy.110), calls=%async_computation.3 | async-start | bytes 524288 | tf_op jit(solution)/shard_map/all_to_all | solution.py:49
  170.7 2.0 convolution_add_fusion
  172.6 2.1 fusion.47
  174.7 1.6 copy.113
  176.5 7.3 %all-to-all-done.3 = f32[32,16,128]{2,1,0:T(8,128)} async-done(((f32[32,16,128]{2,1,0:T(8,128)}), f32[32,16,128]{2,1,0:T(8,128)}, u32[]{:S(2)}, u32[]{:S(2)}) %all-to-all-start.3) | async-done | bytes 262176 | tf_op jit(solution)/shard_map/all_to_all | solution.py:49
  183.7 1.4 convolution_add_fusion.1
  187.7 3.0 %fusion.8 = (f32[512,512]{1,0:T(8,128)}, bf16[512,512]{1,0:T(8,128)(2,1)}) fusion(bf16[512,512]{1,0:T(8,128)(2,1)S(1)} %copy-done.7, f32[512,512]{1,0:T(8,128)S(1)} %copy-done.14, bf16[512,512]{1,0:T(8,128)(2,1)S(1)} %get-tuple-element.35, f32[512]{0:T(512)S(1)} %copy-done.24, f32[512,512]{1,0:T(8,128)S(1)} %copy.113, f32[512,512]{1,0:T(8,128)S(1)} %copy-done.9, ...), kind=kOutput, calls=%fused_computation.23 | convolution fusion | flops 405274624 | bytes 6162432 | tf_op jit(solution)/shard_map/dot_general | solution.py:39
  190.8 1.6 copy.114
  192.8 1.1 reduce-window.16
  194.5 1.1 add_convert_fusion.3
  195.6 2.3 collective-permute-start.14
  197.8 1.4 collective-permute-start.15
  199.9 1.3 multiply_reduce_fusion.1
  201.3 2.2 collective-permute-done.14
  203.5 2.4 %collective-permute-done.15 = bf16[512,128]{1,0:T(8,128)(2,1)S(1)} collective-permute-done((bf16[512,128]{1,0:T(8,128)(2,1)S(1)}, bf16[512,128]{1,0:T(8,128)(2,1)S(1)}, u32[]{:S(2)}, u32[]{:S(2)}) %collective-permute-start.15) | collective-permute-done | bytes 131104 | tf_op jit(solution)/shard_map/ppermute | solution.py:271
  208.1 4.5 %all-to-all-start.4 = ((f32[32,8,128]{2,1,0:T(8,128)}), f32[32,8,128]{2,1,0:T(8,128)S(1)}, u32[]{:S(2)}, u32[]{:S(2)}) async-start(f32[32,8,128]{2,1,0:T(8,128)} %broadcast_in_dim_broadcast_in_dim_broadcast_in_dim.2), calls=%async_computation.5 | async-start | bytes 262144 | tf_op jit(solution)/shard_map/all_to_all | solution.py:49
  214.1 9.4 %all-to-all-done.4 = f32[32,8,128]{2,1,0:T(8,128)S(1)} async-done(((f32[32,8,128]{2,1,0:T(8,128)}), f32[32,8,128]{2,1,0:T(8,128)S(1)}, u32[]{:S(2)}, u32[]{:S(2)}) %all-to-all-start.4) | async-done | bytes 131104 | tf_op jit(solution)/shard_map/all_to_all | solution.py:49
  224.8 1.8 multiply_subtract_fusion
  (155 shorter events, 31.0 us)
Async XLA Ops:
  7.2 43.8 %copy-start = (bf16[512,128]{1,0:T(8,128)(2,1)S(1)}, bf16[512,128]{1,0:T(8,128)(2,1)}, u32[]{:S(2)}) copy-start(bf16[512,128]{1,0:T(8,128)(2,1)} %param.11) | copy-start | bytes 393220
  7.2 7.9 %copy-start.17 = (f32[128,512]{1,0:T(8,128)S(1)}, f32[128,512]{1,0:T(8,128)}, u32[]{:S(2)}) copy-start(f32[128,512]{1,0:T(8,128)} %param.15) | copy-start | bytes 786436
  7.2 8.6 %copy-start.25 = (f32[8,512]{1,0:T(8,128)S(1)}, f32[8,512]{1,0:T(8,128)}, u32[]{:S(2)}) copy-start(f32[8,512]{1,0:T(8,128)} %param.12) | copy-start | bytes 49156
  7.2 72.4 %all-gather.2.cloned.1.call-start = ((), (), s32[]{:S(2)}) async-start(), calls=%async_computation.6 | async-start | bytes 1179648 | tf_op jit(solution)/shard_map/all_gather | solution.py:183
  9.9 9.4 %copy-start.6 = (bf16[512,512]{1,0:T(8,128)(2,1)S(1)}, bf16[512,512]{1,0:T(8,128)(2,1)}, u32[]{:S(2)}) copy-start(bf16[512,512]{1,0:T(8,128)(2,1)} %param.9) | copy-start | bytes 1572868
  9.9 9.4 %copy-start.16 = (bf16[512,128]{1,0:T(8,128)(2,1)S(1)}, bf16[512,128]{1,0:T(8,128)(2,1)}, u32[]{:S(2)}) copy-start(bf16[512,128]{1,0:T(8,128)(2,1)} %param.10) | copy-start | bytes 393220
  10.9 20.8 %collective-permute-start.1 = (bf16[384,1024]{1,0:T(8,128)(2,1)}, bf16[384,1024]{1,0:T(8,128)(2,1)}, u32[]{:S(2)}, u32[]{:S(2)}) collective-permute-start(bf16[384,1024]{1,0:T(8,128)(2,1)} %pad_maximum_fusion), channel_id=1, source_target_pairs={{0,64},{64,128},{128,192},{192,0},{1,65},{65,129},{129,193},{193,1... | collective-permute-start | bytes 2359304 | tf_op jit(solution)/shard_map/ppermute | solution.py:57
  13.4 19.3 %collective-permute-start.2 = (bf16[384,1024]{1,0:T(8,128)(2,1)}, bf16[384,1024]{1,0:T(8,128)(2,1)}, u32[]{:S(2)}, u32[]{:S(2)}) collective-permute-start(bf16[384,1024]{1,0:T(8,128)(2,1)} %pad_maximum_fusion.1), channel_id=1, source_target_pairs={{0,192},{64,0},{128,64},{192,128},{1,193},{65,1},{129,65},{193,129... | collective-permute-start | bytes 2359304 | tf_op jit(solution)/shard_map/ppermute | solution.py:57
  17.9 1.1 copy-start.21
  18.8 29.0 %copy-start.28 = (f32[8]{0:T(128)S(1)}, f32[8]{0:T(128)}, u32[]{:S(2)}) copy-start(f32[8]{0:T(128)} %param.13) | copy-start | bytes 100
  19.3 41.1 %copy-start.8 = (f32[512,512]{1,0:T(8,128)}, f32[512,512]{1,0:T(8,128)S(1)}, u32[]{:S(2)}) copy-start(f32[512,512]{1,0:T(8,128)S(1)} %copy.99) | copy-start | bytes 3145732
  21.0 50.2 %copy-start.22 = (f32[8,512]{1,0:T(8,128)S(1)}, f32[8,512]{1,0:T(8,128)}, u32[]{:S(2)}) copy-start(f32[8,512]{1,0:T(8,128)} %copy-done.21) | copy-start | bytes 49156
  32.7 27.7 %all-to-all-start = ((f32[32,24,128]{2,1,0:T(8,128)}), f32[32,24,128]{2,1,0:T(8,128)S(1)}, u32[]{:S(2)}, u32[]{:S(2)}) async-start(f32[32,24,128]{2,1,0:T(8,128)} %pad_maximum_fusion.6), calls=%async_computation | async-start | bytes 786432 | tf_op jit(solution)/shard_map/all_to_all | solution.py:49
  44.9 10.5 %collective-permute-start.3 = (bf16[128,1024]{1,0:T(8,128)(2,1)S(1)}, bf16[128,1024]{1,0:T(8,128)(2,1)S(1)}, u32[]{:S(2)}, u32[]{:S(2)}) collective-permute-start(bf16[128,1024]{1,0:T(8,128)(2,1)S(1)} %slice.75), channel_id=1, source_target_pairs={{0,64},{64,128},{128,192},{192,0},{1,65},{65,129},{129,193},{193,1... | collective-permute-start | bytes 786440 | tf_op jit(solution)/shard_map/ppermute | solution.py:57
  46.8 69.9 %collective-permute-start = (bf16[256,1024]{1,0:T(8,128)(2,1)S(1)}, bf16[256,1024]{1,0:T(8,128)(2,1)}, u32[]{:S(2)}, u32[]{:S(2)}) collective-permute-start(bf16[256,1024]{1,0:T(8,128)(2,1)S(1)} %get-tuple-element.40.own_in.refs_0_), channel_id=1, source_target_pairs={{0,1},{1,0},{2,3},{3,2},{4,5},{5,4},{6,7},{7,6},{8,9},{9,8},{10,11... | collective-permute-start | bytes 1572872 | tf_op jit(solution)/shard_map/ppermute | solution.py:53
  49.4 10.8 %collective-permute-start.4 = (bf16[128,1024]{1,0:T(8,128)(2,1)S(1)}, bf16[128,1024]{1,0:T(8,128)(2,1)S(1)}, u32[]{:S(2)}, u32[]{:S(2)}) collective-permute-start(bf16[128,1024]{1,0:T(8,128)(2,1)S(1)} %slice.76), channel_id=1, source_target_pairs={{0,192},{64,0},{128,64},{192,128},{1,193},{65,1},{129,65},{193,129... | collective-permute-start | bytes 786440 | tf_op jit(solution)/shard_map/ppermute | solution.py:57
  60.3 23.3 %collective-permute-start.5 = (bf16[256,1024]{1,0:T(8,128)(2,1)S(1)}, bf16[256,1024]{1,0:T(8,128)(2,1)S(1)}, u32[]{:S(2)}, u32[]{:S(2)}) collective-permute-start(bf16[256,1024]{1,0:T(8,128)(2,1)S(1)} %constant_dynamic-update-slice_fusion.own_in.refs_2_), channel_id=1, source_target_pairs={{0,1},{1,0},{2,3},{3,2},{4,5},{5,4},{6,7},{7,6},{8,9},{9,8},{10,11... | collective-permute-start | bytes 1572872 | tf_op jit(solution)/shard_map/ppermute | solution.py:53
  62.2 21.3 %all-to-all-start.1 = ((f32[32,16,128]{2,1,0:T(8,128)}), f32[32,16,128]{2,1,0:T(8,128)S(1)}, u32[]{:S(2)}, u32[]{:S(2)}) async-start(f32[32,16,128]{2,1,0:T(8,128)} %copy.101), calls=%async_computation.1 | async-start | bytes 524288 | tf_op jit(solution)/shard_map/all_to_all | solution.py:49
  71.2 4.2 %copy-start.23 = (f32[512,8]{0,1:T(8,128)S(1)}, f32[512,8]{0,1:T(8,128)}, u32[]{:S(2)}) copy-start(f32[512,8]{0,1:T(8,128)} %get-tuple-element.36) | copy-start | bytes 49156
  79.0 14.1 %collective-permute-start.7 = (bf16[256,1024]{1,0:T(8,128)(2,1)S(1)}, bf16[256,1024]{1,0:T(8,128)(2,1)}, u32[]{:S(2)}, u32[]{:S(2)}) collective-permute-start(bf16[256,1024]{1,0:T(8,128)(2,1)S(1)} %slice.78.own_in.refs_3_), channel_id=1, source_target_pairs={{0,1},{1,0},{2,3},{3,2},{4,5},{5,4},{6,7},{7,6},{8,9},{9,8},{10,11... | collective-permute-start | bytes 1572872 | tf_op jit(solution)/shard_map/ppermute | solution.py:53
  79.3 17.5 %collective-permute-start.9 = (bf16[256,1024]{1,0:T(8,128)(2,1)S(1)}, bf16[256,1024]{1,0:T(8,128)(2,1)}, u32[]{:S(2)}, u32[]{:S(2)}) collective-permute-start(bf16[256,1024]{1,0:T(8,128)(2,1)S(1)} %slice.81.own_in.refs_1_), channel_id=1, source_target_pairs={{0,1},{1,0},{2,3},{3,2},{4,5},{5,4},{6,7},{7,6},{8,9},{9,8},{10,11... | collective-permute-start | bytes 1572872 | tf_op jit(solution)/shard_map/ppermute | solution.py:53
  83.6 0.8 copy-start.3
  84.4 1.2 copy-start.1
  85.6 1.0 copy-start.4
  86.7 2.3 copy-start.10
  86.7 2.3 copy-start.13
  86.7 8.5 %copy-start.2 = (bf16[1024,512]{1,0:T(8,128)(2,1)S(1)}, bf16[1024,512]{1,0:T(8,128)(2,1)}, u32[]{:S(2)}) copy-start(bf16[1024,512]{1,0:T(8,128)(2,1)} %all-gather.2.cloned.1.call-done.weight_in) | copy-start | bytes 3145732
  87.8 11.7 %collective-permute-start.6 = (bf16[256,512]{1,0:T(8,128)(2,1)S(1)}, bf16[256,512]{1,0:T(8,128)(2,1)S(1)}, u32[]{:S(2)}, u32[]{:S(2)}) collective-permute-start(bf16[256,512]{1,0:T(8,128)(2,1)S(1)} %get-tuple-element.48), channel_id=1, source_target_pairs={{0,64},{64,128},{128,192},{192,0},{1,65},{65,129},{129,193},{193,1... | collective-permute-start | bytes 786440 | tf_op jit(solution)/shard_map/ppermute | solution.py:57
  91.9 28.3 %collective-permute-start.17 = (bf16[512,512]{1,0:T(8,128)(2,1)}, bf16[512,512]{1,0:T(8,128)(2,1)}, u32[]{:S(2)}, u32[]{:S(2)}) collective-permute-start(bf16[512,512]{1,0:T(8,128)(2,1)} %get-tuple-element.49.refs_8_), channel_id=1, source_target_pairs={{0,64},{64,128},{128,192},{192,0},{1,65},{65,129},{129,193},{193,1... | collective-permute-start | bytes 1572872 | tf_op jit(solution)/shard_map/ppermute | solution.py:57
  93.1 25.2 %collective-permute-start.19 = (bf16[512,512]{1,0:T(8,128)(2,1)}, bf16[512,512]{1,0:T(8,128)(2,1)}, u32[]{:S(2)}, u32[]{:S(2)}) collective-permute-start(bf16[512,512]{1,0:T(8,128)(2,1)} %get-tuple-element.49.refs_8_), channel_id=1, source_target_pairs={{0,192},{64,0},{128,64},{192,128},{1,193},{65,1},{129,65},{193,129... | collective-permute-start | bytes 1572872 | tf_op jit(solution)/shard_map/ppermute | solution.py:57
  96.8 13.3 %collective-permute-start.10 = (bf16[256,512]{1,0:T(8,128)(2,1)S(1)}, bf16[256,512]{1,0:T(8,128)(2,1)S(1)}, u32[]{:S(2)}, u32[]{:S(2)}) collective-permute-start(bf16[256,512]{1,0:T(8,128)(2,1)S(1)} %get-tuple-element.47), channel_id=1, source_target_pairs={{0,192},{64,0},{128,64},{192,128},{1,193},{65,1},{129,65},{193,129... | collective-permute-start | bytes 786440 | tf_op jit(solution)/shard_map/ppermute | solution.py:57
  100.4 23.3 %collective-permute-start.8 = (bf16[512,512]{1,0:T(8,128)(2,1)}, bf16[512,512]{1,0:T(8,128)(2,1)}, u32[]{:S(2)}, u32[]{:S(2)}) collective-permute-start(bf16[512,512]{1,0:T(8,128)(2,1)} %pad_maximum_fusion.2), channel_id=1, source_target_pairs={{0,64},{64,128},{128,192},{192,0},{1,65},{65,129},{129,193},{193,1... | collective-permute-start | bytes 1572872 | tf_op jit(solution)/shard_map/ppermute | solution.py:57
  111.0 13.8 %collective-permute-start.11 = (bf16[512,512]{1,0:T(8,128)(2,1)}, bf16[512,512]{1,0:T(8,128)(2,1)}, u32[]{:S(2)}, u32[]{:S(2)}) collective-permute-start(bf16[512,512]{1,0:T(8,128)(2,1)} %pad_maximum_fusion.3), channel_id=1, source_target_pairs={{0,192},{64,0},{128,64},{192,128},{1,193},{65,1},{129,65},{193,129... | collective-permute-start | bytes 1572872 | tf_op jit(solution)/shard_map/ppermute | solution.py:57
  118.3 9.8 %copy-start.19 = (bf16[512,512]{0,1:T(8,128)(2,1)S(1)}, bf16[512,512]{0,1:T(8,128)(2,1)}, u32[]{:S(2)}) copy-start(bf16[512,512]{0,1:T(8,128)(2,1)} %copy.102) | copy-start | bytes 1572868
  120.0 27.4 %collective-permute-start.20 = (bf16[256,512]{1,0:T(8,128)(2,1)}, bf16[256,512]{1,0:T(8,128)(2,1)}, u32[]{:S(2)}, u32[]{:S(2)}) collective-permute-start(bf16[256,512]{1,0:T(8,128)(2,1)} %slice.104), channel_id=1, source_target_pairs={{0,192},{64,0},{128,64},{192,128},{1,193},{65,1},{129,65},{193,129... | collective-permute-start | bytes 786440 | tf_op jit(solution)/shard_map/ppermute | solution.py:57
  121.9 25.5 %collective-permute-start.18 = (bf16[256,512]{1,0:T(8,128)(2,1)}, bf16[256,512]{1,0:T(8,128)(2,1)}, u32[]{:S(2)}, u32[]{:S(2)}) collective-permute-start(bf16[256,512]{1,0:T(8,128)(2,1)} %slice.103), channel_id=1, source_target_pairs={{0,64},{64,128},{128,192},{192,0},{1,65},{65,129},{129,193},{193,1... | collective-permute-start | bytes 786440 | tf_op jit(solution)/shard_map/ppermute | solution.py:57
  128.1 3.9 %copy-start.11 = (f32[512,512]{1,0:T(8,128)S(1)}, f32[512,512]{1,0:T(8,128)}, u32[]{:S(2)}) copy-start(f32[512,512]{1,0:T(8,128)} %copy.104) | copy-start | bytes 3145732
  132.0 16.5 %copy-start.5 = (bf16[256,1024]{1,0:T(8,128)(2,1)S(1)}, bf16[256,1024]{1,0:T(8,128)(2,1)}, u32[]{:S(2)}) copy-start(bf16[256,1024]{1,0:T(8,128)(2,1)} %copy-done.3) | copy-start | bytes 1572868
  133.7 24.7 %all-to-all-start.2 = ((f32[32,16,128]{2,1,0:T(8,128)}), f32[32,16,128]{2,1,0:T(8,128)}, u32[]{:S(2)}, u32[]{:S(2)}) async-start(f32[32,16,128]{2,1,0:T(8,128)} %bitcast.99), calls=%async_computation.2 | async-start | bytes 524288 | tf_op jit(solution)/shard_map/all_to_all | solution.py:49
  145.3 60.8 %reduce-scatter.2.cloned.1.call-start = ((), (), s32[]{:S(2)}) async-start(), calls=%async_computation.7 | async-start | bytes 1179648 | tf_op jit(solution)/shard_map/reduce_scatter | solution.py:245
  154.7 16.0 %copy-start.12 = (f32[512,512]{1,0:T(8,128)S(1)}, f32[512,512]{1,0:T(8,128)}, u32[]{:S(2)}) copy-start(f32[512,512]{1,0:T(8,128)} %copy.104) | copy-start | bytes 3145732
  158.4 25.3 %copy-start.7 = (bf16[512,512]{1,0:T(8,128)(2,1)S(1)}, bf16[512,512]{1,0:T(8,128)(2,1)}, u32[]{:S(2)}) copy-start(bf16[512,512]{1,0:T(8,128)(2,1)} %param.9) | copy-start | bytes 1572868
  158.4 25.3 %copy-start.9 = (f32[512,512]{1,0:T(8,128)S(1)}, f32[512,512]{1,0:T(8,128)}, u32[]{:S(2)}) copy-start(f32[512,512]{1,0:T(8,128)} %copy-done.8) | copy-start | bytes 3145732
  159.9 16.3 %copy-start.27 = (f32[512]{0:T(512)S(1)}, f32[512]{0:T(512)}, u32[]{:S(2)}) copy-start(f32[512]{0:T(512)} %get-tuple-element.34) | copy-start | bytes 6148
  160.8 22.9 %all-to-all-start.3 = ((f32[32,16,128]{2,1,0:T(8,128)}), f32[32,16,128]{2,1,0:T(8,128)}, u32[]{:S(2)}, u32[]{:S(2)}) async-start(f32[32,16,128]{2,1,0:T(8,128)} %copy.110), calls=%async_computation.3 | async-start | bytes 524288 | tf_op jit(solution)/shard_map/all_to_all | solution.py:49
  170.7 17.1 %copy-start.24 = (f32[512]{0:T(512)S(1)}, f32[512]{0:T(512)}, u32[]{:S(2)}) copy-start(f32[512]{0:T(512)} %mul.134) | copy-start | bytes 6148
  183.7 4.0 %copy-start.14 = (f32[512,512]{1,0:T(8,128)S(1)}, f32[512,512]{1,0:T(8,128)}, u32[]{:S(2)}) copy-start(f32[512,512]{1,0:T(8,128)} %get-tuple-element.50) | copy-start | bytes 3145732
  186.2 0.8 copy-start.15
  187.7 6.8 %collective-permute-start.12 = (f32[512,128]{1,0:T(8,128)}, f32[512,128]{1,0:T(8,128)}, u32[]{:S(2)}, u32[]{:S(2)}) collective-permute-start(f32[512,128]{1,0:T(8,128)} %constant_dynamic-slice_fusion), channel_id=1, source_target_pairs={{0,1},{1,0},{2,3},{3,2},{4,5},{5,4},{6,7},{7,6},{8,9},{9,8},{10,11... | collective-permute-start | bytes 786440 | tf_op jit(solution)/shard_map/ppermute | solution.py:53
  187.7 12.1 %copy-start.26 = (f32[512]{0:T(512)S(1)}, f32[512]{0:T(512)}, u32[]{:S(2)}) copy-start(f32[512]{0:T(512)} %mul.147) | copy-start | bytes 6148
  190.8 33.3 %copy-start.29 = (f32[8]{0:T(128)S(1)}, f32[8]{0:T(128)}, u32[]{:S(2)}) copy-start(f32[8]{0:T(128)} %param.17) | copy-start | bytes 100
  190.8 34.1 %copy-start.18 = (f32[128,512]{1,0:T(8,128)S(1)}, f32[128,512]{1,0:T(8,128)}, u32[]{:S(2)}) copy-start(f32[128,512]{1,0:T(8,128)} %param.15) | copy-start | bytes 786436
  190.8 34.1 %copy-start.20 = (f32[128,512]{1,0:T(8,128)S(1)}, f32[128,512]{1,0:T(8,128)}, u32[]{:S(2)}) copy-start(f32[128,512]{1,0:T(8,128)} %param.16) | copy-start | bytes 786436
  195.6 7.9 %collective-permute-start.14 = (bf16[512,128]{1,0:T(8,128)(2,1)S(1)}, bf16[512,128]{1,0:T(8,128)(2,1)S(1)}, u32[]{:S(2)}, u32[]{:S(2)}) collective-permute-start(bf16[512,128]{1,0:T(8,128)(2,1)S(1)} %add_convert_fusion.3), channel_id=1, source_target_pairs={{0,4},{2,6},{4,0},{6,2},{1,5},{3,7},{5,1},{7,3},{8,12},{10,14},{12... | collective-permute-start | bytes 393224 | tf_op jit(solution)/shard_map/ppermute | solution.py:271
  197.8 8.0 %collective-permute-start.15 = (bf16[512,128]{1,0:T(8,128)(2,1)S(1)}, bf16[512,128]{1,0:T(8,128)(2,1)S(1)}, u32[]{:S(2)}, u32[]{:S(2)}) collective-permute-start(bf16[512,128]{1,0:T(8,128)(2,1)S(1)} %add_convert_fusion.3), channel_id=1, source_target_pairs={{0,6},{2,0},{4,2},{6,4},{1,7},{3,1},{5,3},{7,5},{8,14},{10,8},{12,... | collective-permute-start | bytes 393224 | tf_op jit(solution)/shard_map/ppermute | solution.py:271
  199.2 6.7 %collective-permute-start.13 = (bf16[512,128]{1,0:T(8,128)(2,1)S(1)}, bf16[512,128]{1,0:T(8,128)(2,1)S(1)}, u32[]{:S(2)}, u32[]{:S(2)}) collective-permute-start(bf16[512,128]{1,0:T(8,128)(2,1)S(1)} %add_convert_fusion.3), channel_id=1, source_target_pairs={{0,2},{2,4},{4,6},{6,0},{1,3},{3,5},{5,7},{7,1},{8,10},{10,12},{12... | collective-permute-start | bytes 393224 | tf_op jit(solution)/shard_map/ppermute | solution.py:271
  206.0 7.2 %collective-permute-start.16 = (f32[512,128]{1,0:T(8,128)S(1)}, f32[512,128]{1,0:T(8,128)S(1)}, u32[]{:S(2)}, u32[]{:S(2)}) collective-permute-start(f32[512,128]{1,0:T(8,128)S(1)} %convert_add_fusion), channel_id=1, source_target_pairs={{0,1},{1,0},{2,3},{3,2},{4,5},{5,4},{6,7},{7,6},{8,9},{9,8},{10,11... | collective-permute-start | bytes 786440 | tf_op jit(solution)/shard_map/ppermute | solution.py:53
  208.1 15.4 %all-to-all-start.4 = ((f32[32,8,128]{2,1,0:T(8,128)}), f32[32,8,128]{2,1,0:T(8,128)S(1)}, u32[]{:S(2)}, u32[]{:S(2)}) async-start(f32[32,8,128]{2,1,0:T(8,128)} %broadcast_in_dim_broadcast_in_dim_broadcast_in_dim.2), calls=%async_computation.5 | async-start | bytes 262144 | tf_op jit(solution)/shard_map/all_to_all | solution.py:49
Sparse Core Ops, SparseCore 0:
  15.9 42.7 all-gather.1
  154.8 41.2 reduce-scatter.1

commit v6 on v5

--- a/solution.py
+++ b/solution.py
@@ -181,13 +181,11 @@
     quarter = WIDTH // 4
 
     weight_rows = lax.all_gather(out_master.astype(bf16), "z", axis=0, tiled=True)
-    def piece(step, start, rows):
+    owns = []
+    for step in range(4):
         to = lax.rem(ring + step, 4)
-        return lax.dynamic_slice(out_grad, (core * half + start, to * quarter), (rows, quarter))
-
-    near = half // 2
-    up = ring_shift(jnp.concatenate([piece(1, 0, half), piece(2, 0, near)]), 1)
-    down = ring_shift(jnp.concatenate([piece(3, 0, half), piece(2, near, near)]), 3)
+        piece = lax.dynamic_slice(out_grad, (core * half, to * quarter), (half, quarter))
+        owns.append(ring_shift(piece, step))
 
     running = jnp.cumsum(log_decay, axis=1)
     last_sum = running[:, -1:]
@@ -208,12 +206,11 @@
     packed = jnp.concatenate(
         [local_state.reshape(BLOCKS, 16, 128), totals.reshape(BLOCKS, 8, 128)], axis=1
     )
-    packed, up, down = lax.optimization_barrier((packed, up, down))
-    far = jnp.concatenate([ring_shift(up[half:], 1), ring_shift(down[half:], 3)])
-    owns = [piece(0, 0, half), up[:half], far, down[:half]]
     packed = swap(packed, CTX)
     weights = block_weights(packed[:, 16, 0])
-    start = swap(chain(weights, packed[:, :16], False), CTX).reshape(width, 128)
+    entering = chain(weights, packed[:, :16], False)
+    start = swap(entering, CTX).reshape(width, 128)
+    owns, _ = lax.optimization_barrier((owns, start))
     others = [swap_core(piece) for piece in owns]
     start, weight_rows = lax.optimization_barrier((start, weight_rows))
 
@@ -235,9 +232,7 @@
         ring_shift(jnp.concatenate([from_up.astype(bf16), part_down[half:]]), 1),
         ring_shift(jnp.concatenate([part_up[:half], from_down.astype(bf16)]), 3),
     ]
-    y_up, y_down = ring_shift(out_y, 1), ring_shift(out_y, 3)
-    y_far = jnp.concatenate([ring_shift(y_up[:half], 1), ring_shift(y_down[half:], 3)])
-    ring_y = [out_y, y_up, y_far, y_down]
+    ring_y = [ring_shift(out_y, step) for step in range(4)]
     parts, _ = lax.optimization_barrier((parts, out_y))
     grad_low = sum(part.astype(f32) for part in parts).astype(bf16)
 
@@ -261,11 +256,17 @@
         x_decayed.astype(bf16), end.astype(bf16), ((1,), (0,))
     )
 
+    skip_part = jnp.sum((grad * head_x).reshape(tokens, heads, head_width), axis=(0, 2))
+    square_part = jnp.sum((weight_grad * weight_grad).reshape(-1, heads, head_width), axis=(0, 2))
+    small = jnp.concatenate([skip_part, square_part, jnp.zeros((112,), f32)])
+
     both = jnp.concatenate([write_grad, read_grad], axis=0)
-    both, end = lax.optimization_barrier((both, end))
     keep = lax.dynamic_slice_in_dim(both, core * tokens, tokens, axis=0)
     give = lax.dynamic_slice_in_dim(both, (1 - core) * tokens, tokens, axis=0)
     mine = (keep + swap_core(give)).astype(bf16)
+    mine, end, small = lax.optimization_barrier((mine, end, small))
+    small = spread(jnp.broadcast_to(small[None], (8, 128)), CTX, BLOCKS)
+    small = jnp.sum(small, axis=0)[0]
     column = lax.axis_index("y")
     terms = [mine] + [
         lax.ppermute(mine, "y", [(i, (i + step) % 4) for i in range(4)]) for step in range(1, 4)
@@ -289,12 +290,6 @@
     above = jnp.sum(end_state * end.reshape(heads, -1), axis=1)
     decay_grad = local_tail + above[:, None]
 
-    skip_part = jnp.sum((grad * head_x).reshape(tokens, heads, head_width), axis=(0, 2))
-    square_part = jnp.sum((weight_grad * weight_grad).reshape(-1, heads, head_width), axis=(0, 2))
-    small = jnp.concatenate([skip_part, square_part, jnp.zeros((112,), f32)])
-    small = spread(jnp.broadcast_to(small[None], (8, 128)), CTX, BLOCKS)
-    small = jnp.sum(small, axis=0)[0]
-
     skip_total, square_total = small[:heads], small[heads : 2 * heads]
     mean_square = square_total / float(WIDTH * head_width)
     new_second = beta_two * squared_average + (1.0 - beta_two) * mean_square

time: 235 us -> 227 us (0.966)
  waiting for transfers between devices: 52.8 us -> 66.4 us
  starting transfers between devices: 69.5 us -> 56.2 us
  local copies, waits for them, and re-layouts: 32.2 us -> 28.3 us
  other arithmetic: 21.7 us -> 17.8 us
    all_to_all x5, starting transfers between devices: 46.1 us -> 35 us  [swap(): return lax.all_to_all(value, axes, 0, 0, tiled=True)]
    all_to_all x5, waiting for transfers between devices: 20.6 us -> 31.7 us  [swap(): return lax.all_to_all(value, axes, 0, 0, tiled=True)]
    slice x8 -> x2, local copies, waits for them, and re-layouts: 7.67 us -> 0.17 us  [the longest x2 2.15 us: shards(): owns = [piece(0, 0, half), up[:half], far, down[:half]]]
    ppermute x12 -> x10, waiting for transfers between devices: 27.6 us -> 34.7 us  [ring_shift(): lax.ppermute(value, 'x', [(i, (i + step) % 4) for i in range(4)])]
    ppermute x3, waiting for transfers between devices: 4.59 us -> 0.01 us  [shards(): lax.ppermute(mine, 'y', [(i, (i + step) % 4) for i in range(4)])]
    concatenate x3 -> x0, other arithmetic: 3 us -> none  [the longest x1 1.07 us: shards(): jnp.concatenate([ring_shift(y_up[:half], 1), ring_shift(y_down[half:], 3)])]
    dot_general x5, matrix products: 8.78 us -> 6.27 us  [mm(): return lax.dot_general(a, b, (dims, ((), ())), preferred_element_type=f32)]
    ppermute x12 -> x10, starting transfers between devices: 18.2 us -> 15.7 us  [ring_shift(): lax.ppermute(value, 'x', [(i, (i + step) % 4) for i in range(4)])]
  transfers between devices with their start and end apart: 28 -> 26, of which waited for: 11 -> 8; matrix products, arithmetic and copies ran while one was open for 32% -> 27% of each run, Pallas kernels for 5% -> 5%
where the time goes in v6:
time: 227 us; the launch traced here: 225 us
  waiting for transfers between devices  66.4 us (29%)
  starting transfers between devices  56.2 us (25%)
  matrix products  29.8 us (13%)
  local copies, waits for them, and re-layouts  28.3 us (12%)
  other arithmetic  17.8 us (8%)
  between operations  14.6 us (6%)
  Pallas kernels  12.1 us (5%)
    all_to_all x5, starting transfers between devices, swap(): return lax.all_to_all(value, axes, 0, 0, tiled=True)  35 us
    ppermute x10, waiting for transfers between devices, ring_shift(): lax.ppermute(value, 'x', [(i, (i + step) % 4) for i in range(4)])  34.7 us
    all_to_all x5, waiting for transfers between devices, swap(): return lax.all_to_all(value, axes, 0, 0, tiled=True)  31.7 us
    ppermute x10, starting transfers between devices, ring_shift(): lax.ppermute(value, 'x', [(i, (i + step) % 4) for i in range(4)])  15.7 us
    dot_general x6, matrix products, exact(): lax.dot_general(a.astype(f32), b.astype(f32), (dims, ((), ())), precision...  12.5 us
    unnamed x69, local copies, waits for them, and re-layouts  6.28 us
    dot_general x5, matrix products, mm(): return lax.dot_general(a, b, (dims, ((), ())), preferred_element_type=f32)  6.27 us
    pallas_call x1, Pallas kernels, weight_grad_part(): pl.pallas_call(weight_grad_kernel, out_shape=jax.ShapeDtypeStruct((quarte...  6.25 us
  transfers between devices with their start and end apart: 26, of which 8 were waited for; matrix products, arithmetic and copies ran while one was open for 27% of the time, Pallas kernels for 5%

profile of v6, /device:TPU:8, one launch (start us, length us, event | category | flops | bytes accessed | tf_op | source)
XLA Modules:
  0.0 225.3 jit_solution(4553560090854895776)
XLA Ops:
  7.2 2.3 %reduce-window.14 = f32[8,4,128]{2,0,1:T(8,128)S(1)} reduce-window(f32[8,4,128]{2,0,1:T(8,128)} %bitcast.112, f32[]{:T(128)} %constant.71.clone.1), window={size=1x1x128 pad=0_0x0_0x127_0}, to_apply=%region_0.0 | reduce-window | flops 520192 | bytes 32772 | tf_op jit(solution)/shard_map/reduce-window
  11.8 2.4 %fusion.13 = f32[512,128]{1,0:T(8,128)S(1)} fusion(bf16[512,128]{1,0:T(8,128)(2,1)} %param.10, f32[512,512]{1,0:T(8,128)S(1)} %copy.99, bf16[512,512]{1,0:T(8,128)(2,1)} %param.9), kind=kOutput, calls=%fused_computation.32 | convolution fusion | flops 403177472 | bytes 1966080 | tf_op jit(solution)/shard_map/dot_general | solution.py:39
  15.1 11.3 %all-to-all-start = ((f32[32,24,128]{2,1,0:T(8,128)}), f32[32,24,128]{2,1,0:T(8,128)S(1)}, u32[]{:S(2)}, u32[]{:S(2)}) async-start(f32[32,24,128]{2,1,0:T(8,128)} %pad_maximum_fusion.2), calls=%async_computation | async-start | bytes 786432 | tf_op jit(solution)/shard_map/all_to_all | solution.py:49
  27.2 2.7 %fusion.46 = (bf16[256,1024]{1,0:T(8,128)(2,1)}, bf16[256,1024]{1,0:T(8,128)(2,1)}, bf16[256,1024]{1,0:T(8,128)(2,1)S(1)}, bf16[256,1024]{1,0:T(8,128)(2,1)}) fusion(bf16[512,4096]{1,0:T(8,128)(2,1)} %param.14, s32[]{:T(128)S(6)} %select_n.156, s32[]{:T(128)S(6)} %select_n.160, s32[]{:T(128)S(6)} %select_n.158, s32[]{:T(128)S(6)} %select_n.157, s32[]{:T(128)S(6)} %select_n.159), kind=kLoop, calls=%fused_computation.97 | loop fusion | bytes 4194324 | tf_op jit(solution)/shard_map/dynamic_slice | solution.py:187
  29.9 1.8 collective-permute-start
  31.7 2.7 %collective-permute-start.1 = (bf16[256,1024]{1,0:T(8,128)(2,1)}, bf16[256,1024]{1,0:T(8,128)(2,1)S(1)}, u32[]{:S(2)}, u32[]{:S(2)}) collective-permute-start(bf16[256,1024]{1,0:T(8,128)(2,1)} %get-tuple-element.45), channel_id=1, source_target_pairs={{0,128},{64,192},{128,0},{192,64},{1,129},{65,193},{129,1},{193,65... | collective-permute-start | bytes 1572872 | tf_op jit(solution)/shard_map/ppermute | solution.py:57
  34.4 1.4 collective-permute-start.2
  35.9 5.1 %all-to-all-done = f32[32,24,128]{2,1,0:T(8,128)S(1)} async-done(((f32[32,24,128]{2,1,0:T(8,128)}), f32[32,24,128]{2,1,0:T(8,128)S(1)}, u32[]{:S(2)}, u32[]{:S(2)}) %all-to-all-start) | async-done | bytes 393248 | tf_op jit(solution)/shard_map/all_to_all | solution.py:49
  41.9 0.9 copy.101
  42.8 5.2 %all-to-all-start.1 = ((f32[32,16,128]{2,1,0:T(8,128)}), f32[32,16,128]{2,1,0:T(8,128)S(1)}, u32[]{:S(2)}, u32[]{:S(2)}) async-start(f32[32,16,128]{2,1,0:T(8,128)} %copy.101), calls=%async_computation.1 | async-start | bytes 524288 | tf_op jit(solution)/shard_map/all_to_all | solution.py:49
  48.1 1.0 copy.102
  50.5 1.3 fusion.48
  51.7 10.6 %collective-permute-done.1.own_in.refs_2_ = bf16[256,1024]{1,0:T(8,128)(2,1)S(1)} collective-permute-done((bf16[256,1024]{1,0:T(8,128)(2,1)}, bf16[256,1024]{1,0:T(8,128)(2,1)S(1)}, u32[]{:S(2)}, u32[]{:S(2)}) %collective-permute-start.1) | collective-permute-done | bytes 524320 | tf_op jit(solution)/shard_map/ppermute | solution.py:57
  62.5 4.5 %fusion.1 = f32[8,512,64]{1,2,0:T(8,128)} fusion(bf16[512,8,64]{0,2,1:T(8,128)(2,1)} %bitcast.106, f32[512,512]{1,0:T(8,128)} %fusion.48, f32[8,512]{1,0:T(8,128)} %copy-done.28), kind=kOutput, calls=%fused_computation.5 | convolution fusion | flops 278921216 | bytes 2637824 | tf_op jit(solution)/shard_map/hts,shp->thp/dot_general | solution.py:220
  67.0 2.5 %copy.105 = f32[512,512]{1,0:T(8,128)} copy(f32[512,512]{0,1:T(8,128)} %bitcast.104) | data formatting | bytes 2097152 | tf_op jit(solution)/shard_map/reshape | solution.py:221
  69.6 1.1 broadcast_in_dim.65
  70.7 2.6 %copy.104 = f32[512,512]{1,0:T(8,128)} copy(f32[512,512]{0,1:T(8,128)} %bitcast.101) | data formatting | bytes 2097152 | tf_op jit(solution)/shard_map/reshape | solution.py:199
  74.2 0.8 copy-done.5
  75.0 1.2 copy-done.1
  76.2 1.0 copy-done.6
  77.3 1.0 ring_grad.5
  78.4 1.7 collective-permute-start.5
  80.0 3.0 %fusion.7 = (bf16[512,512]{1,0:T(8,128)(2,1)}, f32[512,512]{1,0:T(8,128)}) fusion(bf16[512,512]{1,0:T(8,128)(2,1)} %param.9, f32[512]{0:T(512)} %mul.132, f32[512,512]{1,0:T(8,128)S(1)} %copy-done.16, f32[512,512]{1,0:T(8,128)S(1)} %copy-done.12, f32[512,128]{1,0:T(8,128)S(1)} %bitcast.94, bf16[512,128]{1,0:T(8,128)(2,1)S(1)} %copy-done), kind=kOutput, calls=%fused_computation.22 | convolution fusion | flops 404226048 | bytes 4589568 | tf_op jit(solution)/shard_map/dot_general | solution.py:39
  83.5 2.8 %collective-permute-start.13 = (bf16[512,512]{1,0:T(8,128)(2,1)}, bf16[512,512]{1,0:T(8,128)(2,1)}, u32[]{:S(2)}, u32[]{:S(2)}) collective-permute-start(bf16[512,512]{1,0:T(8,128)(2,1)} %get-tuple-element.52.refs_8_), channel_id=1, source_target_pairs={{0,128},{64,192},{128,0},{192,64},{1,129},{65,193},{129,1},{193,65... | collective-permute-start | bytes 1572872 | tf_op jit(solution)/shard_map/ppermute | solution.py:57
  86.3 1.6 ring_grad.6
  88.0 1.5 collective-permute-start.14
  89.4 1.6 ring_grad.7
  91.3 0.9 pad_maximum_fusion
  92.1 23.4 %collective-permute-done.9 = bf16[256,512]{1,0:T(8,128)(2,1)S(1)} collective-permute-done((bf16[256,512]{1,0:T(8,128)(2,1)S(1)}, bf16[256,512]{1,0:T(8,128)(2,1)S(1)}, u32[]{:S(2)}, u32[]{:S(2)}) %collective-permute-start.9) | collective-permute-done | bytes 262176 | tf_op jit(solution)/shard_map/ppermute | solution.py:57
  115.5 1.4 collective-permute-start.7
  117.0 0.8 pad_maximum_fusion.1
  117.8 1.9 collective-permute-start.10
  121.0 1.6 ring_grad.4
  122.6 1.0 copy-done.4
  123.7 1.0 copy-done.7
  124.7 6.2 %weight_grad.1 = bf16[1024,512]{1,0:T(8,128)(2,1)} custom-call(s32[1]{0:T(128)} %bitcast.core_ref, bf16[256,1024]{1,0:T(8,128)(2,1)S(1)} %get-tuple-element.20.own_in.refs_0_, bf16[256,1024]{1,0:T(8,128)(2,1)S(1)} %collective-permute-done.own_in.refs_1_, bf16[256,1024]{1,0:T(8,128)(2,1)S(1)} %collective-permute-done.1.own_in.refs_2_, ...), custom_call_target="tpu_custom_call" | custom-call | flops 2147483648 | bytes 8388608 | tf_op jit(solution)/shard_map/weight_grad/pallas_call | solution.py:143
  131.7 2.2 fusion.9
  134.2 1.7 fusion.15
  135.9 8.5 %all-to-all-start.2 = ((f32[32,16,128]{2,1,0:T(8,128)}), f32[32,16,128]{2,1,0:T(8,128)}, u32[]{:S(2)}, u32[]{:S(2)}) async-start(f32[32,16,128]{2,1,0:T(8,128)} %bitcast.19), calls=%async_computation.2 | async-start | bytes 524288 | tf_op jit(solution)/shard_map/all_to_all | solution.py:49
  144.4 2.8 %multiply_reduce_fusion = bf16[512,512]{1,0:T(8,128)(2,1)S(1)} fusion(f32[8,512]{1,0:T(8,128)} %copy-done.28, bf16[512,8,64]{0,2,1:T(8,128)(2,1)S(1)} %bitcast.108, bf16[512,8,64]{0,2,1:T(8,128)(2,1)S(1)} %bitcast.107), kind=kOutput, calls=%fused_computation | convolution fusion | flops 278659072 | bytes 1589248 | tf_op jit(solution)/shard_map/thp,shp->hts/dot_general | solution.py:250
  147.3 1.0 fusion.50
  148.3 9.8 %all-to-all-done.2 = f32[32,16,128]{2,1,0:T(8,128)} async-done(((f32[32,16,128]{2,1,0:T(8,128)}), f32[32,16,128]{2,1,0:T(8,128)}, u32[]{:S(2)}, u32[]{:S(2)}) %all-to-all-start.2) | async-done | bytes 262176 | tf_op jit(solution)/shard_map/all_to_all | solution.py:49
  158.1 1.4 fusion.25
  159.5 0.9 copy.110
  160.4 5.5 %all-to-all-start.3 = ((f32[32,16,128]{2,1,0:T(8,128)}), f32[32,16,128]{2,1,0:T(8,128)S(1)}, u32[]{:S(2)}, u32[]{:S(2)}) async-start(f32[32,16,128]{2,1,0:T(8,128)} %copy.110), calls=%async_computation.3 | async-start | bytes 524288 | tf_op jit(solution)/shard_map/all_to_all | solution.py:49
  165.9 1.4 fusion.49
  167.2 1.3 convolution_add_fusion
  168.6 8.2 %all-to-all-done.3 = f32[32,16,128]{2,1,0:T(8,128)S(1)} async-done(((f32[32,16,128]{2,1,0:T(8,128)}), f32[32,16,128]{2,1,0:T(8,128)S(1)}, u32[]{:S(2)}, u32[]{:S(2)}) %all-to-all-start.3) | async-done | bytes 262176 | tf_op jit(solution)/shard_map/all_to_all | solution.py:49
  176.8 1.2 convolution_add_fusion.1
  178.0 0.9 fusion.21
  178.9 3.7 %fusion = f32[8,64,512]{2,1,0:T(8,128)} fusion(bf16[512,8,64]{0,2,1:T(8,128)(2,1)} %bitcast.109, f32[512,512]{1,0:T(8,128)} %fusion.48, f32[8,512]{1,0:T(8,128)S(1)} %copy-done.29), kind=kOutput, calls=%fused_computation.4 | convolution fusion | flops 278921216 | bytes 2637824 | tf_op jit(solution)/shard_map/hst,shp->thp/dot_general | solution.py:249
  182.6 2.6 %copy.113 = f32[512,512]{1,0:T(8,128)} copy(f32[512,512]{0,1:T(8,128)} %bitcast.103) | data formatting | bytes 2097152 | tf_op jit(solution)/shard_map/reshape | solution.py:281
  185.4 1.1 fusion.24
  186.5 1.0 fusion.19
  187.8 2.4 %collective-permute-start.16 = (bf16[512,128]{1,0:T(8,128)(2,1)S(1)}, bf16[512,128]{1,0:T(8,128)(2,1)S(1)}, u32[]{:S(2)}, u32[]{:S(2)}) collective-permute-start(bf16[512,128]{1,0:T(8,128)(2,1)S(1)} %fusion.24), channel_id=1, source_target_pairs={{0,4},{2,6},{4,0},{6,2},{1,5},{3,7},{5,1},{7,3},{8,12},{10,14},{12... | collective-permute-start | bytes 393224 | tf_op jit(solution)/shard_map/ppermute | solution.py:272
  190.2 1.4 collective-permute-start.17
  192.2 3.6 %fusion.8 = (f32[512,512]{1,0:T(8,128)}, bf16[512,512]{1,0:T(8,128)(2,1)}) fusion(bf16[512,512]{1,0:T(8,128)(2,1)S(1)} %copy-done.9, f32[512,512]{1,0:T(8,128)} %get-tuple-element.53, bf16[512,512]{1,0:T(8,128)(2,1)S(1)} %copy-done.15, f32[512]{0:T(512)} %mul.132, f32[512,512]{1,0:T(8,128)} %copy.113, f32[512,512]{1,0:T(8,128)S(1)} %copy-done.11, ...), kind=kOutput, calls=%fused_computation.23 | convolution fusion | flops 405274624 | bytes 6162432 | tf_op jit(solution)/shard_map/dot_general | solution.py:39
  195.8 1.6 copy.114
  197.9 1.1 reduce-window.16
  200.7 4.5 %all-to-all-start.4 = ((f32[32,8,128]{2,1,0:T(8,128)}), f32[32,8,128]{2,1,0:T(8,128)S(1)}, u32[]{:S(2)}, u32[]{:S(2)}) async-start(f32[32,8,128]{2,1,0:T(8,128)} %broadcast_in_dim_broadcast_in_dim_broadcast_in_dim.2), calls=%async_computation.5 | async-start | bytes 262144 | tf_op jit(solution)/shard_map/all_to_all | solution.py:49
  205.8 1.0 convert_add_fusion
  207.0 8.5 %all-to-all-done.4 = f32[32,8,128]{2,1,0:T(8,128)S(1)} async-done(((f32[32,8,128]{2,1,0:T(8,128)}), f32[32,8,128]{2,1,0:T(8,128)S(1)}, u32[]{:S(2)}, u32[]{:S(2)}) %all-to-all-start.4) | async-done | bytes 131104 | tf_op jit(solution)/shard_map/all_to_all | solution.py:49
  216.7 0.9 multiply_subtract_fusion
  217.6 0.8 broadcast_select_fusion
  (146 shorter events, 15.7 us)
Async XLA Ops:
  7.2 43.3 %copy-start = (bf16[512,128]{1,0:T(8,128)(2,1)S(1)}, bf16[512,128]{1,0:T(8,128)(2,1)}, u32[]{:S(2)}) copy-start(bf16[512,128]{1,0:T(8,128)(2,1)} %param.11) | copy-start | bytes 393220
  7.2 19.3 %copy-start.22 = (f32[128,512]{1,0:T(8,128)S(1)}, f32[128,512]{1,0:T(8,128)}, u32[]{:S(2)}) copy-start(f32[128,512]{1,0:T(8,128)} %param.15) | copy-start | bytes 786436
  10.3 1.1 copy-start.28
  11.8 15.5 %copy-start.10 = (f32[512,512]{1,0:T(8,128)}, f32[512,512]{1,0:T(8,128)S(1)}, u32[]{:S(2)}) copy-start(f32[512,512]{1,0:T(8,128)S(1)} %copy.99) | copy-start | bytes 3145732
  14.2 17.5 %copy-start.17 = (f32[512,128]{1,0:T(8,128)}, f32[512,128]{1,0:T(8,128)S(1)}, u32[]{:S(2)}) copy-start(f32[512,128]{1,0:T(8,128)S(1)} %fusion.13) | copy-start | bytes 786436
  14.3 33.7 %copy-start.8 = (bf16[512,512]{1,0:T(8,128)(2,1)S(1)}, bf16[512,512]{1,0:T(8,128)(2,1)}, u32[]{:S(2)}) copy-start(bf16[512,512]{1,0:T(8,128)(2,1)} %param.9) | copy-start | bytes 1572868
  15.1 25.9 %all-to-all-start = ((f32[32,24,128]{2,1,0:T(8,128)}), f32[32,24,128]{2,1,0:T(8,128)S(1)}, u32[]{:S(2)}, u32[]{:S(2)}) async-start(f32[32,24,128]{2,1,0:T(8,128)} %pad_maximum_fusion.2), calls=%async_computation | async-start | bytes 786432 | tf_op jit(solution)/shard_map/all_to_all | solution.py:49
  26.4 24.0 %copy-start.20 = (bf16[512,128]{1,0:T(8,128)(2,1)S(1)}, bf16[512,128]{1,0:T(8,128)(2,1)}, u32[]{:S(2)}) copy-start(bf16[512,128]{1,0:T(8,128)(2,1)} %param.10) | copy-start | bytes 393220
  26.4 47.7 %all-gather.2.cloned.1.call-start = ((), (), s32[]{:S(2)}) async-start(), calls=%async_computation.6 | async-start | bytes 1179648 | tf_op jit(solution)/shard_map/all_gather | solution.py:183
  29.9 21.8 %collective-permute-start = (bf16[256,1024]{1,0:T(8,128)(2,1)}, bf16[256,1024]{1,0:T(8,128)(2,1)S(1)}, u32[]{:S(2)}, u32[]{:S(2)}) collective-permute-start(bf16[256,1024]{1,0:T(8,128)(2,1)} %get-tuple-element.43), channel_id=1, source_target_pairs={{0,64},{64,128},{128,192},{192,0},{1,65},{65,129},{129,193},{193,1... | collective-permute-start | bytes 1572872 | tf_op jit(solution)/shard_map/ppermute | solution.py:57
  31.7 30.6 %collective-permute-start.1 = (bf16[256,1024]{1,0:T(8,128)(2,1)}, bf16[256,1024]{1,0:T(8,128)(2,1)S(1)}, u32[]{:S(2)}, u32[]{:S(2)}) collective-permute-start(bf16[256,1024]{1,0:T(8,128)(2,1)} %get-tuple-element.45), channel_id=1, source_target_pairs={{0,128},{64,192},{128,0},{192,64},{1,129},{65,193},{129,1},{193,65... | collective-permute-start | bytes 1572872 | tf_op jit(solution)/shard_map/ppermute | solution.py:57
  34.4 27.9 %collective-permute-start.2 = (bf16[256,1024]{1,0:T(8,128)(2,1)}, bf16[256,1024]{1,0:T(8,128)(2,1)S(1)}, u32[]{:S(2)}, u32[]{:S(2)}) collective-permute-start(bf16[256,1024]{1,0:T(8,128)(2,1)} %get-tuple-element.42), channel_id=1, source_target_pairs={{0,192},{64,0},{128,64},{192,128},{1,193},{65,1},{129,65},{193,129... | collective-permute-start | bytes 1572872 | tf_op jit(solution)/shard_map/ppermute | solution.py:57
  42.8 19.7 %all-to-all-start.1 = ((f32[32,16,128]{2,1,0:T(8,128)}), f32[32,16,128]{2,1,0:T(8,128)S(1)}, u32[]{:S(2)}, u32[]{:S(2)}) async-start(f32[32,16,128]{2,1,0:T(8,128)} %copy.101), calls=%async_computation.1 | async-start | bytes 524288 | tf_op jit(solution)/shard_map/all_to_all | solution.py:49
  48.0 138.5 %reduce-scatter.2.cloned.1.call-start = ((), (), s32[]{:S(2)}) async-start(), calls=%async_computation.7 | async-start | bytes 1179648 | tf_op jit(solution)/shard_map/reduce_scatter | solution.py:240
  62.4 24.0 %copy-start.3 = (bf16[256,1024]{1,0:T(8,128)(2,1)}, bf16[256,1024]{1,0:T(8,128)(2,1)S(1)}, u32[]{:S(2)}) copy-start(bf16[256,1024]{1,0:T(8,128)(2,1)S(1)} %collective-permute-done.2.own_in.refs_3_) | copy-start | bytes 1572868
  62.5 11.7 %collective-permute-start.4 = (bf16[256,1024]{1,0:T(8,128)(2,1)S(1)}, bf16[256,1024]{1,0:T(8,128)(2,1)S(1)}, u32[]{:S(2)}, u32[]{:S(2)}) collective-permute-start(bf16[256,1024]{1,0:T(8,128)(2,1)S(1)} %collective-permute-done.1.own_in.refs_2_), channel_id=1, source_target_pairs={{0,1},{1,0},{2,3},{3,2},{4,5},{5,4},{6,7},{7,6},{8,9},{9,8},{10,11... | collective-permute-start | bytes 1572872 | tf_op jit(solution)/shard_map/ppermute | solution.py:53
  62.5 7.0 %copy-start.30 = (f32[512,8]{0,1:T(8,128)S(1)}, f32[512,8]{0,1:T(8,128)}, u32[]{:S(2)}) copy-start(f32[512,8]{0,1:T(8,128)} %get-tuple-element.40) | copy-start | bytes 49156
  73.2 44.6 %collective-permute-start.3 = (bf16[256,1024]{1,0:T(8,128)(2,1)S(1)}, bf16[256,1024]{1,0:T(8,128)(2,1)}, u32[]{:S(2)}, u32[]{:S(2)}) collective-permute-start(bf16[256,1024]{1,0:T(8,128)(2,1)S(1)} %get-tuple-element.20.own_in.refs_0_), channel_id=1, source_target_pairs={{0,1},{1,0},{2,3},{3,2},{4,5},{5,4},{6,7},{7,6},{8,9},{9,8},{10,11... | collective-permute-start | bytes 1572872 | tf_op jit(solution)/shard_map/ppermute | solution.py:53
  73.7 9.9 %collective-permute-start.6 = (bf16[256,1024]{1,0:T(8,128)(2,1)S(1)}, bf16[256,1024]{1,0:T(8,128)(2,1)}, u32[]{:S(2)}, u32[]{:S(2)}) collective-permute-start(bf16[256,1024]{1,0:T(8,128)(2,1)S(1)} %collective-permute-done.2.own_in.refs_3_), channel_id=1, source_target_pairs={{0,1},{1,0},{2,3},{3,2},{4,5},{5,4},{6,7},{7,6},{8,9},{9,8},{10,11... | collective-permute-start | bytes 1572872 | tf_op jit(solution)/shard_map/ppermute | solution.py:53
  73.8 14.2 %collective-permute-start.8 = (bf16[256,1024]{1,0:T(8,128)(2,1)S(1)}, bf16[256,1024]{1,0:T(8,128)(2,1)}, u32[]{:S(2)}, u32[]{:S(2)}) collective-permute-start(bf16[256,1024]{1,0:T(8,128)(2,1)S(1)} %collective-permute-done.own_in.refs_1_), channel_id=1, source_target_pairs={{0,1},{1,0},{2,3},{3,2},{4,5},{5,4},{6,7},{7,6},{8,9},{9,8},{10,11... | collective-permute-start | bytes 1572872 | tf_op jit(solution)/shard_map/ppermute | solution.py:53
  74.2 0.8 copy-start.5
  75.0 1.2 copy-start.1
  76.2 1.0 copy-start.6
  77.2 2.8 %copy-start.12 = (f32[512,512]{1,0:T(8,128)S(1)}, f32[512,512]{1,0:T(8,128)}, u32[]{:S(2)}) copy-start(f32[512,512]{1,0:T(8,128)} %copy.104) | copy-start | bytes 3145732
  77.3 2.8 %copy-start.16 = (f32[512,512]{1,0:T(8,128)S(1)}, f32[512,512]{1,0:T(8,128)}, u32[]{:S(2)}) copy-start(f32[512,512]{1,0:T(8,128)} %copy.105) | copy-start | bytes 3145732
  77.3 9.1 %copy-start.2 = (bf16[1024,512]{1,0:T(8,128)(2,1)S(1)}, bf16[1024,512]{1,0:T(8,128)(2,1)}, u32[]{:S(2)}) copy-start(bf16[1024,512]{1,0:T(8,128)(2,1)} %all-gather.2.cloned.1.call-done.weight_in) | copy-start | bytes 3145732
  78.4 12.7 %collective-permute-start.5 = (bf16[256,512]{1,0:T(8,128)(2,1)S(1)}, bf16[256,512]{1,0:T(8,128)(2,1)S(1)}, u32[]{:S(2)}, u32[]{:S(2)}) collective-permute-start(bf16[256,512]{1,0:T(8,128)(2,1)S(1)} %get-tuple-element.51), channel_id=1, source_target_pairs={{0,64},{64,128},{128,192},{192,0},{1,65},{65,129},{129,193},{193,1... | collective-permute-start | bytes 786440 | tf_op jit(solution)/shard_map/ppermute | solution.py:57
  83.0 39.6 %collective-permute-start.12 = (bf16[512,512]{1,0:T(8,128)(2,1)}, bf16[512,512]{1,0:T(8,128)(2,1)}, u32[]{:S(2)}, u32[]{:S(2)}) collective-permute-start(bf16[512,512]{1,0:T(8,128)(2,1)} %get-tuple-element.52.refs_8_), channel_id=1, source_target_pairs={{0,64},{64,128},{128,192},{192,0},{1,65},{65,129},{129,193},{193,1... | collective-permute-start | bytes 1572872 | tf_op jit(solution)/shard_map/ppermute | solution.py:57
  83.5 39.1 %collective-permute-start.13 = (bf16[512,512]{1,0:T(8,128)(2,1)}, bf16[512,512]{1,0:T(8,128)(2,1)}, u32[]{:S(2)}, u32[]{:S(2)}) collective-permute-start(bf16[512,512]{1,0:T(8,128)(2,1)} %get-tuple-element.52.refs_8_), channel_id=1, source_target_pairs={{0,128},{64,192},{128,0},{192,64},{1,129},{65,193},{129,1},{193,65... | collective-permute-start | bytes 1572872 | tf_op jit(solution)/shard_map/ppermute | solution.py:57
  88.0 34.6 %collective-permute-start.14 = (bf16[512,512]{1,0:T(8,128)(2,1)}, bf16[512,512]{1,0:T(8,128)(2,1)}, u32[]{:S(2)}, u32[]{:S(2)}) collective-permute-start(bf16[512,512]{1,0:T(8,128)(2,1)} %get-tuple-element.52.refs_8_), channel_id=1, source_target_pairs={{0,192},{64,0},{128,64},{192,128},{1,193},{65,1},{129,65},{193,129... | collective-permute-start | bytes 1572872 | tf_op jit(solution)/shard_map/ppermute | solution.py:57
  91.1 24.4 %collective-permute-start.9 = (bf16[256,512]{1,0:T(8,128)(2,1)S(1)}, bf16[256,512]{1,0:T(8,128)(2,1)S(1)}, u32[]{:S(2)}, u32[]{:S(2)}) collective-permute-start(bf16[256,512]{1,0:T(8,128)(2,1)S(1)} %get-tuple-element.50), channel_id=1, source_target_pairs={{0,192},{64,0},{128,64},{192,128},{1,193},{65,1},{129,65},{193,129... | collective-permute-start | bytes 786440 | tf_op jit(solution)/shard_map/ppermute | solution.py:57
  115.5 15.5 %collective-permute-start.7 = (bf16[512,512]{1,0:T(8,128)(2,1)}, bf16[512,512]{1,0:T(8,128)(2,1)}, u32[]{:S(2)}, u32[]{:S(2)}) collective-permute-start(bf16[512,512]{1,0:T(8,128)(2,1)} %pad_maximum_fusion), channel_id=1, source_target_pairs={{0,64},{64,128},{128,192},{192,0},{1,65},{65,129},{129,193},{193,1... | collective-permute-start | bytes 1572872 | tf_op jit(solution)/shard_map/ppermute | solution.py:57
  117.8 13.9 %collective-permute-start.10 = (bf16[512,512]{1,0:T(8,128)(2,1)}, bf16[512,512]{1,0:T(8,128)(2,1)}, u32[]{:S(2)}, u32[]{:S(2)}) collective-permute-start(bf16[512,512]{1,0:T(8,128)(2,1)} %pad_maximum_fusion.1), channel_id=1, source_target_pairs={{0,192},{64,0},{128,64},{192,128},{1,193},{65,1},{129,65},{193,129... | collective-permute-start | bytes 1572872 | tf_op jit(solution)/shard_map/ppermute | solution.py:57
  122.6 1.0 copy-start.4
  123.7 1.0 copy-start.7
  131.0 3.2 %copy-start.13 = (f32[512,512]{1,0:T(8,128)S(1)}, f32[512,512]{1,0:T(8,128)}, u32[]{:S(2)}) copy-start(f32[512,512]{1,0:T(8,128)} %copy.104) | copy-start | bytes 3145732
  131.0 13.4 %copy-start.25 = (bf16[512,512]{0,1:T(8,128)(2,1)S(1)}, bf16[512,512]{0,1:T(8,128)(2,1)}, u32[]{:S(2)}) copy-start(bf16[512,512]{0,1:T(8,128)(2,1)} %copy.102) | copy-start | bytes 1572868
  133.9 10.5 %copy-start.14 = (bf16[512,512]{1,0:T(8,128)(2,1)}, bf16[512,512]{1,0:T(8,128)(2,1)S(1)}, u32[]{:S(2)}) copy-start(bf16[512,512]{1,0:T(8,128)(2,1)S(1)} %get-tuple-element.39) | copy-start | bytes 1572868
  134.1 10.3 %copy-start.26 = (bf16[512,512]{0,1:T(8,128)(2,1)}, bf16[512,512]{0,1:T(8,128)(2,1)S(1)}, u32[]{:S(2)}) copy-start(bf16[512,512]{0,1:T(8,128)(2,1)S(1)} %copy.106) | copy-start | bytes 1572868
  135.9 22.3 %all-to-all-start.2 = ((f32[32,16,128]{2,1,0:T(8,128)}), f32[32,16,128]{2,1,0:T(8,128)}, u32[]{:S(2)}, u32[]{:S(2)}) async-start(f32[32,16,128]{2,1,0:T(8,128)} %bitcast.19), calls=%async_computation.2 | async-start | bytes 524288 | tf_op jit(solution)/shard_map/all_to_all | solution.py:49
  147.3 13.1 %copy-start.19 = (bf16[512,512]{1,0:T(8,128)(2,1)}, bf16[512,512]{1,0:T(8,128)(2,1)S(1)}, u32[]{:S(2)}) copy-start(bf16[512,512]{1,0:T(8,128)(2,1)S(1)} %multiply_reduce_fusion) | copy-start | bytes 1572868
  147.3 29.5 %copy-start.9 = (bf16[512,512]{1,0:T(8,128)(2,1)S(1)}, bf16[512,512]{1,0:T(8,128)(2,1)}, u32[]{:S(2)}) copy-start(bf16[512,512]{1,0:T(8,128)(2,1)} %param.9) | copy-start | bytes 1572868
  147.3 29.5 %copy-start.11 = (f32[512,512]{1,0:T(8,128)S(1)}, f32[512,512]{1,0:T(8,128)}, u32[]{:S(2)}) copy-start(f32[512,512]{1,0:T(8,128)} %copy-done.10) | copy-start | bytes 3145732
  159.5 19.4 %copy-start.29 = (f32[8,512]{1,0:T(8,128)S(1)}, f32[8,512]{1,0:T(8,128)}, u32[]{:S(2)}) copy-start(f32[8,512]{1,0:T(8,128)} %copy-done.28) | copy-start | bytes 49156
  160.4 16.4 %all-to-all-start.3 = ((f32[32,16,128]{2,1,0:T(8,128)}), f32[32,16,128]{2,1,0:T(8,128)S(1)}, u32[]{:S(2)}, u32[]{:S(2)}) async-start(f32[32,16,128]{2,1,0:T(8,128)} %copy.110), calls=%async_computation.3 | async-start | bytes 524288 | tf_op jit(solution)/shard_map/all_to_all | solution.py:49
  178.9 6.3 %copy-start.32 = (f32[512]{0:T(512)S(1)}, f32[512]{0:T(512)}, u32[]{:S(2)}) copy-start(f32[512]{0:T(512)} %get-tuple-element.38) | copy-start | bytes 6148
  178.9 13.3 %copy-start.15 = (bf16[512,512]{1,0:T(8,128)(2,1)S(1)}, bf16[512,512]{1,0:T(8,128)(2,1)}, u32[]{:S(2)}) copy-start(bf16[512,512]{1,0:T(8,128)(2,1)} %copy-done.14) | copy-start | bytes 1572868
  178.9 13.3 %copy-start.21 = (bf16[512,128]{1,0:T(8,128)(2,1)S(1)}, bf16[512,128]{1,0:T(8,128)(2,1)}, u32[]{:S(2)}) copy-start(bf16[512,128]{1,0:T(8,128)(2,1)} %param.10) | copy-start | bytes 393220
  178.9 6.5 %collective-permute-start.11 = (f32[512,128]{1,0:T(8,128)}, f32[512,128]{1,0:T(8,128)}, u32[]{:S(2)}, u32[]{:S(2)}) collective-permute-start(f32[512,128]{1,0:T(8,128)} %fusion.21), channel_id=1, source_target_pairs={{0,1},{1,0},{2,3},{3,2},{4,5},{5,4},{6,7},{7,6},{8,9},{9,8},{10,11... | collective-permute-start | bytes 786440 | tf_op jit(solution)/shard_map/ppermute | solution.py:53
  187.8 18.1 %collective-permute-start.16 = (bf16[512,128]{1,0:T(8,128)(2,1)S(1)}, bf16[512,128]{1,0:T(8,128)(2,1)S(1)}, u32[]{:S(2)}, u32[]{:S(2)}) collective-permute-start(bf16[512,128]{1,0:T(8,128)(2,1)S(1)} %fusion.24), channel_id=1, source_target_pairs={{0,4},{2,6},{4,0},{6,2},{1,5},{3,7},{5,1},{7,3},{8,12},{10,14},{12... | collective-permute-start | bytes 393224 | tf_op jit(solution)/shard_map/ppermute | solution.py:272
  190.2 15.7 %collective-permute-start.17 = (bf16[512,128]{1,0:T(8,128)(2,1)S(1)}, bf16[512,128]{1,0:T(8,128)(2,1)S(1)}, u32[]{:S(2)}, u32[]{:S(2)}) collective-permute-start(bf16[512,128]{1,0:T(8,128)(2,1)S(1)} %fusion.24), channel_id=1, source_target_pairs={{0,6},{2,0},{4,2},{6,4},{1,7},{3,1},{5,3},{7,5},{8,14},{10,8},{12,... | collective-permute-start | bytes 393224 | tf_op jit(solution)/shard_map/ppermute | solution.py:272
  191.6 14.3 %collective-permute-start.15 = (bf16[512,128]{1,0:T(8,128)(2,1)S(1)}, bf16[512,128]{1,0:T(8,128)(2,1)}, u32[]{:S(2)}, u32[]{:S(2)}) collective-permute-start(bf16[512,128]{1,0:T(8,128)(2,1)S(1)} %fusion.24), channel_id=1, source_target_pairs={{0,2},{2,4},{4,6},{6,0},{1,3},{3,5},{5,7},{7,1},{8,10},{10,12},{12... | collective-permute-start | bytes 393224 | tf_op jit(solution)/shard_map/ppermute | solution.py:272
  192.2 7.4 %copy-start.18 = (f32[512,128]{1,0:T(8,128)S(1)}, f32[512,128]{1,0:T(8,128)}, u32[]{:S(2)}) copy-start(f32[512,128]{1,0:T(8,128)} %copy-done.17) | copy-start | bytes 786436
  192.2 7.4 %copy-start.31 = (f32[512]{0:T(512)S(1)}, f32[512]{0:T(512)}, u32[]{:S(2)}) copy-start(f32[512]{0:T(512)} %mul.147) | copy-start | bytes 6148
  195.8 19.7 %copy-start.33 = (f32[8]{0:T(128)S(1)}, f32[8]{0:T(128)}, u32[]{:S(2)}) copy-start(f32[8]{0:T(128)} %param.17) | copy-start | bytes 100
  195.8 20.9 %copy-start.23 = (f32[128,512]{1,0:T(8,128)S(1)}, f32[128,512]{1,0:T(8,128)}, u32[]{:S(2)}) copy-start(f32[128,512]{1,0:T(8,128)} %param.15) | copy-start | bytes 786436
  195.8 20.9 %copy-start.24 = (bf16[128,512]{1,0:T(8,128)(2,1)S(1)}, bf16[128,512]{1,0:T(8,128)(2,1)}, u32[]{:S(2)}) copy-start(bf16[128,512]{1,0:T(8,128)(2,1)} %reduce-scatter.2.cloned.1.call-done) | copy-start | bytes 393220
  195.8 20.9 %copy-start.27 = (f32[128,512]{1,0:T(8,128)S(1)}, f32[128,512]{1,0:T(8,128)}, u32[]{:S(2)}) copy-start(f32[128,512]{1,0:T(8,128)} %param.16) | copy-start | bytes 786436
  200.7 14.8 %all-to-all-start.4 = ((f32[32,8,128]{2,1,0:T(8,128)}), f32[32,8,128]{2,1,0:T(8,128)S(1)}, u32[]{:S(2)}, u32[]{:S(2)}) async-start(f32[32,8,128]{2,1,0:T(8,128)} %broadcast_in_dim_broadcast_in_dim_broadcast_in_dim.2), calls=%async_computation.5 | async-start | bytes 262144 | tf_op jit(solution)/shard_map/all_to_all | solution.py:49
  206.9 10.7 %collective-permute-start.18 = (f32[512,128]{1,0:T(8,128)S(1)}, f32[512,128]{1,0:T(8,128)S(1)}, u32[]{:S(2)}, u32[]{:S(2)}) collective-permute-start(f32[512,128]{1,0:T(8,128)S(1)} %convert_add_fusion), channel_id=1, source_target_pairs={{0,1},{1,0},{2,3},{3,2},{4,5},{5,4},{6,7},{7,6},{8,9},{9,8},{10,11... | collective-permute-start | bytes 786440 | tf_op jit(solution)/shard_map/ppermute | solution.py:53
Sparse Core Ops, SparseCore 0:
  29.6 43.0 all-gather.1
  131.1 39.4 reduce-scatter.1

commit v7 on v6

--- a/solution.py
+++ b/solution.py
@@ -222,16 +222,11 @@
     out_y = (core_y + skip_wide * head_x).astype(bf16)
 
     core_one = jnp.full((1,), core, jnp.int32)
-    part_far, part_down, part_up, part_own = (
-        ring_grad_part(core_one, owns[step], others[step], weight_rows) for step in (2, 3, 1, 0)
-    )
-    from_up = ring_shift(part_far[:half], 1).astype(f32) + part_down[:half].astype(f32)
-    from_down = ring_shift(part_far[half:], 3).astype(f32) + part_up[half:].astype(f32)
     parts = [
-        part_own,
-        ring_shift(jnp.concatenate([from_up.astype(bf16), part_down[half:]]), 1),
-        ring_shift(jnp.concatenate([part_up[:half], from_down.astype(bf16)]), 3),
+        ring_shift(ring_grad_part(core_one, owns[step], others[step], weight_rows), 4 - step)
+        for step in (2, 1, 3)
     ]
+    parts.append(ring_grad_part(core_one, owns[0], others[0], weight_rows))
     ring_y = [ring_shift(out_y, step) for step in range(4)]
     parts, _ = lax.optimization_barrier((parts, out_y))
     grad_low = sum(part.astype(f32) for part in parts).astype(bf16)
@@ -243,10 +238,14 @@
     grad_decayed = grad * from_start_wide
     carried = exact(grad_decayed, read_vector, ((0,), (0,)))
     carried = swap(carried.reshape(BLOCKS, 16, 128), CTX)
-    end = swap(chain(weights, carried, True), CTX).reshape(width, 128)
-
     grad_heads = grad_low.reshape(tokens, heads, head_width)
     inner = jnp.einsum("hst,shp->thp", mixed, grad_heads, preferred_element_type=f32)
+    inner = inner.reshape(tokens, width)
+    entering = chain(weights, carried, True)
+    entering, inner = lax.optimization_barrier((entering, inner))
+    end = swap(entering, CTX).reshape(width, 128)
+
+
     cross_dots = jnp.einsum("thp,shp->hts", grad_heads, x_heads, preferred_element_type=f32)
     pair_weights = jnp.sum(lower_decay * cross_dots, axis=0).astype(bf16)
     read_grad = mm(pair_weights, write_vector, ((1,), (0,))) + mm(
@@ -271,6 +270,7 @@
     terms = [mine] + [
         lax.ppermute(mine, "y", [(i, (i + step) % 4) for i in range(4)]) for step in range(1, 4)
     ]
+    terms, small = lax.optimization_barrier((terms, small))
     keep = 0.0
     for y in range(4):
         keep = keep + lax.select_n(lax.rem(column + 4 - y, 4), *terms).astype(f32)
@@ -278,7 +278,7 @@
     write_sum = jnp.where(core == 0, keep, give)
     read_sum = jnp.where(core == 0, give, keep)
 
-    core_grad = inner.reshape(tokens, width) + exact(write_vector, end, ((1,), (1,))) * to_end_wide
+    core_grad = inner + exact(write_vector, end, ((1,), (1,))) * to_end_wide
     input_grad = (core_grad + skip_wide * grad).astype(bf16)
 
     terms = (grad * core_y - head_x * core_grad).reshape(tokens, heads, head_width)

time: 227 us -> 213 us (0.938); the launches traced: 225 us -> 209 us
  waiting for transfers between devices: 66.4 us -> 44 us
  starting transfers between devices: 56.2 us -> 60 us
  other arithmetic: 17.8 us -> 21 us
  local copies, waits for them, and re-layouts: 28.3 us -> 25.1 us
    ppermute x10 -> x9, waiting for transfers between devices: 34.7 us -> 17.2 us  [ring_shift(): lax.ppermute(value, 'x', [(i, (i + step) % 4) for i in range(4)])]
    all_to_all x5, waiting for transfers between devices: 31.7 us -> 16.2 us  [swap(): return lax.all_to_all(value, axes, 0, 0, tiled=True)]
    reduce_scatter x1, waiting for transfers between devices: 0.02 us -> 5.61 us  [shards(): lax.psum_scatter(partial, 'z', scatter_dimension=0, tiled=True).astype(f32)]
    all_gather x1, waiting for transfers between devices: 0.01 us -> 4.94 us  [shards(): lax.all_gather(out_master.astype(bf16), 'z', axis=0, tiled=True)]
    all_to_all x5, starting transfers between devices: 35 us -> 38.1 us  [swap(): return lax.all_to_all(value, axes, 0, 0, tiled=True)]
    reshape x2 -> x1, local copies, waits for them, and re-layouts: 5.08 us -> 2.55 us  [shards(): inner.reshape(tokens, width)]
    optimization_barrier x0 -> x2, local copies, waits for them, and re-layouts: none -> 2.42 us  [shards(): entering, inner = lax.optimization_barrier((entering, inner))]
    unnamed x69 -> x59, local copies, waits for them, and re-layouts: 6.28 us -> 4.19 us
  transfers between devices with their start and end apart: 26 -> 25, of which waited for: 8 -> 9; matrix products, arithmetic and copies ran while one was open for 27% -> 30% of each run, Pallas kernels for 5% -> 7%
where the time goes in v7:
time: 213 us; the launch traced here: 209 us
  starting transfers between devices  60 us (28%)
  waiting for transfers between devices  44 us (21%)
  matrix products  30.3 us (14%)
  local copies, waits for them, and re-layouts  25.1 us (12%)
  other arithmetic  21 us (10%)
  between operations  14.6 us (7%)
  Pallas kernels  13.7 us (6%)
    all_to_all x5, starting transfers between devices, swap(): return lax.all_to_all(value, axes, 0, 0, tiled=True)  38.1 us
    ppermute x9, waiting for transfers between devices, ring_shift(): lax.ppermute(value, 'x', [(i, (i + step) % 4) for i in range(4)])  17.2 us
    all_to_all x5, waiting for transfers between devices, swap(): return lax.all_to_all(value, axes, 0, 0, tiled=True)  16.2 us
    ppermute x9, starting transfers between devices, ring_shift(): lax.ppermute(value, 'x', [(i, (i + step) % 4) for i in range(4)])  15.2 us
    dot_general x6, matrix products, exact(): lax.dot_general(a.astype(f32), b.astype(f32), (dims, ((), ())), precision...  13.1 us
    pallas_call x4, Pallas kernels, ring_grad_part(): pl.pallas_call(ring_grad_kernel, out_shape=jax.ShapeDtypeStruct((2 * half...  7.71 us
    dot_general x5, matrix products, mm(): return lax.dot_general(a, b, (dims, ((), ())), preferred_element_type=f32)  6.95 us
    pallas_call x1, Pallas kernels, weight_grad_part(): pl.pallas_call(weight_grad_kernel, out_shape=jax.ShapeDtypeStruct((quarte...  5.97 us
  transfers between devices with their start and end apart: 25, of which 9 were waited for; matrix products, arithmetic and copies ran while one was open for 30% of the time, Pallas kernels for 7%

profile of v7, /device:TPU:8, one launch (start us, length us, event | category | flops | bytes accessed | tf_op | source)
XLA Modules:
  0.0 208.6 jit_solution(13951289460496771224)
XLA Ops:
  7.2 2.3 %reduce-window.14 = f32[8,4,128]{2,0,1:T(8,128)S(1)} reduce-window(f32[8,4,128]{2,0,1:T(8,128)} %bitcast.107, f32[]{:T(128)} %constant.60.clone.1), window={size=1x1x128 pad=0_0x0_0x127_0}, to_apply=%region_0.0 | reduce-window | flops 520192 | bytes 32772 | tf_op jit(solution)/shard_map/reduce-window
  11.8 2.4 %fusion.13 = f32[512,128]{1,0:T(8,128)S(1)} fusion(bf16[512,128]{1,0:T(8,128)(2,1)} %param.10, f32[512,512]{1,0:T(8,128)S(1)} %copy.99, bf16[512,512]{1,0:T(8,128)(2,1)} %param.9), kind=kOutput, calls=%fused_computation.32 | convolution fusion | flops 403177472 | bytes 1966080 | tf_op jit(solution)/shard_map/dot_general | solution.py:39
  14.9 0.8 pad_maximum_fusion
  15.7 11.3 %all-to-all-start = ((f32[32,24,128]{2,1,0:T(8,128)}), f32[32,24,128]{2,1,0:T(8,128)S(1)}, u32[]{:S(2)}, u32[]{:S(2)}) async-start(f32[32,24,128]{2,1,0:T(8,128)} %pad_maximum_fusion), calls=%async_computation | async-start | bytes 786432 | tf_op jit(solution)/shard_map/all_to_all | solution.py:49
  27.8 2.8 %fusion.46 = (bf16[256,1024]{1,0:T(8,128)(2,1)S(1)}, bf16[256,1024]{1,0:T(8,128)(2,1)}, bf16[256,1024]{1,0:T(8,128)(2,1)S(1)}, bf16[256,1024]{1,0:T(8,128)(2,1)}) fusion(bf16[512,4096]{1,0:T(8,128)(2,1)} %param.14, s32[]{:T(128)S(6)} %select_n.158, s32[]{:T(128)S(6)} %select_n.162, s32[]{:T(128)S(6)} %select_n.160, s32[]{:T(128)S(6)} %select_n.159, ...), kind=kLoop, calls=%fused_computation.93 | loop fusion | bytes 4194324 | tf_op jit(solution)/shard_map/dynamic_slice | solution.py:187
  30.6 1.8 collective-permute-start
  32.4 2.7 %collective-permute-start.1 = (bf16[256,1024]{1,0:T(8,128)(2,1)}, bf16[256,1024]{1,0:T(8,128)(2,1)S(1)}, u32[]{:S(2)}, u32[]{:S(2)}) collective-permute-start(bf16[256,1024]{1,0:T(8,128)(2,1)} %get-tuple-element.61), channel_id=1, source_target_pairs={{0,128},{64,192},{128,0},{192,64},{1,129},{65,193},{129,1},{193,65... | collective-permute-start | bytes 1572872 | tf_op jit(solution)/shard_map/ppermute | solution.py:57
  35.1 1.4 collective-permute-start.2
  36.5 5.0 %all-to-all-done = f32[32,24,128]{2,1,0:T(8,128)S(1)} async-done(((f32[32,24,128]{2,1,0:T(8,128)}), f32[32,24,128]{2,1,0:T(8,128)S(1)}, u32[]{:S(2)}, u32[]{:S(2)}) %all-to-all-start) | async-done | bytes 393248 | tf_op jit(solution)/shard_map/all_to_all | solution.py:49
  42.5 0.9 copy.101
  43.4 5.2 %all-to-all-start.1 = ((f32[32,16,128]{2,1,0:T(8,128)}), f32[32,16,128]{2,1,0:T(8,128)S(1)}, u32[]{:S(2)}, u32[]{:S(2)}) async-start(f32[32,16,128]{2,1,0:T(8,128)} %copy.101), calls=%async_computation.1 | async-start | bytes 524288 | tf_op jit(solution)/shard_map/all_to_all | solution.py:49
  48.6 14.4 %collective-permute-done.1.own_in.refs_2_ = bf16[256,1024]{1,0:T(8,128)(2,1)S(1)} collective-permute-done((bf16[256,1024]{1,0:T(8,128)(2,1)}, bf16[256,1024]{1,0:T(8,128)(2,1)S(1)}, u32[]{:S(2)}, u32[]{:S(2)}) %collective-permute-start.1) | collective-permute-done | bytes 524320 | tf_op jit(solution)/shard_map/ppermute | solution.py:57
  63.6 2.1 copy.102
  65.7 2.2 %fusion.47 = f32[512,512]{1,0:T(8,128)} fusion(bf16[512,128]{1,0:T(8,128)(2,1)S(1)} %copy-done, bf16[512,128]{1,0:T(8,128)(2,1)} %param.10), kind=kOutput, calls=%fused_computation.94 | convolution fusion | flops 67108864 | bytes 1310720 | tf_op jit(solution)/shard_map/dot_general | solution.py:25
  68.4 4.9 %all-gather.2.cloned.1.call-done.weight_in = bf16[1024,512]{1,0:T(8,128)(2,1)} async-done(((bf16[128,512]{1,0:T(8,128)(2,1)}), bf16[1024,512]{1,0:T(8,128)(2,1)}) %all-gather.2.cloned.1.call-update) | async-done | bytes 1048592 | tf_op jit(solution)/shard_map/all_gather | solution.py:183
  73.4 1.4 copy-done.1
  74.8 1.9 ring_grad.4
  76.6 3.0 %collective-permute-start.4 = (bf16[512,512]{1,0:T(8,128)(2,1)}, bf16[512,512]{1,0:T(8,128)(2,1)}, u32[]{:S(2)}, u32[]{:S(2)}) collective-permute-start(bf16[512,512]{1,0:T(8,128)(2,1)} %ring_grad.4), channel_id=1, source_target_pairs={{0,128},{64,192},{128,0},{192,64},{1,129},{65,193},{129,1},{193,65... | collective-permute-start | bytes 1572872 | tf_op jit(solution)/shard_map/ppermute | solution.py:57
  79.6 1.9 ring_grad.5
  81.5 1.2 collective-permute-start.6
  82.7 2.4 %ring_grad.6 = bf16[512,512]{1,0:T(8,128)(2,1)} custom-call(s32[1]{0:T(128)} %bitcast.6.core_ref, bf16[256,1024]{1,0:T(8,128)(2,1)S(1)} %collective-permute-done.2.own_in.refs_3_, bf16[256,1024]{1,0:T(8,128)(2,1)} %collective-permute-done.7.other_in.refs_7_, bf16[1024,512]{1,0:T(8,128)(2,1)S(1)} %copy-done.1), custom_call_target="tpu_custom_call" | custom-call | flops 536870912 | bytes 3145728 | tf_op jit(solution)/shard_map/ring_grad/pallas_call | solution.py:103
  85.1 1.1 collective-permute-start.8
  86.3 3.4 %fusion.1 = f32[8,512,64]{1,2,0:T(8,128)} fusion(bf16[512,8,64]{0,2,1:T(8,128)(2,1)S(1)} %bitcast.102, f32[512,512]{1,0:T(8,128)S(1)} %copy-done.16, f32[8,512]{1,0:T(8,128)S(1)} %copy-done.24), kind=kOutput, calls=%fused_computation.5 | convolution fusion | flops 278921216 | bytes 2637824 | tf_op jit(solution)/shard_map/hts,shp->thp/dot_general | solution.py:220
  91.0 2.5 %copy.105 = f32[512,512]{1,0:T(8,128)} copy(f32[512,512]{0,1:T(8,128)} %bitcast.99) | data formatting | bytes 2097152 | tf_op jit(solution)/shard_map/reshape | solution.py:221
  93.6 1.9 broadcast_in_dim.65
  95.5 2.5 %copy.104 = f32[512,512]{1,0:T(8,128)} copy(f32[512,512]{0,1:T(8,128)} %bitcast.95) | data formatting | bytes 2097152 | tf_op jit(solution)/shard_map/reshape | solution.py:199
  98.0 3.7 %fusion.7 = (bf16[512,512]{1,0:T(8,128)(2,1)}, f32[512,512]{1,0:T(8,128)}) fusion(bf16[512,512]{1,0:T(8,128)(2,1)} %param.9, f32[512]{0:T(512)} %mul.129, f32[512,512]{1,0:T(8,128)} %copy.105, f32[512,512]{1,0:T(8,128)} %copy.104, f32[512,128]{1,0:T(8,128)S(1)} %bitcast.91, bf16[512,128]{1,0:T(8,128)(2,1)S(1)} %copy-done), kind=kOutput, calls=%fused_computation.22 | convolution fusion | flops 404226048 | bytes 4589568 | tf_op jit(solution)/shard_map/dot_general | solution.py:39
  102.3 3.2 %collective-permute-start.12 = (bf16[512,512]{1,0:T(8,128)(2,1)}, bf16[512,512]{1,0:T(8,128)(2,1)}, u32[]{:S(2)}, u32[]{:S(2)}) collective-permute-start(bf16[512,512]{1,0:T(8,128)(2,1)} %get-tuple-element.67.refs_8_), channel_id=1, source_target_pairs={{0,128},{64,192},{128,0},{192,64},{1,129},{65,193},{129,1},{193,65... | collective-permute-start | bytes 1572872 | tf_op jit(solution)/shard_map/ppermute | solution.py:57
  105.5 1.6 ring_grad.7
  107.3 2.4 %fusion.9 = (f32[512]{0:T(512)}, bf16[512,512]{1,0:T(8,128)(2,1)S(1)}) fusion(bf16[512,512]{1,0:T(8,128)(2,1)S(1)} %copy-done.7, bf16[512,512]{1,0:T(8,128)(2,1)S(1)} %ring_grad.7, bf16[512,512]{1,0:T(8,128)(2,1)} %collective-permute-done.8, bf16[512,512]{1,0:T(8,128)(2,1)} %collective-permute-done.6, bf16[512,512]{1,0:T(8,128)(2,1)} %collective-permute-done.4), kind=kLoop, calls=%fused_computation.24 | loop fusion | flops 3145216 | bytes 3147776 | tf_op jit(solution)/shard_map/reduce_sum | solution.py:258
  109.7 1.7 fusion.15
  111.4 1.0 copy.109
  112.4 6.1 %all-to-all-start.2 = ((f32[32,16,128]{2,1,0:T(8,128)}), f32[32,16,128]{2,1,0:T(8,128)}, u32[]{:S(2)}, u32[]{:S(2)}) async-start(f32[32,16,128]{2,1,0:T(8,128)} %bitcast.97), calls=%async_computation.2 | async-start | bytes 524288 | tf_op jit(solution)/shard_map/all_to_all | solution.py:49
  118.6 3.1 %multiply_reduce_fusion = bf16[512,512]{1,0:T(8,128)(2,1)S(1)} fusion(f32[8,512]{1,0:T(8,128)} %copy-done.23, bf16[512,8,64]{0,2,1:T(8,128)(2,1)} %bitcast.103, bf16[512,8,64]{0,2,1:T(8,128)(2,1)} %bitcast.101), kind=kOutput, calls=%fused_computation | convolution fusion | flops 278659072 | bytes 1589248 | tf_op jit(solution)/shard_map/thp,shp->hts/dot_general | solution.py:249
  121.8 1.0 fusion.49
  122.8 1.9 collective-permute-done.12.refs_10_
  124.8 0.8 collective-permute-done.13.refs_11_
  125.6 6.0 %weight_grad.1 = bf16[1024,512]{1,0:T(8,128)(2,1)} custom-call(s32[1]{0:T(128)} %bitcast.6.core_ref, bf16[256,1024]{1,0:T(8,128)(2,1)S(1)} %get-tuple-element.32.own_in.refs_0_, bf16[256,1024]{1,0:T(8,128)(2,1)S(1)} %collective-permute-done.own_in.refs_1_, bf16[256,1024]{1,0:T(8,128)(2,1)S(1)} %collective-permute-done.1.own_in.refs_2_, ...), custom_call_target="tpu_custom_call" | custom-call | flops 2147483648 | bytes 8388608 | tf_op jit(solution)/shard_map/weight_grad/pallas_call | solution.py:143
  131.6 3.7 %fusion = f32[8,64,512]{2,1,0:T(8,128)} fusion(bf16[512,8,64]{0,2,1:T(8,128)(2,1)} %bitcast.104, f32[512,512]{1,0:T(8,128)} %fusion.47, f32[8,512]{1,0:T(8,128)} %copy-done.23), kind=kOutput, calls=%fused_computation.4 | convolution fusion | flops 278921216 | bytes 2637824 | tf_op jit(solution)/shard_map/hst,shp->thp/dot_general | solution.py:242
  135.3 1.5 fusion.25
  136.9 0.9 copy.110
  137.7 8.2 %all-to-all-start.3 = ((f32[32,16,128]{2,1,0:T(8,128)}), f32[32,16,128]{2,1,0:T(8,128)}, u32[]{:S(2)}, u32[]{:S(2)}) async-start(f32[32,16,128]{2,1,0:T(8,128)} %copy.110), calls=%async_computation.3 | async-start | bytes 524288 | tf_op jit(solution)/shard_map/all_to_all | solution.py:49
  146.0 1.4 fusion.48
  147.4 1.0 convolution_add_fusion
  148.4 10.1 %all-to-all-done.3 = f32[32,16,128]{2,1,0:T(8,128)} async-done(((f32[32,16,128]{2,1,0:T(8,128)}), f32[32,16,128]{2,1,0:T(8,128)}, u32[]{:S(2)}, u32[]{:S(2)}) %all-to-all-start.3) | async-done | bytes 262176 | tf_op jit(solution)/shard_map/all_to_all | solution.py:49
  158.5 1.3 convolution_add_fusion.1
  159.8 1.9 fusion.21
  162.5 1.6 copy.113
  164.1 1.8 fusion.24
  165.9 5.6 %reduce-scatter.2.cloned.1.call-done = bf16[128,512]{1,0:T(8,128)(2,1)} async-done(((bf16[1024,512]{1,0:T(8,128)(2,1)}), bf16[128,512]{1,0:T(8,128)(2,1)}) %reduce-scatter.2.cloned.1.call-update) | async-done | bytes 131088 | tf_op jit(solution)/shard_map/reduce_scatter | solution.py:235
  171.5 1.0 fusion.19
  173.4 1.5 collective-permute-start.14
  174.9 2.0 collective-permute-start.15
  176.9 1.9 collective-permute-start.16
  179.5 7.3 %all-to-all-start.4 = ((f32[32,8,128]{2,1,0:T(8,128)}), f32[32,8,128]{2,1,0:T(8,128)}, u32[]{:S(2)}, u32[]{:S(2)}) async-start(f32[32,8,128]{2,1,0:T(8,128)} %broadcast_in_dim_broadcast_in_dim_broadcast_in_dim.2), calls=%async_computation.5 | async-start | bytes 262144 | tf_op jit(solution)/shard_map/all_to_all | solution.py:49
  186.8 3.4 %fusion.8 = (f32[512,512]{1,0:T(8,128)}, bf16[512,512]{1,0:T(8,128)(2,1)}) fusion(bf16[512,512]{1,0:T(8,128)(2,1)S(1)} %copy-done.8, f32[512,512]{1,0:T(8,128)} %get-tuple-element.68, bf16[512,512]{1,0:T(8,128)(2,1)S(1)} %get-tuple-element.55, f32[512]{0:T(512)S(1)} %copy-done.25, f32[512,512]{1,0:T(8,128)S(1)} %copy.113, f32[512,512]{1,0:T(8,128)S(1)} %copy-done.10, ...), kind=kOutput, calls=%fused_computation.23 | convolution fusion | flops 405274624 | bytes 6162432 | tf_op jit(solution)/shard_map/dot_general | solution.py:39
  190.2 1.6 copy.114
  192.2 1.1 reduce-window.16
  193.6 1.3 multiply_reduce_fusion.1
  196.1 0.9 all-to-all-done.4
  197.0 0.9 reduce_sum.92
  198.0 1.2 convert_add_fusion
  200.0 0.9 multiply_subtract_fusion
  200.9 0.8 broadcast_select_fusion
  (127 shorter events, 13.3 us)
Async XLA Ops:
  7.2 58.5 %copy-start = (bf16[512,128]{1,0:T(8,128)(2,1)S(1)}, bf16[512,128]{1,0:T(8,128)(2,1)}, u32[]{:S(2)}) copy-start(bf16[512,128]{1,0:T(8,128)(2,1)} %param.11) | copy-start | bytes 393220
  7.2 19.9 %copy-start.17 = (f32[128,512]{1,0:T(8,128)S(1)}, f32[128,512]{1,0:T(8,128)}, u32[]{:S(2)}) copy-start(f32[128,512]{1,0:T(8,128)} %param.15) | copy-start | bytes 786436
  10.3 1.1 copy-start.23
  11.8 16.0 %copy-start.9 = (f32[512,512]{1,0:T(8,128)}, f32[512,512]{1,0:T(8,128)S(1)}, u32[]{:S(2)}) copy-start(f32[512,512]{1,0:T(8,128)S(1)} %copy.99) | copy-start | bytes 3145732
  14.2 0.7 copy-start.13
  15.7 25.9 %all-to-all-start = ((f32[32,24,128]{2,1,0:T(8,128)}), f32[32,24,128]{2,1,0:T(8,128)S(1)}, u32[]{:S(2)}, u32[]{:S(2)}) async-start(f32[32,24,128]{2,1,0:T(8,128)} %pad_maximum_fusion), calls=%async_computation | async-start | bytes 786432 | tf_op jit(solution)/shard_map/all_to_all | solution.py:49
  27.0 46.3 %all-gather.2.cloned.1.call-start = ((), (), s32[]{:S(2)}) async-start(), calls=%async_computation.6 | async-start | bytes 1179648 | tf_op jit(solution)/shard_map/all_gather | solution.py:183
  30.6 18.0 %collective-permute-start = (bf16[256,1024]{1,0:T(8,128)(2,1)}, bf16[256,1024]{1,0:T(8,128)(2,1)S(1)}, u32[]{:S(2)}, u32[]{:S(2)}) collective-permute-start(bf16[256,1024]{1,0:T(8,128)(2,1)} %get-tuple-element.59), channel_id=1, source_target_pairs={{0,64},{64,128},{128,192},{192,0},{1,65},{65,129},{129,193},{193,1... | collective-permute-start | bytes 1572872 | tf_op jit(solution)/shard_map/ppermute | solution.py:57
  32.4 30.6 %collective-permute-start.1 = (bf16[256,1024]{1,0:T(8,128)(2,1)}, bf16[256,1024]{1,0:T(8,128)(2,1)S(1)}, u32[]{:S(2)}, u32[]{:S(2)}) collective-permute-start(bf16[256,1024]{1,0:T(8,128)(2,1)} %get-tuple-element.61), channel_id=1, source_target_pairs={{0,128},{64,192},{128,0},{192,64},{1,129},{65,193},{129,1},{193,65... | collective-permute-start | bytes 1572872 | tf_op jit(solution)/shard_map/ppermute | solution.py:57
  35.1 27.9 %collective-permute-start.2 = (bf16[256,1024]{1,0:T(8,128)(2,1)S(1)}, bf16[256,1024]{1,0:T(8,128)(2,1)S(1)}, u32[]{:S(2)}, u32[]{:S(2)}) collective-permute-start(bf16[256,1024]{1,0:T(8,128)(2,1)S(1)} %get-tuple-element.58), channel_id=1, source_target_pairs={{0,192},{64,0},{128,64},{192,128},{1,193},{65,1},{129,65},{193,129... | collective-permute-start | bytes 1572872 | tf_op jit(solution)/shard_map/ppermute | solution.py:57
  43.4 19.7 %all-to-all-start.1 = ((f32[32,16,128]{2,1,0:T(8,128)}), f32[32,16,128]{2,1,0:T(8,128)S(1)}, u32[]{:S(2)}, u32[]{:S(2)}) async-start(f32[32,16,128]{2,1,0:T(8,128)} %copy.101), calls=%async_computation.1 | async-start | bytes 524288 | tf_op jit(solution)/shard_map/all_to_all | solution.py:49
  63.1 10.2 %collective-permute-start.3 = (bf16[256,1024]{1,0:T(8,128)(2,1)S(1)}, bf16[256,1024]{1,0:T(8,128)(2,1)S(1)}, u32[]{:S(2)}, u32[]{:S(2)}) collective-permute-start(bf16[256,1024]{1,0:T(8,128)(2,1)S(1)} %collective-permute-done.1.own_in.refs_2_), channel_id=1, source_target_pairs={{0,1},{1,0},{2,3},{3,2},{4,5},{5,4},{6,7},{7,6},{8,9},{9,8},{10,11... | collective-permute-start | bytes 1572872 | tf_op jit(solution)/shard_map/ppermute | solution.py:53
  63.1 16.5 %collective-permute-start.5 = (bf16[256,1024]{1,0:T(8,128)(2,1)S(1)}, bf16[256,1024]{1,0:T(8,128)(2,1)S(1)}, u32[]{:S(2)}, u32[]{:S(2)}) collective-permute-start(bf16[256,1024]{1,0:T(8,128)(2,1)S(1)} %collective-permute-done.own_in.refs_1_), channel_id=1, source_target_pairs={{0,1},{1,0},{2,3},{3,2},{4,5},{5,4},{6,7},{7,6},{8,9},{9,8},{10,11... | collective-permute-start | bytes 1572872 | tf_op jit(solution)/shard_map/ppermute | solution.py:53
  63.6 19.1 %collective-permute-start.7 = (bf16[256,1024]{1,0:T(8,128)(2,1)S(1)}, bf16[256,1024]{1,0:T(8,128)(2,1)}, u32[]{:S(2)}, u32[]{:S(2)}) collective-permute-start(bf16[256,1024]{1,0:T(8,128)(2,1)S(1)} %collective-permute-done.2.own_in.refs_3_), channel_id=1, source_target_pairs={{0,1},{1,0},{2,3},{3,2},{4,5},{5,4},{6,7},{7,6},{8,9},{9,8},{10,11... | collective-permute-start | bytes 1572872 | tf_op jit(solution)/shard_map/ppermute | solution.py:53
  67.9 34.4 %collective-permute-start.9 = (bf16[256,1024]{1,0:T(8,128)(2,1)S(1)}, bf16[256,1024]{1,0:T(8,128)(2,1)}, u32[]{:S(2)}, u32[]{:S(2)}) collective-permute-start(bf16[256,1024]{1,0:T(8,128)(2,1)S(1)} %get-tuple-element.32.own_in.refs_0_), channel_id=1, source_target_pairs={{0,1},{1,0},{2,3},{3,2},{4,5},{5,4},{6,7},{7,6},{8,9},{9,8},{10,11... | collective-permute-start | bytes 1572872 | tf_op jit(solution)/shard_map/ppermute | solution.py:53
  73.3 16.3 %copy-start.3 = (bf16[256,1024]{1,0:T(8,128)(2,1)}, bf16[256,1024]{1,0:T(8,128)(2,1)S(1)}, u32[]{:S(2)}) copy-start(bf16[256,1024]{1,0:T(8,128)(2,1)S(1)} %collective-permute-done.3.other_in.refs_6_) | copy-start | bytes 1572868
  73.4 1.4 copy-start.1
  74.8 11.5 %copy-start.16 = (f32[512,512]{1,0:T(8,128)S(1)}, f32[512,512]{1,0:T(8,128)}, u32[]{:S(2)}) copy-start(f32[512,512]{1,0:T(8,128)} %fusion.47) | copy-start | bytes 3145732
  74.8 11.5 %copy-start.20 = (bf16[512,512]{0,1:T(8,128)(2,1)S(1)}, bf16[512,512]{0,1:T(8,128)(2,1)}, u32[]{:S(2)}) copy-start(bf16[512,512]{0,1:T(8,128)(2,1)} %copy.102) | copy-start | bytes 1572868
  74.8 11.5 %copy-start.24 = (f32[8,512]{1,0:T(8,128)S(1)}, f32[8,512]{1,0:T(8,128)}, u32[]{:S(2)}) copy-start(f32[8,512]{1,0:T(8,128)} %copy-done.23) | copy-start | bytes 49156
  76.6 30.5 %collective-permute-start.4 = (bf16[512,512]{1,0:T(8,128)(2,1)}, bf16[512,512]{1,0:T(8,128)(2,1)}, u32[]{:S(2)}, u32[]{:S(2)}) collective-permute-start(bf16[512,512]{1,0:T(8,128)(2,1)} %ring_grad.4), channel_id=1, source_target_pairs={{0,128},{64,192},{128,0},{192,64},{1,129},{65,193},{129,1},{193,65... | collective-permute-start | bytes 1572872 | tf_op jit(solution)/shard_map/ppermute | solution.py:57
  79.6 10.0 %copy-start.5 = (bf16[256,1024]{1,0:T(8,128)(2,1)}, bf16[256,1024]{1,0:T(8,128)(2,1)S(1)}, u32[]{:S(2)}) copy-start(bf16[256,1024]{1,0:T(8,128)(2,1)S(1)} %collective-permute-done.5.other_in.refs_5_) | copy-start | bytes 1572868
  81.5 25.8 %collective-permute-start.6 = (bf16[512,512]{1,0:T(8,128)(2,1)}, bf16[512,512]{1,0:T(8,128)(2,1)}, u32[]{:S(2)}, u32[]{:S(2)}) collective-permute-start(bf16[512,512]{1,0:T(8,128)(2,1)} %ring_grad.5), channel_id=1, source_target_pairs={{0,192},{64,0},{128,64},{192,128},{1,193},{65,1},{129,65},{193,129... | collective-permute-start | bytes 1572872 | tf_op jit(solution)/shard_map/ppermute | solution.py:57
  85.1 22.1 %collective-permute-start.8 = (bf16[512,512]{1,0:T(8,128)(2,1)}, bf16[512,512]{1,0:T(8,128)(2,1)}, u32[]{:S(2)}, u32[]{:S(2)}) collective-permute-start(bf16[512,512]{1,0:T(8,128)(2,1)} %ring_grad.6), channel_id=1, source_target_pairs={{0,64},{64,128},{128,192},{192,0},{1,65},{65,129},{129,193},{193,1... | collective-permute-start | bytes 1572872 | tf_op jit(solution)/shard_map/ppermute | solution.py:57
  93.6 12.0 %copy-start.2 = (bf16[1024,512]{1,0:T(8,128)(2,1)S(1)}, bf16[1024,512]{1,0:T(8,128)(2,1)}, u32[]{:S(2)}) copy-start(bf16[1024,512]{1,0:T(8,128)(2,1)} %all-gather.2.cloned.1.call-done.weight_in) | copy-start | bytes 3145732
  98.0 9.3 %copy-start.7 = (bf16[512,512]{1,0:T(8,128)(2,1)S(1)}, bf16[512,512]{1,0:T(8,128)(2,1)}, u32[]{:S(2)}) copy-start(bf16[512,512]{1,0:T(8,128)(2,1)} %param.9) | copy-start | bytes 1572868
  98.0 11.7 %copy-start.11 = (f32[512,512]{1,0:T(8,128)S(1)}, f32[512,512]{1,0:T(8,128)}, u32[]{:S(2)}) copy-start(f32[512,512]{1,0:T(8,128)} %copy.104) | copy-start | bytes 3145732
  101.7 21.1 %collective-permute-start.11 = (bf16[512,512]{1,0:T(8,128)(2,1)}, bf16[512,512]{1,0:T(8,128)(2,1)}, u32[]{:S(2)}, u32[]{:S(2)}) collective-permute-start(bf16[512,512]{1,0:T(8,128)(2,1)} %get-tuple-element.67.refs_8_), channel_id=1, source_target_pairs={{0,64},{64,128},{128,192},{192,0},{1,65},{65,129},{129,193},{193,1... | collective-permute-start | bytes 1572872 | tf_op jit(solution)/shard_map/ppermute | solution.py:57
  102.3 22.4 %collective-permute-start.12 = (bf16[512,512]{1,0:T(8,128)(2,1)}, bf16[512,512]{1,0:T(8,128)(2,1)}, u32[]{:S(2)}, u32[]{:S(2)}) collective-permute-start(bf16[512,512]{1,0:T(8,128)(2,1)} %get-tuple-element.67.refs_8_), channel_id=1, source_target_pairs={{0,128},{64,192},{128,0},{192,64},{1,129},{65,193},{129,1},{193,65... | collective-permute-start | bytes 1572872 | tf_op jit(solution)/shard_map/ppermute | solution.py:57
  107.2 18.4 %collective-permute-start.13 = (bf16[512,512]{1,0:T(8,128)(2,1)}, bf16[512,512]{1,0:T(8,128)(2,1)S(1)}, u32[]{:S(2)}, u32[]{:S(2)}) collective-permute-start(bf16[512,512]{1,0:T(8,128)(2,1)} %get-tuple-element.67.refs_8_), channel_id=1, source_target_pairs={{0,192},{64,0},{128,64},{192,128},{1,193},{65,1},{129,65},{193,129... | collective-permute-start | bytes 1572872 | tf_op jit(solution)/shard_map/ppermute | solution.py:57
  112.4 22.9 %all-to-all-start.2 = ((f32[32,16,128]{2,1,0:T(8,128)}), f32[32,16,128]{2,1,0:T(8,128)}, u32[]{:S(2)}, u32[]{:S(2)}) async-start(f32[32,16,128]{2,1,0:T(8,128)} %bitcast.97), calls=%async_computation.2 | async-start | bytes 524288 | tf_op jit(solution)/shard_map/all_to_all | solution.py:49
  118.6 52.9 %reduce-scatter.2.cloned.1.call-start = ((), (), s32[]{:S(2)}) async-start(), calls=%async_computation.7 | async-start | bytes 1179648 | tf_op jit(solution)/shard_map/reduce_scatter | solution.py:235
  118.6 7.0 %copy-start.4 = (bf16[256,1024]{1,0:T(8,128)(2,1)S(1)}, bf16[256,1024]{1,0:T(8,128)(2,1)}, u32[]{:S(2)}) copy-start(bf16[256,1024]{1,0:T(8,128)(2,1)} %copy-done.3) | copy-start | bytes 1572868
  118.6 7.0 %copy-start.6 = (bf16[256,1024]{1,0:T(8,128)(2,1)S(1)}, bf16[256,1024]{1,0:T(8,128)(2,1)}, u32[]{:S(2)}) copy-start(bf16[256,1024]{1,0:T(8,128)(2,1)} %copy-done.5) | copy-start | bytes 1572868
  121.8 1.1 copy-start.15
  131.6 15.7 %copy-start.12 = (f32[512,512]{1,0:T(8,128)S(1)}, f32[512,512]{1,0:T(8,128)}, u32[]{:S(2)}) copy-start(f32[512,512]{1,0:T(8,128)} %copy.104) | copy-start | bytes 3145732
  135.3 23.1 %copy-start.8 = (bf16[512,512]{1,0:T(8,128)(2,1)S(1)}, bf16[512,512]{1,0:T(8,128)(2,1)}, u32[]{:S(2)}) copy-start(bf16[512,512]{1,0:T(8,128)(2,1)} %param.9) | copy-start | bytes 1572868
  135.3 23.1 %copy-start.10 = (f32[512,512]{1,0:T(8,128)S(1)}, f32[512,512]{1,0:T(8,128)}, u32[]{:S(2)}) copy-start(f32[512,512]{1,0:T(8,128)} %copy-done.9) | copy-start | bytes 3145732
  136.8 24.9 %copy-start.27 = (f32[8]{0:T(128)S(1)}, f32[8]{0:T(128)}, u32[]{:S(2)}) copy-start(f32[8]{0:T(128)} %get-tuple-element.48) | copy-start | bytes 100
  136.8 25.0 %copy-start.26 = (f32[512]{0:T(512)S(1)}, f32[512]{0:T(512)}, u32[]{:S(2)}) copy-start(f32[512]{0:T(512)} %get-tuple-element.54) | copy-start | bytes 6148
  137.7 20.8 %all-to-all-start.3 = ((f32[32,16,128]{2,1,0:T(8,128)}), f32[32,16,128]{2,1,0:T(8,128)}, u32[]{:S(2)}, u32[]{:S(2)}) async-start(f32[32,16,128]{2,1,0:T(8,128)} %copy.110), calls=%async_computation.3 | async-start | bytes 524288 | tf_op jit(solution)/shard_map/all_to_all | solution.py:49
  147.3 39.4 %copy-start.25 = (f32[512]{0:T(512)S(1)}, f32[512]{0:T(512)}, u32[]{:S(2)}) copy-start(f32[512]{0:T(512)} %mul.129) | copy-start | bytes 6148
  159.8 2.1 %copy-start.14 = (f32[512,128]{1,0:T(8,128)}, f32[512,128]{1,0:T(8,128)S(1)}, u32[]{:S(2)}) copy-start(f32[512,128]{1,0:T(8,128)S(1)} %convolution_add_fusion.1) | copy-start | bytes 786436
  161.7 2.4 %collective-permute-start.10 = (f32[512,128]{1,0:T(8,128)}, f32[512,128]{1,0:T(8,128)}, u32[]{:S(2)}, u32[]{:S(2)}) collective-permute-start(f32[512,128]{1,0:T(8,128)} %fusion.21), channel_id=1, source_target_pairs={{0,1},{1,0},{2,3},{3,2},{4,5},{5,4},{6,7},{7,6},{8,9},{9,8},{10,11... | collective-permute-start | bytes 786440 | tf_op jit(solution)/shard_map/ppermute | solution.py:53
  173.4 24.6 %collective-permute-start.14 = (bf16[512,128]{1,0:T(8,128)(2,1)}, bf16[512,128]{1,0:T(8,128)(2,1)}, u32[]{:S(2)}, u32[]{:S(2)}) collective-permute-start(bf16[512,128]{1,0:T(8,128)(2,1)} %fusion.24), channel_id=1, source_target_pairs={{0,2},{2,4},{4,6},{6,0},{1,3},{3,5},{5,7},{7,1},{8,10},{10,12},{12... | collective-permute-start | bytes 393224 | tf_op jit(solution)/shard_map/ppermute | solution.py:271
  174.9 23.1 %collective-permute-start.15 = (bf16[512,128]{1,0:T(8,128)(2,1)}, bf16[512,128]{1,0:T(8,128)(2,1)}, u32[]{:S(2)}, u32[]{:S(2)}) collective-permute-start(bf16[512,128]{1,0:T(8,128)(2,1)} %fusion.24), channel_id=1, source_target_pairs={{0,4},{2,6},{4,0},{6,2},{1,5},{3,7},{5,1},{7,3},{8,12},{10,14},{12... | collective-permute-start | bytes 393224 | tf_op jit(solution)/shard_map/ppermute | solution.py:271
  176.9 21.1 %collective-permute-start.16 = (bf16[512,128]{1,0:T(8,128)(2,1)}, bf16[512,128]{1,0:T(8,128)(2,1)}, u32[]{:S(2)}, u32[]{:S(2)}) collective-permute-start(bf16[512,128]{1,0:T(8,128)(2,1)} %fusion.24), channel_id=1, source_target_pairs={{0,6},{2,0},{4,2},{6,4},{1,7},{3,1},{5,3},{7,5},{8,14},{10,8},{12,... | collective-permute-start | bytes 393224 | tf_op jit(solution)/shard_map/ppermute | solution.py:271
  179.5 17.5 %all-to-all-start.4 = ((f32[32,8,128]{2,1,0:T(8,128)}), f32[32,8,128]{2,1,0:T(8,128)}, u32[]{:S(2)}, u32[]{:S(2)}) async-start(f32[32,8,128]{2,1,0:T(8,128)} %broadcast_in_dim_broadcast_in_dim_broadcast_in_dim.2), calls=%async_computation.5 | async-start | bytes 262144 | tf_op jit(solution)/shard_map/all_to_all | solution.py:49
  186.8 12.5 %copy-start.28 = (f32[8]{0:T(128)S(1)}, f32[8]{0:T(128)}, u32[]{:S(2)}) copy-start(f32[8]{0:T(128)} %param.17) | copy-start | bytes 100
  190.2 7.8 %copy-start.21 = (bf16[512,128]{1,0:T(8,128)(2,1)S(1)}, bf16[512,128]{1,0:T(8,128)(2,1)}, u32[]{:S(2)}) copy-start(bf16[512,128]{1,0:T(8,128)(2,1)} %fusion.24) | copy-start | bytes 393220
  190.2 9.9 %copy-start.18 = (f32[128,512]{1,0:T(8,128)S(1)}, f32[128,512]{1,0:T(8,128)}, u32[]{:S(2)}) copy-start(f32[128,512]{1,0:T(8,128)} %param.15) | copy-start | bytes 786436
  190.2 9.9 %copy-start.19 = (bf16[128,512]{1,0:T(8,128)(2,1)S(1)}, bf16[128,512]{1,0:T(8,128)(2,1)}, u32[]{:S(2)}) copy-start(bf16[128,512]{1,0:T(8,128)(2,1)} %reduce-scatter.2.cloned.1.call-done) | copy-start | bytes 393220
  190.2 9.9 %copy-start.22 = (f32[128,512]{1,0:T(8,128)S(1)}, f32[128,512]{1,0:T(8,128)}, u32[]{:S(2)}) copy-start(f32[128,512]{1,0:T(8,128)} %param.16) | copy-start | bytes 786436
  199.2 1.7 collective-permute-start.17
Sparse Core Ops, SparseCore 0:
  30.2 43.0 all-gather.1
  131.7 39.7 reduce-scatter.1

commit v8 on v7

--- a/solution.py
+++ b/solution.py
@@ -210,15 +210,16 @@
     weights = block_weights(packed[:, 16, 0])
     entering = chain(weights, packed[:, :16], False)
     start = swap(entering, CTX).reshape(width, 128)
-    owns, _ = lax.optimization_barrier((owns, start))
-    others = [swap_core(piece) for piece in owns]
-    start, weight_rows = lax.optimization_barrier((start, weight_rows))
 
     scores = mm(read_vector, write_vector, ((1,), (1,)))
     mixed = (lower_decay * scores[None]).astype(bf16)
     x_heads = head_input.reshape(tokens, heads, head_width)
     inner = jnp.einsum("hts,shp->thp", mixed, x_heads, preferred_element_type=f32)
-    core_y = inner.reshape(tokens, width) + exact(read_vector, start, ((1,), (1,))) * from_start_wide
+    inner = inner.reshape(tokens, width)
+    owns, inner, from_start_wide = lax.optimization_barrier((owns, inner, from_start_wide))
+    others = [swap_core(piece) for piece in owns]
+    start, weight_rows = lax.optimization_barrier((start, weight_rows))
+    core_y = inner + exact(read_vector, start, ((1,), (1,))) * from_start_wide
     out_y = (core_y + skip_wide * head_x).astype(bf16)
 
     core_one = jnp.full((1,), core, jnp.int32)

time: 213 us -> 212 us (level)
  local copies, waits for them, and re-layouts: 25.1 us -> 30.4 us
  matrix products: 30.3 us -> 26.3 us
  Pallas kernels: 13.7 us -> 11.4 us
    all_to_all x5, waiting for transfers between devices: 16.2 us -> 26.2 us  [swap(): return lax.all_to_all(value, axes, 0, 0, tiled=True)]
    optimization_barrier x0 -> x2, local copies, waits for them, and re-layouts: none -> 5.12 us  [shards(): lax.optimization_barrier((owns, inner, from_start_wide))]
    reshape x2 -> x0, local copies, waits for them, and re-layouts: 5.08 us -> none  [the longest x1 2.55 us: shards(): inner.reshape(tokens, width)]
    all_gather x1, waiting for transfers between devices: 4.94 us -> 0.01 us  [shards(): lax.all_gather(out_master.astype(bf16), 'z', axis=0, tiled=True)]
    dot_general x6, matrix products: 13.1 us -> 9.75 us  [exact(): lax.dot_general(a.astype(f32), b.astype(f32), (dims, ((), ())), precision...]
    all_to_all x5, starting transfers between devices: 38.1 us -> 41 us  [swap(): return lax.all_to_all(value, axes, 0, 0, tiled=True)]
    pallas_call x4, Pallas kernels: 7.71 us -> 5.31 us  [ring_grad_part(): pl.pallas_call(ring_grad_kernel, out_shape=jax.ShapeDtypeStruct((2 * half...]
    ppermute x9, waiting for transfers between devices: 17.2 us -> 14.8 us  [ring_shift(): lax.ppermute(value, 'x', [(i, (i + step) % 4) for i in range(4)])]
  transfers between devices with their start and end apart: 25 -> 25, of which waited for: 9 -> 9; matrix products, arithmetic and copies ran while one was open for 30% -> 32% of each run, Pallas kernels for 7% -> 5%
where the time goes in v8:
time: 212 us; the launch traced here: 209 us
  starting transfers between devices  61.6 us (29%)
  waiting for transfers between devices  44.5 us (21%)
  local copies, waits for them, and re-layouts  30.4 us (14%)
  matrix products  26.3 us (12%)
  other arithmetic  19.8 us (9%)
  between operations  14.6 us (7%)
  Pallas kernels  11.4 us (5%)
    all_to_all x5, starting transfers between devices, swap(): return lax.all_to_all(value, axes, 0, 0, tiled=True)  41 us
    all_to_all x5, waiting for transfers between devices, swap(): return lax.all_to_all(value, axes, 0, 0, tiled=True)  26.2 us
    ppermute x9, starting transfers between devices, ring_shift(): lax.ppermute(value, 'x', [(i, (i + step) % 4) for i in range(4)])  15.2 us
    ppermute x9, waiting for transfers between devices, ring_shift(): lax.ppermute(value, 'x', [(i, (i + step) % 4) for i in range(4)])  14.8 us
    dot_general x6, matrix products, exact(): lax.dot_general(a.astype(f32), b.astype(f32), (dims, ((), ())), precision...  9.75 us
    pallas_call x1, Pallas kernels, weight_grad_part(): pl.pallas_call(weight_grad_kernel, out_shape=jax.ShapeDtypeStruct((quarte...  6.1 us
    pallas_call x4, Pallas kernels, ring_grad_part(): pl.pallas_call(ring_grad_kernel, out_shape=jax.ShapeDtypeStruct((2 * half...  5.31 us
    optimization_barrier x2, local copies, waits for them, and re-layouts, shards(): lax.optimization_barrier((owns, inner, from_start_wide))  5.12 us
  transfers between devices with their start and end apart: 25, of which 9 were waited for; matrix products, arithmetic and copies ran while one was open for 32% of the time, Pallas kernels for 5%

profile of v8, /device:TPU:8, one launch (start us, length us, event | category | flops | bytes accessed | tf_op | source)
XLA Modules:
  0.0 208.7 jit_solution(8488856994704295827)
XLA Ops:
  7.3 2.9 %fusion.45 = (bf16[256,1024]{1,0:T(8,128)(2,1)}, bf16[256,1024]{1,0:T(8,128)(2,1)}, bf16[256,1024]{1,0:T(8,128)(2,1)S(1)}, bf16[256,1024]{1,0:T(8,128)(2,1)}) fusion(bf16[512,4096]{1,0:T(8,128)(2,1)} %param.14, s32[]{:T(128)S(6)} %select_n.158, s32[]{:T(128)S(6)} %select_n.162, s32[]{:T(128)S(6)} %select_n.160, s32[]{:T(128)S(6)} %select_n.159, s32[]{:T(128)S(6)} %select_n.161), kind=kLoop, calls=%fused_computation.92 | loop fusion | bytes 4194324 | tf_op jit(solution)/shard_map/dynamic_slice | solution.py:187
  10.2 1.5 collective-permute-start
  11.6 2.7 %collective-permute-start.1 = (bf16[256,1024]{1,0:T(8,128)(2,1)}, bf16[256,1024]{1,0:T(8,128)(2,1)S(1)}, u32[]{:S(2)}, u32[]{:S(2)}) collective-permute-start(bf16[256,1024]{1,0:T(8,128)(2,1)} %get-tuple-element.67), channel_id=1, source_target_pairs={{0,128},{64,192},{128,0},{192,64},{1,129},{65,193},{129,1},{193,65... | collective-permute-start | bytes 1572872 | tf_op jit(solution)/shard_map/ppermute | solution.py:57
  14.4 1.4 collective-permute-start.2
  16.5 1.1 reduce-window.14
  19.5 1.1 broadcast_in_dim.55
  20.6 2.5 %copy.99 = f32[512,512]{1,0:T(8,128)} copy(f32[512,512]{0,1:T(8,128)} %bitcast.93) | data formatting | bytes 2097152 | tf_op jit(solution)/shard_map/reshape | solution.py:198
  23.2 2.2 %fusion.12 = f32[512,128]{1,0:T(8,128)S(1)} fusion(bf16[512,128]{1,0:T(8,128)(2,1)S(1)} %copy-done, f32[512,512]{1,0:T(8,128)} %copy.99, bf16[512,512]{1,0:T(8,128)(2,1)S(1)} %copy-done.3), kind=kOutput, calls=%fused_computation.31 | convolution fusion | flops 403177472 | bytes 1966080 | tf_op jit(solution)/shard_map/dot_general | solution.py:39
  26.3 8.9 %all-to-all-start = ((f32[32,24,128]{2,1,0:T(8,128)}), f32[32,24,128]{2,1,0:T(8,128)S(1)}, u32[]{:S(2)}, u32[]{:S(2)}) async-start(f32[32,24,128]{2,1,0:T(8,128)} %pad_maximum_fusion), calls=%async_computation | async-start | bytes 786432 | tf_op jit(solution)/shard_map/all_to_all | solution.py:49
  35.2 1.0 copy.100
  36.5 4.7 %fusion.1 = f32[8,512,64]{1,2,0:T(8,128)} fusion(bf16[512,8,64]{0,2,1:T(8,128)(2,1)} %bitcast.99, f32[512,512]{1,0:T(8,128)S(1)} %fusion.46, f32[8,512]{1,0:T(8,128)S(1)} %get-tuple-element.63), kind=kOutput, calls=%fused_computation.5 | convolution fusion | flops 278921216 | bytes 2637824 | tf_op jit(solution)/shard_map/hts,shp->thp/dot_general | solution.py:217
  41.3 1.1 broadcast_in_dim.65
  42.4 10.2 %all-to-all-done = f32[32,24,128]{2,1,0:T(8,128)S(1)} async-done(((f32[32,24,128]{2,1,0:T(8,128)}), f32[32,24,128]{2,1,0:T(8,128)S(1)}, u32[]{:S(2)}, u32[]{:S(2)}) %all-to-all-start) | async-done | bytes 393248 | tf_op jit(solution)/shard_map/all_to_all | solution.py:49
  54.5 5.2 %all-to-all-start.1 = ((f32[32,16,128]{2,1,0:T(8,128)}), f32[32,16,128]{2,1,0:T(8,128)S(1)}, u32[]{:S(2)}, u32[]{:S(2)}) async-start(f32[32,16,128]{2,1,0:T(8,128)} %copy.102), calls=%async_computation.1 | async-start | bytes 524288 | tf_op jit(solution)/shard_map/all_to_all | solution.py:49
  60.3 1.3 broadcast_in_dim.66
  61.6 1.3 mul.129
  62.9 2.6 %copy.105 = f32[512,512]{1,0:T(8,128)} copy(f32[512,512]{0,1:T(8,128)} %bitcast.97) | data formatting | bytes 2097152 | tf_op jit(solution)/shard_map/optimization_barrier | solution.py:219
  65.4 2.6 %copy.104 = f32[512,512]{1,0:T(8,128)} copy(f32[512,512]{0,1:T(8,128)} %bitcast.92) | data formatting | bytes 2097152 | tf_op jit(solution)/shard_map/optimization_barrier | solution.py:219
  68.1 2.5 %all-to-all-done.1 = f32[32,16,128]{2,1,0:T(8,128)S(1)} async-done(((f32[32,16,128]{2,1,0:T(8,128)}), f32[32,16,128]{2,1,0:T(8,128)S(1)}, u32[]{:S(2)}, u32[]{:S(2)}) %all-to-all-start.1) | async-done | bytes 262176 | tf_op jit(solution)/shard_map/all_to_all | solution.py:49
  70.6 1.2 copy-done.1
  71.9 1.0 ring_grad.4
  73.0 1.6 collective-permute-start.4
  74.5 1.0 ring_grad.5
  75.6 2.1 collective-permute-start.6
  77.7 1.6 ring_grad.6
  80.2 1.4 fusion.6
  82.2 3.9 %collective-permute-start.12 = (bf16[512,512]{1,0:T(8,128)(2,1)}, bf16[512,512]{1,0:T(8,128)(2,1)}, u32[]{:S(2)}, u32[]{:S(2)}) collective-permute-start(bf16[512,512]{1,0:T(8,128)(2,1)} %get-tuple-element.60.refs_8_), channel_id=1, source_target_pairs={{0,128},{64,192},{128,0},{192,64},{1,129},{65,193},{129,1},{193,65... | collective-permute-start | bytes 1572872 | tf_op jit(solution)/shard_map/ppermute | solution.py:57
  86.1 1.6 ring_grad.7
  87.7 1.7 collective-permute-done.4
  89.4 1.2 collective-permute-start.13
  90.6 8.6 %collective-permute-done.6 = bf16[512,512]{1,0:T(8,128)(2,1)S(1)} collective-permute-done((bf16[512,512]{1,0:T(8,128)(2,1)S(1)}, bf16[512,512]{1,0:T(8,128)(2,1)S(1)}, u32[]{:S(2)}, u32[]{:S(2)}) %collective-permute-start.6) | collective-permute-done | bytes 524320 | tf_op jit(solution)/shard_map/ppermute | solution.py:57
  99.1 1.0 fusion.8
  100.9 1.7 fusion.14
  102.6 2.0 copy.109
  104.7 8.6 %all-to-all-start.2 = ((f32[32,16,128]{2,1,0:T(8,128)}), f32[32,16,128]{2,1,0:T(8,128)}, u32[]{:S(2)}, u32[]{:S(2)}) async-start(f32[32,16,128]{2,1,0:T(8,128)} %bitcast.95), calls=%async_computation.2 | async-start | bytes 524288 | tf_op jit(solution)/shard_map/all_to_all | solution.py:49
  113.3 3.1 %multiply_reduce_fusion = bf16[512,512]{1,0:T(8,128)(2,1)S(1)} fusion(f32[8,512]{1,0:T(8,128)} %copy-done.24, bf16[512,8,64]{0,2,1:T(8,128)(2,1)} %bitcast.101, bf16[512,8,64]{0,2,1:T(8,128)(2,1)} %bitcast.100), kind=kOutput, calls=%fused_computation | convolution fusion | flops 278659072 | bytes 1589248 | tf_op jit(solution)/shard_map/thp,shp->hts/dot_general | solution.py:250
  117.2 1.0 fusion.48
  118.2 3.7 %collective-permute-done.12.refs_10_ = bf16[512,512]{1,0:T(8,128)(2,1)} collective-permute-done((bf16[512,512]{1,0:T(8,128)(2,1)}, bf16[512,512]{1,0:T(8,128)(2,1)}, u32[]{:S(2)}, u32[]{:S(2)}) %collective-permute-start.12) | collective-permute-done | bytes 524320 | tf_op jit(solution)/shard_map/ppermute | solution.py:57
  122.8 6.1 %weight_grad.1 = bf16[1024,512]{1,0:T(8,128)(2,1)} custom-call(s32[1]{0:T(128)} %bitcast.6.core_ref, bf16[256,1024]{1,0:T(8,128)(2,1)S(1)} %get-tuple-element.34.own_in.refs_0_, bf16[256,1024]{1,0:T(8,128)(2,1)S(1)} %collective-permute-done.own_in.refs_1_, bf16[256,1024]{1,0:T(8,128)(2,1)S(1)} %collective-permute-done.1.own_in.refs_2_, ...), custom_call_target="tpu_custom_call" | custom-call | flops 2147483648 | bytes 8388608 | tf_op jit(solution)/shard_map/weight_grad/pallas_call | solution.py:143
  129.0 3.8 %fusion = f32[8,64,512]{2,1,0:T(8,128)} fusion(bf16[512,8,64]{0,2,1:T(8,128)(2,1)} %bitcast.102, f32[512,512]{1,0:T(8,128)} %copy-done.18, f32[8,512]{1,0:T(8,128)} %copy-done.24), kind=kOutput, calls=%fused_computation.4 | convolution fusion | flops 278921216 | bytes 2637824 | tf_op jit(solution)/shard_map/hst,shp->thp/dot_general | solution.py:243
  132.7 1.5 fusion.24
  134.3 0.9 copy.110
  135.1 10.2 %all-to-all-start.3 = ((f32[32,16,128]{2,1,0:T(8,128)}), f32[32,16,128]{2,1,0:T(8,128)}, u32[]{:S(2)}, u32[]{:S(2)}) async-start(f32[32,16,128]{2,1,0:T(8,128)} %copy.110), calls=%async_computation.3 | async-start | bytes 524288 | tf_op jit(solution)/shard_map/all_to_all | solution.py:49
  145.3 1.3 fusion.47
  146.7 1.0 convolution_add_fusion
  147.7 12.4 %all-to-all-done.3 = f32[32,16,128]{2,1,0:T(8,128)} async-done(((f32[32,16,128]{2,1,0:T(8,128)}), f32[32,16,128]{2,1,0:T(8,128)}, u32[]{:S(2)}, u32[]{:S(2)}) %all-to-all-start.3) | async-done | bytes 262176 | tf_op jit(solution)/shard_map/all_to_all | solution.py:49
  160.1 1.3 convolution_add_fusion.1
  162.1 1.8 fusion.20
  164.8 1.6 copy.113
  166.3 1.8 fusion.23
  168.1 3.5 %reduce-scatter.2.cloned.1.call-done = bf16[128,512]{1,0:T(8,128)(2,1)} async-done(((bf16[1024,512]{1,0:T(8,128)(2,1)}), bf16[128,512]{1,0:T(8,128)(2,1)}) %reduce-scatter.2.cloned.1.call-update) | async-done | bytes 131088 | tf_op jit(solution)/shard_map/reduce_scatter | solution.py:236
  171.6 1.0 fusion.18
  173.5 1.3 collective-permute-start.14
  174.8 1.3 collective-permute-start.15
  176.1 1.9 collective-permute-start.16
  178.7 8.2 %all-to-all-start.4 = ((f32[32,8,128]{2,1,0:T(8,128)}), f32[32,8,128]{2,1,0:T(8,128)}, u32[]{:S(2)}, u32[]{:S(2)}) async-start(f32[32,8,128]{2,1,0:T(8,128)} %broadcast_in_dim_broadcast_in_dim_broadcast_in_dim.2), calls=%async_computation.5 | async-start | bytes 262144 | tf_op jit(solution)/shard_map/all_to_all | solution.py:49
  186.9 3.3 %fusion.7 = (f32[512,512]{1,0:T(8,128)}, bf16[512,512]{1,0:T(8,128)(2,1)}) fusion(bf16[512,512]{1,0:T(8,128)(2,1)S(1)} %copy-done.5, f32[512,512]{1,0:T(8,128)} %get-tuple-element.61, bf16[512,512]{1,0:T(8,128)(2,1)S(1)} %copy-done.10, f32[512]{0:T(512)S(1)} %copy-done.27, f32[512,512]{1,0:T(8,128)S(1)} %copy.113, f32[512,512]{1,0:T(8,128)S(1)} %copy-done.6, ...), kind=kOutput, calls=%fused_computation.22 | convolution fusion | flops 405274624 | bytes 6162432 | tf_op jit(solution)/shard_map/dot_general | solution.py:39
  190.2 1.6 copy.114
  192.2 1.1 reduce-window.16
  193.7 1.3 multiply_reduce_fusion.1
  196.1 1.0 all-to-all-done.4
  197.1 0.9 reduce_sum.92
  198.1 1.2 convert_add_fusion
  200.1 0.9 multiply_subtract_fusion
  (134 shorter events, 17.0 us)
Async XLA Ops:
  7.2 16.0 %copy-start = (bf16[512,128]{1,0:T(8,128)(2,1)S(1)}, bf16[512,128]{1,0:T(8,128)(2,1)}, u32[]{:S(2)}) copy-start(bf16[512,128]{1,0:T(8,128)(2,1)} %param.10) | copy-start | bytes 393220
  7.2 8.6 %copy-start.19 = (f32[128,512]{1,0:T(8,128)S(1)}, f32[128,512]{1,0:T(8,128)}, u32[]{:S(2)}) copy-start(f32[128,512]{1,0:T(8,128)} %param.15) | copy-start | bytes 786436
  7.2 9.3 %copy-start.28 = (f32[8,512]{1,0:T(8,128)S(1)}, f32[8,512]{1,0:T(8,128)}, u32[]{:S(2)}) copy-start(f32[8,512]{1,0:T(8,128)} %param.12) | copy-start | bytes 49156
  7.2 16.0 %copy-start.3 = (bf16[512,512]{1,0:T(8,128)(2,1)S(1)}, bf16[512,512]{1,0:T(8,128)(2,1)}, u32[]{:S(2)}) copy-start(bf16[512,512]{1,0:T(8,128)(2,1)} %param.9) | copy-start | bytes 1572868
  7.2 63.4 %all-gather.2.cloned.1.call-start = ((), (), s32[]{:S(2)}) async-start(), calls=%async_computation.6 | async-start | bytes 1179648 | tf_op jit(solution)/shard_map/all_gather | solution.py:183
  10.2 31.1 %collective-permute-start = (bf16[256,1024]{1,0:T(8,128)(2,1)}, bf16[256,1024]{1,0:T(8,128)(2,1)S(1)}, u32[]{:S(2)}, u32[]{:S(2)}) collective-permute-start(bf16[256,1024]{1,0:T(8,128)(2,1)} %get-tuple-element.65), channel_id=1, source_target_pairs={{0,64},{64,128},{128,192},{192,0},{1,65},{65,129},{129,193},{193,1... | collective-permute-start | bytes 1572872 | tf_op jit(solution)/shard_map/ppermute | solution.py:57
  11.6 29.6 %collective-permute-start.1 = (bf16[256,1024]{1,0:T(8,128)(2,1)}, bf16[256,1024]{1,0:T(8,128)(2,1)S(1)}, u32[]{:S(2)}, u32[]{:S(2)}) collective-permute-start(bf16[256,1024]{1,0:T(8,128)(2,1)} %get-tuple-element.67), channel_id=1, source_target_pairs={{0,128},{64,192},{128,0},{192,64},{1,129},{65,193},{129,1},{193,65... | collective-permute-start | bytes 1572872 | tf_op jit(solution)/shard_map/ppermute | solution.py:57
  14.4 21.8 %copy-start.15 = (bf16[512,128]{1,0:T(8,128)(2,1)S(1)}, bf16[512,128]{1,0:T(8,128)(2,1)}, u32[]{:S(2)}) copy-start(bf16[512,128]{1,0:T(8,128)(2,1)} %param.11) | copy-start | bytes 393220
  14.4 26.9 %collective-permute-start.2 = (bf16[256,1024]{1,0:T(8,128)(2,1)}, bf16[256,1024]{1,0:T(8,128)(2,1)S(1)}, u32[]{:S(2)}, u32[]{:S(2)}) collective-permute-start(bf16[256,1024]{1,0:T(8,128)(2,1)} %get-tuple-element.64), channel_id=1, source_target_pairs={{0,192},{64,0},{128,64},{192,128},{1,193},{65,1},{129,65},{193,129... | collective-permute-start | bytes 1572872 | tf_op jit(solution)/shard_map/ppermute | solution.py:57
  18.6 17.9 %copy-start.24 = (f32[8,512]{1,0:T(8,128)}, f32[8,512]{1,0:T(8,128)S(1)}, u32[]{:S(2)}) copy-start(f32[8,512]{1,0:T(8,128)S(1)} %get-tuple-element.63) | copy-start | bytes 49156
  25.4 15.9 %copy-start.12 = (f32[512,128]{1,0:T(8,128)}, f32[512,128]{1,0:T(8,128)S(1)}, u32[]{:S(2)}) copy-start(f32[512,128]{1,0:T(8,128)S(1)} %fusion.12) | copy-start | bytes 786436
  26.3 26.3 %all-to-all-start = ((f32[32,24,128]{2,1,0:T(8,128)}), f32[32,24,128]{2,1,0:T(8,128)S(1)}, u32[]{:S(2)}, u32[]{:S(2)}) async-start(f32[32,24,128]{2,1,0:T(8,128)} %pad_maximum_fusion), calls=%async_computation | async-start | bytes 786432 | tf_op jit(solution)/shard_map/all_to_all | solution.py:49
  36.5 4.8 %copy-start.18 = (f32[512,512]{1,0:T(8,128)}, f32[512,512]{1,0:T(8,128)S(1)}, u32[]{:S(2)}) copy-start(f32[512,512]{1,0:T(8,128)S(1)} %fusion.46) | copy-start | bytes 3145732
  36.5 4.8 %copy-start.25 = (f32[512,8]{0,1:T(8,128)S(1)}, f32[512,8]{0,1:T(8,128)}, u32[]{:S(2)}) copy-start(f32[512,8]{0,1:T(8,128)} %get-tuple-element.62) | copy-start | bytes 49156
  42.4 28.2 %collective-permute-start.3 = (bf16[256,1024]{1,0:T(8,128)(2,1)S(1)}, bf16[256,1024]{1,0:T(8,128)(2,1)S(1)}, u32[]{:S(2)}, u32[]{:S(2)}) collective-permute-start(bf16[256,1024]{1,0:T(8,128)(2,1)S(1)} %collective-permute-done.1.own_in.refs_2_), channel_id=1, source_target_pairs={{0,1},{1,0},{2,3},{3,2},{4,5},{5,4},{6,7},{7,6},{8,9},{9,8},{10,11... | collective-permute-start | bytes 1572872 | tf_op jit(solution)/shard_map/ppermute | solution.py:53
  54.5 16.2 %all-to-all-start.1 = ((f32[32,16,128]{2,1,0:T(8,128)}), f32[32,16,128]{2,1,0:T(8,128)S(1)}, u32[]{:S(2)}, u32[]{:S(2)}) async-start(f32[32,16,128]{2,1,0:T(8,128)} %copy.102), calls=%async_computation.1 | async-start | bytes 524288 | tf_op jit(solution)/shard_map/all_to_all | solution.py:49
  59.7 14.9 %collective-permute-start.5 = (bf16[256,1024]{1,0:T(8,128)(2,1)S(1)}, bf16[256,1024]{1,0:T(8,128)(2,1)S(1)}, u32[]{:S(2)}, u32[]{:S(2)}) collective-permute-start(bf16[256,1024]{1,0:T(8,128)(2,1)S(1)} %collective-permute-done.own_in.refs_1_), channel_id=1, source_target_pairs={{0,1},{1,0},{2,3},{3,2},{4,5},{5,4},{6,7},{7,6},{8,9},{9,8},{10,11... | collective-permute-start | bytes 1572872 | tf_op jit(solution)/shard_map/ppermute | solution.py:53
  59.8 17.9 %collective-permute-start.7 = (bf16[256,1024]{1,0:T(8,128)(2,1)S(1)}, bf16[256,1024]{1,0:T(8,128)(2,1)}, u32[]{:S(2)}, u32[]{:S(2)}) collective-permute-start(bf16[256,1024]{1,0:T(8,128)(2,1)S(1)} %collective-permute-done.2.own_in.refs_3_), channel_id=1, source_target_pairs={{0,1},{1,0},{2,3},{3,2},{4,5},{5,4},{6,7},{7,6},{8,9},{9,8},{10,11... | collective-permute-start | bytes 1572872 | tf_op jit(solution)/shard_map/ppermute | solution.py:53
  68.0 14.2 %collective-permute-start.9 = (bf16[256,1024]{1,0:T(8,128)(2,1)S(1)}, bf16[256,1024]{1,0:T(8,128)(2,1)}, u32[]{:S(2)}, u32[]{:S(2)}) collective-permute-start(bf16[256,1024]{1,0:T(8,128)(2,1)S(1)} %get-tuple-element.34.own_in.refs_0_), channel_id=1, source_target_pairs={{0,1},{1,0},{2,3},{3,2},{4,5},{5,4},{6,7},{7,6},{8,9},{9,8},{10,11... | collective-permute-start | bytes 1572872 | tf_op jit(solution)/shard_map/ppermute | solution.py:53
  70.6 1.2 copy-start.1
  71.9 7.7 %copy-start.7 = (f32[512,512]{1,0:T(8,128)S(1)}, f32[512,512]{1,0:T(8,128)}, u32[]{:S(2)}) copy-start(f32[512,512]{1,0:T(8,128)} %copy.104) | copy-start | bytes 3145732
  71.9 7.7 %copy-start.16 = (bf16[512,128]{1,0:T(8,128)(2,1)S(1)}, bf16[512,128]{1,0:T(8,128)(2,1)}, u32[]{:S(2)}) copy-start(bf16[512,128]{1,0:T(8,128)(2,1)} %param.11) | copy-start | bytes 393220
  72.9 7.3 %copy-start.4 = (bf16[512,512]{1,0:T(8,128)(2,1)S(1)}, bf16[512,512]{1,0:T(8,128)(2,1)}, u32[]{:S(2)}) copy-start(bf16[512,512]{1,0:T(8,128)(2,1)} %param.9) | copy-start | bytes 1572868
  72.9 7.3 %copy-start.11 = (f32[512,512]{1,0:T(8,128)S(1)}, f32[512,512]{1,0:T(8,128)}, u32[]{:S(2)}) copy-start(f32[512,512]{1,0:T(8,128)} %copy.105) | copy-start | bytes 3145732
  72.9 7.3 %copy-start.26 = (f32[512]{0:T(512)S(1)}, f32[512]{0:T(512)}, u32[]{:S(2)}) copy-start(f32[512]{0:T(512)} %mul.129) | copy-start | bytes 6148
  73.0 16.5 %collective-permute-start.4 = (bf16[512,512]{1,0:T(8,128)(2,1)S(1)}, bf16[512,512]{1,0:T(8,128)(2,1)S(1)}, u32[]{:S(2)}, u32[]{:S(2)}) collective-permute-start(bf16[512,512]{1,0:T(8,128)(2,1)S(1)} %ring_grad.4), channel_id=1, source_target_pairs={{0,128},{64,192},{128,0},{192,64},{1,129},{65,193},{129,1},{193,65... | collective-permute-start | bytes 1572872 | tf_op jit(solution)/shard_map/ppermute | solution.py:57
  75.6 10.5 %copy-start.2 = (bf16[1024,512]{1,0:T(8,128)(2,1)S(1)}, bf16[1024,512]{1,0:T(8,128)(2,1)}, u32[]{:S(2)}) copy-start(bf16[1024,512]{1,0:T(8,128)(2,1)} %all-gather.2.cloned.1.call-done.weight_in) | copy-start | bytes 3145732
  75.6 23.5 %collective-permute-start.6 = (bf16[512,512]{1,0:T(8,128)(2,1)S(1)}, bf16[512,512]{1,0:T(8,128)(2,1)S(1)}, u32[]{:S(2)}, u32[]{:S(2)}) collective-permute-start(bf16[512,512]{1,0:T(8,128)(2,1)S(1)} %ring_grad.5), channel_id=1, source_target_pairs={{0,192},{64,0},{128,64},{192,128},{1,193},{65,1},{129,65},{193,129... | collective-permute-start | bytes 1572872 | tf_op jit(solution)/shard_map/ppermute | solution.py:57
  79.3 19.9 %collective-permute-start.8 = (bf16[512,512]{1,0:T(8,128)(2,1)S(1)}, bf16[512,512]{1,0:T(8,128)(2,1)S(1)}, u32[]{:S(2)}, u32[]{:S(2)}) collective-permute-start(bf16[512,512]{1,0:T(8,128)(2,1)S(1)} %ring_grad.6), channel_id=1, source_target_pairs={{0,64},{64,128},{128,192},{192,0},{1,65},{65,129},{129,193},{193,1... | collective-permute-start | bytes 1572872 | tf_op jit(solution)/shard_map/ppermute | solution.py:57
  81.6 36.6 %collective-permute-start.11 = (bf16[512,512]{1,0:T(8,128)(2,1)}, bf16[512,512]{1,0:T(8,128)(2,1)}, u32[]{:S(2)}, u32[]{:S(2)}) collective-permute-start(bf16[512,512]{1,0:T(8,128)(2,1)} %get-tuple-element.60.refs_8_), channel_id=1, source_target_pairs={{0,64},{64,128},{128,192},{192,0},{1,65},{65,129},{129,193},{193,1... | collective-permute-start | bytes 1572872 | tf_op jit(solution)/shard_map/ppermute | solution.py:57
  82.2 39.8 %collective-permute-start.12 = (bf16[512,512]{1,0:T(8,128)(2,1)}, bf16[512,512]{1,0:T(8,128)(2,1)}, u32[]{:S(2)}, u32[]{:S(2)}) collective-permute-start(bf16[512,512]{1,0:T(8,128)(2,1)} %get-tuple-element.60.refs_8_), channel_id=1, source_target_pairs={{0,128},{64,192},{128,0},{192,64},{1,129},{65,193},{129,1},{193,65... | collective-permute-start | bytes 1572872 | tf_op jit(solution)/shard_map/ppermute | solution.py:57
  89.4 33.4 %collective-permute-start.13 = (bf16[512,512]{1,0:T(8,128)(2,1)}, bf16[512,512]{1,0:T(8,128)(2,1)}, u32[]{:S(2)}, u32[]{:S(2)}) collective-permute-start(bf16[512,512]{1,0:T(8,128)(2,1)} %get-tuple-element.60.refs_8_), channel_id=1, source_target_pairs={{0,192},{64,0},{128,64},{192,128},{1,193},{65,1},{129,65},{193,129... | collective-permute-start | bytes 1572872 | tf_op jit(solution)/shard_map/ppermute | solution.py:57
  100.1 0.8 copy-start.9
  104.7 28.1 %all-to-all-start.2 = ((f32[32,16,128]{2,1,0:T(8,128)}), f32[32,16,128]{2,1,0:T(8,128)}, u32[]{:S(2)}, u32[]{:S(2)}) async-start(f32[32,16,128]{2,1,0:T(8,128)} %bitcast.95), calls=%async_computation.2 | async-start | bytes 524288 | tf_op jit(solution)/shard_map/all_to_all | solution.py:49
  113.3 58.3 %reduce-scatter.2.cloned.1.call-start = ((), (), s32[]{:S(2)}) async-start(), calls=%async_computation.7 | async-start | bytes 1179648 | tf_op jit(solution)/shard_map/reduce_scatter | solution.py:236
  113.3 3.9 %copy-start.17 = (bf16[512,128]{1,0:T(8,128)(2,1)S(1)}, bf16[512,128]{1,0:T(8,128)(2,1)}, u32[]{:S(2)}) copy-start(bf16[512,128]{1,0:T(8,128)(2,1)} %param.11) | copy-start | bytes 393220
  116.4 0.8 copy-start.14
  128.9 17.7 %copy-start.8 = (f32[512,512]{1,0:T(8,128)S(1)}, f32[512,512]{1,0:T(8,128)}, u32[]{:S(2)}) copy-start(f32[512,512]{1,0:T(8,128)} %copy.104) | copy-start | bytes 3145732
  128.9 17.7 %copy-start.10 = (bf16[512,512]{1,0:T(8,128)(2,1)S(1)}, bf16[512,512]{1,0:T(8,128)(2,1)}, u32[]{:S(2)}) copy-start(bf16[512,512]{1,0:T(8,128)(2,1)} %copy-done.9) | copy-start | bytes 1572868
  132.7 27.4 %copy-start.5 = (bf16[512,512]{1,0:T(8,128)(2,1)S(1)}, bf16[512,512]{1,0:T(8,128)(2,1)}, u32[]{:S(2)}) copy-start(bf16[512,512]{1,0:T(8,128)(2,1)} %param.9) | copy-start | bytes 1572868
  132.7 27.4 %copy-start.6 = (f32[512,512]{1,0:T(8,128)S(1)}, f32[512,512]{1,0:T(8,128)}, u32[]{:S(2)}) copy-start(f32[512,512]{1,0:T(8,128)} %copy.99) | copy-start | bytes 3145732
  134.2 29.7 %copy-start.30 = (f32[8]{0:T(128)S(1)}, f32[8]{0:T(128)}, u32[]{:S(2)}) copy-start(f32[8]{0:T(128)} %get-tuple-element.52) | copy-start | bytes 100
  134.2 29.8 %copy-start.29 = (f32[512]{0:T(512)S(1)}, f32[512]{0:T(512)}, u32[]{:S(2)}) copy-start(f32[512]{0:T(512)} %get-tuple-element.58) | copy-start | bytes 6148
  135.1 25.0 %all-to-all-start.3 = ((f32[32,16,128]{2,1,0:T(8,128)}), f32[32,16,128]{2,1,0:T(8,128)}, u32[]{:S(2)}, u32[]{:S(2)}) async-start(f32[32,16,128]{2,1,0:T(8,128)} %copy.110), calls=%async_computation.3 | async-start | bytes 524288 | tf_op jit(solution)/shard_map/all_to_all | solution.py:49
  146.7 40.2 %copy-start.27 = (f32[512]{0:T(512)S(1)}, f32[512]{0:T(512)}, u32[]{:S(2)}) copy-start(f32[512]{0:T(512)} %mul.129) | copy-start | bytes 6148
  161.4 0.7 copy-start.13
  163.9 2.4 %collective-permute-start.10 = (f32[512,128]{1,0:T(8,128)}, f32[512,128]{1,0:T(8,128)}, u32[]{:S(2)}, u32[]{:S(2)}) collective-permute-start(f32[512,128]{1,0:T(8,128)} %fusion.20), channel_id=1, source_target_pairs={{0,1},{1,0},{2,3},{3,2},{4,5},{5,4},{6,7},{7,6},{8,9},{9,8},{10,11... | collective-permute-start | bytes 786440 | tf_op jit(solution)/shard_map/ppermute | solution.py:53
  173.5 24.6 %collective-permute-start.14 = (bf16[512,128]{1,0:T(8,128)(2,1)}, bf16[512,128]{1,0:T(8,128)(2,1)}, u32[]{:S(2)}, u32[]{:S(2)}) collective-permute-start(bf16[512,128]{1,0:T(8,128)(2,1)} %fusion.23), channel_id=1, source_target_pairs={{0,2},{2,4},{4,6},{6,0},{1,3},{3,5},{5,7},{7,1},{8,10},{10,12},{12... | collective-permute-start | bytes 393224 | tf_op jit(solution)/shard_map/ppermute | solution.py:272
  174.8 23.3 %collective-permute-start.15 = (bf16[512,128]{1,0:T(8,128)(2,1)}, bf16[512,128]{1,0:T(8,128)(2,1)}, u32[]{:S(2)}, u32[]{:S(2)}) collective-permute-start(bf16[512,128]{1,0:T(8,128)(2,1)} %fusion.23), channel_id=1, source_target_pairs={{0,4},{2,6},{4,0},{6,2},{1,5},{3,7},{5,1},{7,3},{8,12},{10,14},{12... | collective-permute-start | bytes 393224 | tf_op jit(solution)/shard_map/ppermute | solution.py:272
  176.1 22.0 %collective-permute-start.16 = (bf16[512,128]{1,0:T(8,128)(2,1)}, bf16[512,128]{1,0:T(8,128)(2,1)}, u32[]{:S(2)}, u32[]{:S(2)}) collective-permute-start(bf16[512,128]{1,0:T(8,128)(2,1)} %fusion.23), channel_id=1, source_target_pairs={{0,6},{2,0},{4,2},{6,4},{1,7},{3,1},{5,3},{7,5},{8,14},{10,8},{12,... | collective-permute-start | bytes 393224 | tf_op jit(solution)/shard_map/ppermute | solution.py:272
  178.7 18.5 %all-to-all-start.4 = ((f32[32,8,128]{2,1,0:T(8,128)}), f32[32,8,128]{2,1,0:T(8,128)}, u32[]{:S(2)}, u32[]{:S(2)}) async-start(f32[32,8,128]{2,1,0:T(8,128)} %broadcast_in_dim_broadcast_in_dim_broadcast_in_dim.2), calls=%async_computation.5 | async-start | bytes 262144 | tf_op jit(solution)/shard_map/all_to_all | solution.py:49
  186.8 12.5 %copy-start.31 = (f32[8]{0:T(128)S(1)}, f32[8]{0:T(128)}, u32[]{:S(2)}) copy-start(f32[8]{0:T(128)} %param.17) | copy-start | bytes 100
  190.2 7.9 %copy-start.22 = (bf16[512,128]{1,0:T(8,128)(2,1)S(1)}, bf16[512,128]{1,0:T(8,128)(2,1)}, u32[]{:S(2)}) copy-start(bf16[512,128]{1,0:T(8,128)(2,1)} %fusion.23) | copy-start | bytes 393220
  190.2 9.9 %copy-start.20 = (f32[128,512]{1,0:T(8,128)S(1)}, f32[128,512]{1,0:T(8,128)}, u32[]{:S(2)}) copy-start(f32[128,512]{1,0:T(8,128)} %param.15) | copy-start | bytes 786436
  190.2 9.9 %copy-start.21 = (bf16[128,512]{1,0:T(8,128)(2,1)S(1)}, bf16[128,512]{1,0:T(8,128)(2,1)}, u32[]{:S(2)}) copy-start(bf16[128,512]{1,0:T(8,128)(2,1)} %reduce-scatter.2.cloned.1.call-done) | copy-start | bytes 393220
  190.2 9.9 %copy-start.23 = (f32[128,512]{1,0:T(8,128)S(1)}, f32[128,512]{1,0:T(8,128)}, u32[]{:S(2)}) copy-start(f32[128,512]{1,0:T(8,128)} %param.16) | copy-start | bytes 786436
  199.3 1.7 collective-permute-start.17
Sparse Core Ops, SparseCore 0:
  16.6 42.7 all-gather.1
  129.1 42.4 reduce-scatter.1
